TPU v7x, 32 devices: a whole 2x2x4 slice. The times are simulated.
32 devices in a mesh: head: 4 (over y, x), blk: 8 (over z, core).
Axes of the slice: x: 2, y: 2, z: 4, core: 2. Of those that a mesh axis runs over, the one named last changes fastest.
Arguments:
- tokens: bfloat16 [2, 2048, 1792], P(None, ('head', 'blk')), may hold values from -6 to 6
- cotangent: bfloat16 [2, 2048, 1792], P(None, ('head', 'blk')), may hold values from -6 to 6
- teacher: bfloat16 [2, 2048, 1792], P(None, ('head', 'blk')), may hold values from -36 to 36
- lengths: int32 [2], replicated, may hold values from 512 to 2048, as said below
- gain_attn: float32 [1792], replicated, may hold values from 0.5 to 1.5
- gain_mlp: float32 [1792], replicated, may hold values from 0.5 to 1.5
- w_query: bfloat16 [1792, 256], P(('head', 'blk')), may hold values from -0.125 to 0.125
- w_key: bfloat16 [1792, 256], P(('head', 'blk')), may hold values from -0.125 to 0.125
- w_value: bfloat16 [1792, 1792], P(('head', 'blk')), may hold values from -0.125 to 0.125
- w_out: bfloat16 [1792, 1792], P(('head', 'blk')), may hold values from -2 to 2
- w_gate: bfloat16 [1792, 4864], P(('head', 'blk')), may hold values from -0.125 to 0.125
- w_up: bfloat16 [1792, 4864], P(('head', 'blk')), may hold values from -0.125 to 0.125
- w_down: bfloat16 [4864, 1792], P(('head', 'blk')), may hold values from -0.078125 to 0.078125
Outputs:
- out: bfloat16 [2, 2048, 1792], P(None, ('head', 'blk'))
- loss: float32 [], replicated
- grad_tokens: float32 [2, 2048, 1792], P(None, ('head', 'blk'))
- grad_w_query: float32 [1792, 256], P(('head', 'blk'))
- grad_w_key: float32 [1792, 256], P(('head', 'blk'))
- grad_w_value: float32 [1792, 1792], P(('head', 'blk'))
- grad_w_out: float32 [1792, 1792], P(('head', 'blk'))
- grad_w_gate: float32 [1792, 4864], P(('head', 'blk'))
- grad_w_up: float32 [1792, 4864], P(('head', 'blk'))
- grad_w_down: float32 [4864, 1792], P(('head', 'blk'))
- grad_gain_attn: float32 [1792], P(('head', 'blk'))
- grad_gain_mlp: float32 [1792], P(('head', 'blk'))
Inputs may be any that keep to these rules, and one draw needn't show every extreme that they name: `lengths`: one sequence, which one varies, fills all 2048 slots; each has at least 512 valid slots.
All inputs are finite; a program needn't handle non-finite values.
Results may differ from a plain program's by a relative error of at most 0.015.
Values may be sent and summed in bfloat16 or wider, within the bound.
No kernel may reach another device: no remote copies, remote signals or barrier semaphores. Data moves between devices by JAX's collectives and lax.ppermute only.
A program may use at most 384 MiB of HBM per device.

v0:
```python
import functools
import math

import jax
import jax.numpy as jnp
from jax import lax
from jax.experimental import pallas as pl
from jax.experimental.pallas import tpu as pltpu
from jax.sharding import Mesh
from jax.sharding import PartitionSpec as P

H = 16
norm_eps = 1e-06
bf16, f32 = jnp.bfloat16, jnp.float32


def dot(a, b, ca, cb):
    return lax.dot_general(a, b, (((ca,), (cb,)), ((), ())), preferred_element_type=f32)


def swap(x, axis, o):
    n = lax.axis_size(axis)
    return lax.ppermute(x, axis, [(i, i ^ o) for i in range(n)])


def rms_scale(values):
    return lax.rsqrt(jnp.mean(values * values, axis=-1, keepdims=True) + norm_eps)


HEAD, LINE, BLK, CROSS = "head", "z", ("z", "c"), ("head", "c")
AXES = (HEAD,) + BLK


def tie(*values):
    return lax.optimization_barrier(values)


def window(moves, beside=()):
    arrays = tie(*[x for x, _, _ in moves])
    return tie([swap(x, axis, o) for x, (_, axis, o) in zip(arrays, moves)], beside)


def over(x, axis):
    return [(x, axis, o) for o in range(1, lax.axis_size(axis))]


def turn_moves(pieces, axis):
    me = lax.axis_index(axis)
    return [(pick(pieces, me ^ o), axis, o) for o in range(1, lax.axis_size(axis))]


def turned(pieces, got, axis):
    me = lax.axis_index(axis)
    return in_place([pick(pieces, me)] + list(got), me)


def return_moves(parts, axis):
    return [(x, axis, o) for o, x in enumerate(parts) if o]


def plus(own, got):
    return sum([x.astype(f32) for x in got], own.astype(f32))


def by_way(blocks):
    return (blocks[3], LINE, 1)


def rest_moves(blocks, passing):
    far = (blocks[2].astype(f32) + passing.astype(f32)).astype(bf16)
    return [(blocks[1], LINE, 1), (far, LINE, 2)]


def exchange(pieces, far_moves=(), far_beside=()):
    got, _ = window([(pieces[k], "c", k) for k in range(1, pieces.shape[0])])
    near = jnp.stack([pieces[0]] + got, axis=1)
    got, far_beside = window([(near[o], LINE, o) for o in range(1, 4)] + list(far_moves), far_beside)
    return [near[0]] + got[:3], got[3:], far_beside


def in_place(got, me):
    whole = jnp.zeros((len(got),) + got[0].shape, got[0].dtype)
    for o, x in enumerate(got):
        whole = lax.dynamic_update_index_in_dim(whole, x, me ^ o, 0)
    return whole


def pick(x, i, axis=0):
    return lax.dynamic_index_in_dim(x, i, axis, keepdims=False)


def line_whole(got):
    return in_place(got, lax.axis_index(LINE))


def core_end(own, got):
    return jnp.moveaxis(in_place([own] + list(got), lax.axis_index("c")), 0, 1)


def core_share(parts, at):
    me = lax.axis_index("c")
    return [(pick(parts, me ^ o, at), "c", o) for o in range(1, lax.axis_size("c"))]


def core_sum(parts, got, at):
    return plus(pick(parts, lax.axis_index("c"), at), got).astype(bf16)


def line_blocks(near, at):
    return [pick(near, lax.axis_index(LINE) ^ o, at) for o in range(4)]


def positions(b, sub, cps, slot, dim, sb):
    shape = (sb, 1) if dim == 0 else (1, sb)
    lane = lax.broadcasted_iota(jnp.int32, shape, dim)
    return ((b ^ (sub * cps + lane // slot)) * slot) + lane % slot


def flip(x):
    return jnp.transpose(x.astype(f32)).astype(bf16)


def kernel_sum(score):
    lifted = score + 4.0
    return lifted * lifted * (1.0 / 32.0) + 0.5


def fwd_kernel(nh, nb, slot, sb, ids, got0, got1, got2, got3, tiles, res, out, vrow):
    got, cores = (got0, got1, got2, got3), nb // 4
    nsub, cps = nb * slot // sb, sb // slot
    h, b = ids[0], ids[1]
    for o in range(nb):
        for oh in range(nh):
            at = (h ^ oh) * nsub + o // cps
            lo = (o % cps) * slot
            piece = got[o // cores][o % cores, :, oh * slot : (oh + 1) * slot]
            tiles[at, :, lo : lo + slot] = piece

    def rows_of(i, c):
        vv = jnp.concatenate([tiles[i, 32:144, :].astype(f32), jnp.ones((16, sb), f32)], axis=0)
        vrow[i] = jnp.transpose(vv).astype(bf16)
        return c

    lax.fori_loop(0, nh * nsub, rows_of, 0)

    for oh in range(nh):
        hq = h ^ oh
        for sub in range(nsub):
            iq = hq * nsub + sub
            qrow = flip(tiles[iq, 0:16, :])
            pos_q = positions(b, sub, cps, slot, 0, sb)

            def step(ik, acc, masked):
                w = kernel_sum(dot(qrow, tiles[ik, 16:32, :], 1, 0))
                if masked:
                    pos_k = positions(b, ik - hq * nsub, cps, slot, 1, sb)
                    w = jnp.where(pos_q >= pos_k, w, 0.0)
                return acc + dot(w.astype(bf16), vrow[ik], 1, 0)

            acc = lax.fori_loop(
                0, hq * nsub, functools.partial(step, masked=False), jnp.zeros((sb, 128), f32)
            )
            acc = lax.fori_loop(hq * nsub, (hq + 1) * nsub, functools.partial(step, masked=True), acc)
            den = acc[:, 112:113]
            mixed = acc / den
            lane = lax.broadcasted_iota(jnp.int32, (sb, 128), 1)
            res[iq] = jnp.where(lane == 112, den, mixed)
            back = jnp.transpose(mixed)[0:112].astype(bf16)
            for c in range(cps):
                o = sub * cps + c
                piece = back[:, c * slot : (c + 1) * slot]
                out[o % cores, o // cores, :, oh * slot : (oh + 1) * slot] = piece


def bwd_kernel(nh, nb, slot, sb, ids, tiles, res, got0, got1, got2, got3, out, gt, krow, acc):
    got, cores = (got0, got1, got2, got3), nb // 4
    nsub, cps = nb * slot // sb, sb // slot
    h, b = ids[0], ids[1]
    for o in range(nb):
        for oh in range(nh):
            at = (h ^ oh) * nsub + o // cps
            lo = (o % cps) * slot
            piece = got[o // cores][o % cores, :, oh * slot : (oh + 1) * slot]
            gt[at, :, lo : lo + slot] = piece

    def rows_of(i, c):
        krow[i] = flip(tiles[i, 16:32, :])
        acc[i] = jnp.zeros((144, sb), f32)
        return c

    lax.fori_loop(0, nh * nsub, rows_of, 0)

    for oh in range(nh):
        hq = h ^ oh
        for sub in range(nsub):
            iq = hq * nsub + sub
            qcol = tiles[iq, 0:16, :]
            qrow = flip(qcol)
            gcol = gt[iq]
            grow = jnp.transpose(gcol.astype(f32))
            kept = res[iq]
            rden = 1.0 / kept[:, 112:113]
            delta = jnp.sum(grow * kept[:, 0:112], axis=1, keepdims=True)
            grow = grow.astype(bf16)
            pos_q = positions(b, sub, cps, slot, 0, sb)

            def step(ik, dq, masked):
                lifted = dot(qrow, tiles[ik, 16:32, :], 1, 0) + 4.0
                g = (dot(grow, tiles[ik, 32:144, :], 1, 0) - delta) * rden
                p = (lifted * lifted * (1.0 / 32.0) + 0.5) * rden
                ds = g * lifted * (1.0 / 16.0)
                if masked:
                    pos_k = positions(b, ik - hq * nsub, cps, slot, 1, sb)
                    keep = pos_q >= pos_k
                    p = jnp.where(keep, p, 0.0)
                    ds = jnp.where(keep, ds, 0.0)
                p, ds = p.astype(bf16), ds.astype(bf16)
                acc[ik, 32:144, :] += dot(gcol, p, 1, 0)
                acc[ik, 16:32, :] += dot(qcol, ds, 1, 0)
                return dq + dot(ds, krow[ik], 1, 0)

            dq = lax.fori_loop(
                0, hq * nsub, functools.partial(step, masked=False), jnp.zeros((sb, 16), f32)
            )
            dq = lax.fori_loop(hq * nsub, (hq + 1) * nsub, functools.partial(step, masked=True), dq)
            acc[iq, 0:16, :] = jnp.transpose(dq)
    for oh in range(nh):
        for o in range(nb):
            at = (h ^ oh) * nsub + o // cps
            lo = (o % cps) * slot
            piece = acc[at, :, lo : lo + slot].astype(bf16)
            out[o % cores, o // cores, :, oh * slot : (oh + 1) * slot] = piece


def rows_of(refs, s):
    return jnp.concatenate([x[s] for x in refs], axis=0)


def to_peers(cores, copies, b, pieces, out):
    for o in range(4 * cores):
        out[o % cores, o // cores] = pieces[(b ^ o) // copies]


def from_peers(cores, copies, b, got, pieces):
    for o in range(4 * cores):
        pieces[o] = got[o // cores][o % cores]
    return lambda p: pieces[b ^ (p * copies)]


def qkv_kernel(hd, copies, fw, vw, ids, x0, x1, x2, x3, w, out, pieces):
    cores = out.shape[0]
    for s in range(x0.shape[0]):
        rows = jnp.dot(rows_of((x0, x1, x2, x3), s), w[...], preferred_element_type=f32)
        cols = jnp.transpose(rows)
        for j in range(hd):
            at = (j * fw, (hd + j) * fw, 2 * hd * fw + j * vw)
            piece = [cols[lo : lo + n] for lo, n in zip(at, (fw, fw, vw))]
            pieces[s * hd + j] = jnp.concatenate(piece, axis=0).astype(bf16)
    to_peers(cores, copies, ids[1], pieces, out)


def out_kernel(hd, copies, ids, g0, g1, g2, g3, w, mixed, own, send, pieces):
    cores, vw, lanes = g0.shape
    seqs, slot = own.shape[:2]
    take = from_peers(cores, copies, ids[1], (g0, g1, g2, g3), pieces)
    for s in range(seqs):
        cols = jnp.concatenate([take(s * hd + j) for j in range(hd)], axis=0)
        mixed[:, s * lanes : (s + 1) * lanes] = cols
        rows = jnp.transpose(cols.astype(f32)).astype(bf16)
        part = jnp.dot(rows, w[...], preferred_element_type=f32)
        own[s] = part[:slot]
        for o in range(1, 4):
            send[o - 1, s] = part[o * slot : (o + 1) * slot].astype(bf16)


def mixed_back_kernel(hd, copies, ids, x0, x1, x2, x3, w, mixed, out, grad, pieces):
    cores, vw, lanes = out.shape[0], out.shape[2], out.shape[3]
    z, c = ids[2], ids[1] % cores
    rows = [rows_of((x0, x1, x2, x3), s) for s in range(x0.shape[0])]
    for s, x in enumerate(rows):
        cols = dot(w[...], x, 1, 1)
        for j in range(hd):
            pieces[s * hd + j] = cols[j * vw : (j + 1) * vw].astype(bf16)
    to_peers(cores, copies, ids[1], pieces, out)
    total = jnp.dot(mixed[...], jnp.concatenate(rows, axis=0), preferred_element_type=f32)
    drow = grad.shape[2]
    for k in range(4 * cores):
        grad[(k % cores) ^ c, (k // cores) ^ z] = total[k * drow : (k + 1) * drow].astype(bf16)


def qkv_back_kernel(hd, copies, fw, vw, ids, g0, g1, g2, g3, x, w, grad, own, send, pieces, cols):
    cores, pw, lanes = g0.shape
    seqs, slot = own.shape[:2]
    z, c = ids[2], ids[1] % cores
    take = from_peers(cores, copies, ids[1], (g0, g1, g2, g3), pieces)
    for s in range(seqs):
        for j in range(hd):
            piece = take(s * hd + j)
            at = (j * fw, (hd + j) * fw, 2 * hd * fw + j * vw)
            lo = 0
            for row, n in zip(at, (fw, fw, vw)):
                cols[row : row + n, s * lanes : (s + 1) * lanes] = piece[lo : lo + n]
                lo += n
    rows = jnp.transpose(cols[...].astype(f32)).astype(bf16)
    for s in range(seqs):
        part = dot(rows[s * lanes : (s + 1) * lanes], w[...], 1, 1)
        own[s] = part[:slot]
        for o in range(1, 4):
            send[o - 1, s] = part[o * slot : (o + 1) * slot].astype(bf16)
    drow, half = grad.shape[3], x.shape[1] // 2
    for i in range(2):
        total = dot(x[:, i * half : (i + 1) * half], rows, 0, 0)
        for k in range(half // drow):
            at = i * (half // drow) + k
            block = total[k * drow : (k + 1) * drow].astype(bf16)
            grad[(at % cores) ^ c, (at // cores % 4) ^ z, at // (4 * cores)] = block


def cut_kernel(nh, run, ids, gate, up, out):
    z = ids[2]
    for zz in range(4):
        parts = []
        for w in (gate, up):
            parts += [w[:, (k * 4 + zz) * run : (k * 4 + zz + 1) * run] for k in range(nh)]
        out[zz ^ z] = jnp.concatenate([x.astype(f32) for x in parts], axis=1).astype(bf16)


def feed_kernel(nh, run, ids, p0, p1, p2, p3, gate, up, grad_gate, grad_up, total, pieces):
    z = ids[2]
    pieces[0], pieces[1], pieces[2], pieces[3] = p0[...], p1[...], p2[...], p3[...]
    for zz in range(4):
        piece = pieces[zz ^ z].astype(f32)
        for at, grad in ((0, grad_gate), (nh * run, grad_up)):
            for k in range(nh):
                lo = (k * 4 + zz) * run
                grad[:, lo : lo + run] = piece[:, at + k * run : at + (k + 1) * run]
    both = grad_gate[...] * gate[...].astype(f32) + grad_up[...] * up[...].astype(f32)
    total[...] = jnp.sum(both, axis=1, keepdims=True)


def heads_kernel(nh, qw, vw, ids, p0, p1, p2, p3, wq, wk, wv, gq, gk, gv, total, pieces):
    h = ids[0]
    pieces[0], pieces[1], pieces[2], pieces[3] = p0[...], p1[...], p2[...], p3[...]
    for k in range(nh):
        piece = pieces[k ^ h].astype(f32)
        gq[:, k * qw : (k + 1) * qw] = piece[:, :qw]
        gk[:, k * qw : (k + 1) * qw] = piece[:, qw : 2 * qw]
        gv[:, k * vw : (k + 1) * vw] = piece[:, 2 * qw :]
    sums = [
        jnp.sum(g[...] * w[...].astype(f32), axis=1, keepdims=True)
        for g, w in ((gq, wq), (gk, wk), (gv, wv))
    ]
    total[...] = sums[0] + sums[1] + sums[2]


def call(body, ids, arrays, outs, scratch, room=6):
    vmem = pl.BlockSpec(memory_space=pltpu.VMEM)
    held = list(arrays) + jax.tree.leaves(outs) + list(scratch)
    held = sum(math.prod(x.shape[:-1]) * max(x.shape[-1], 128) * x.dtype.itemsize for x in held)
    return pl.pallas_call(
        body,
        out_shape=outs,
        in_specs=[pl.BlockSpec(memory_space=pltpu.SMEM)] + [vmem] * len(arrays),
        out_specs=jax.tree.map(lambda _: vmem, outs),
        scratch_shapes=scratch,
        compiler_params=pltpu.CompilerParams(vmem_limit_bytes=held + room * 1024 * 1024),
    )(ids, *arrays)


def shards(
    tokens,
    cotangent,
    teacher,
    lengths,
    gain_attn,
    gain_mlp,
    w_query,
    w_key,
    w_value,
    w_out,
    w_gate,
    w_up,
    w_down,
):
    seqs, slot, width = tokens.shape
    cores = lax.axis_size("c")
    nh, nb = lax.axis_size(HEAD), 4 * cores
    h, b = lax.axis_index(HEAD), lax.axis_index(BLK)
    hd = H // nh
    pairs = seqs * hd
    copies = nb // pairs
    drow = w_query.shape[0]
    fw, vw = w_query.shape[1] // H, w_value.shape[1] // H
    pw = 2 * fw + vw
    ffl = w_gate.shape[1] // 4
    lanes = nh * slot
    sb = min(512, nb * slot)
    n = nb * slot * nh // sb
    ids = jnp.stack([h, b, lax.axis_index(LINE)]).astype(jnp.int32)

    def columns(ws):
        return jnp.concatenate([w.reshape(drow, nh, -1).transpose(1, 0, 2) for w in ws], axis=2)

    def gathered(x):
        return lax.all_gather(x[None], CROSS, axis=0, tiled=True)

    def summed(shares):
        return lax.psum_scatter(shares, CROSS, scatter_dimension=0)

    qkv_cols = columns((w_query, w_key, w_value))
    run = w_gate.shape[1] // (4 * nh)
    feed = jax.ShapeDtypeStruct((4, drow, 2 * ffl), bf16)
    ffn_cols = call(functools.partial(cut_kernel, nh, run), ids, [w_gate, w_up], feed, [])

    place = (h * nb + b) * slot + lax.broadcasted_iota(jnp.int32, (seqs, slot), 1)
    valid = (place < lengths[:, None]).astype(f32)[..., None]
    count = jnp.sum(lengths).astype(f32)

    tokens_f = tokens.astype(f32)
    scale_one = rms_scale(tokens_f)
    own_rows = (tokens_f * scale_one * gain_attn).astype(bf16)
    (*got, ffn_1, ffn_2), (own_rows,) = window(
        turn_moves(qkv_cols, HEAD) + [(ffn_cols[1], LINE, 1), (ffn_cols[2], LINE, 2)], (own_rows,)
    )
    qkv_cols = turned(qkv_cols, got, HEAD)
    (row_1, row_2, qkv_near, qkv_far), _ = window(
        [(own_rows, HEAD, 1), (own_rows, HEAD, 2), (qkv_cols, LINE, 1), (qkv_cols, LINE, 2)]
    )
    (row_3, qkv_last, out_near, out_far), _ = window(
        [(own_rows, HEAD, 3), (qkv_far, LINE, 1), (w_out, LINE, 1), (w_out, LINE, 2)]
    )
    attn_rows = [own_rows, row_1, row_2, row_3]
    qkv_w = line_whole([qkv_cols, qkv_near, qkv_far, qkv_last])
    (*got, out_last), _ = window(over(qkv_w, "c") + [(out_far, LINE, 1)])
    qkv_w = core_end(qkv_w, got).transpose(2, 0, 1, 3, 4).reshape(width, -1)
    out_w = line_whole([w_out, out_near, out_far, out_last])
    normed_attn = jnp.concatenate(attn_rows, axis=1).reshape(-1, width)
    geometry = (nh, nb, slot, sb)
    piece = lambda rows: jax.ShapeDtypeStruct((cores, 4, rows, lanes), bf16)
    held = lambda rows: [pltpu.VMEM((pairs, rows, lanes), bf16)]
    taken = lambda rows: [pltpu.VMEM((nb, rows, lanes), bf16)]
    own_part = jax.ShapeDtypeStruct((seqs, slot, width), f32)
    sent_part = jax.ShapeDtypeStruct((3, seqs, slot, width), bf16)
    pieces = call(
        functools.partial(qkv_kernel, hd, copies, fw, vw),
        ids,
        attn_rows + [qkv_w],
        piece(pw),
        held(pw),
        room=10,
    )
    pieces, out_w = tie(pieces, out_w)
    sent, got, (ffn_last, down_w) = exchange(
        pieces, far_moves=over(out_w, "c"), far_beside=(ffn_cols[3], gathered(w_down))
    )
    down_w = down_w.reshape(-1, width)
    ffn_3 = swap(ffn_last, LINE, 3)
    out_w = core_end(out_w, got).reshape(-1, width)
    tiles, res, mixed_out = call(
        functools.partial(fwd_kernel, *geometry),
        ids,
        sent,
        [
            jax.ShapeDtypeStruct((n, pw, sb), bf16),
            jax.ShapeDtypeStruct((n, sb, 128), f32),
            piece(vw),
        ],
        [pltpu.VMEM((n, sb, 128), bf16)],
        room=14,
    )
    mixed_out, ffn_3 = tie(mixed_out, ffn_3)
    ffn_w = gathered(line_whole([ffn_cols[0], ffn_1, ffn_2, ffn_3]))
    ffn_w = ffn_w.reshape(nh, cores, 4, drow, -1).transpose(0, 2, 1, 3, 4).reshape(width, -1)
    mixed, attn_own, attn_part = call(
        functools.partial(out_kernel, hd, copies),
        ids,
        exchange(mixed_out)[0] + [out_w],
        [jax.ShapeDtypeStruct((hd * vw, seqs * lanes), bf16), own_part, sent_part],
        taken(vw),
        room=10,
    )
    got, _ = window([(attn_part[o - 1], HEAD, o) for o in range(1, 4)])
    residual = tokens_f + plus(attn_own, got)

    scale_two = rms_scale(residual)
    own_rows = (residual * scale_two * gain_mlp).astype(bf16)

    def forward(*rows):
        both = dot(jnp.concatenate([x.reshape(-1, width) for x in rows]), ffn_w, 1, 0)
        gate, up = both[:, :ffl], both[:, ffl:]
        hidden = (jax.nn.silu(gate) * up).astype(bf16)
        part = dot(hidden, down_w, 1, 0).reshape(len(rows), seqs, slot, width)
        return gate, up, hidden, part

    (near, far), (ffn_w,) = window([(own_rows, LINE, 1), (own_rows, LINE, 2)], (ffn_w,))
    (last,), first = window([(far, LINE, 1)], forward(own_rows, near, far))
    kept = [first, forward(last)]
    part = [y for x in kept for y in x[3]]
    normed_mlp = jnp.concatenate([x.reshape(-1, width) for x in (own_rows, near, far, last)])
    hidden = jnp.concatenate([x[2] for x in kept])
    passing = swap(part[3].astype(bf16), LINE, 1)
    got, _ = window(rest_moves([x.astype(bf16) for x in part], passing))
    full = valid * (residual + plus(part[0], got))
    diff = full - teacher.astype(f32)
    (loss,) = tie(jnp.full((1, 64, 128), jnp.sum(valid * diff * diff)))
    loss = lax.all_gather(loss, AXES, axis=0, tiled=True)

    grad_res = valid * (cotangent.astype(f32) + 2.0 * valid * diff / (width * count))
    own_rows = grad_res.astype(bf16)

    def backward(rows, gate, up):
        grad_hidden = dot(jnp.concatenate([x.reshape(-1, width) for x in rows]), down_w, 1, 1)
        sigma = jax.nn.sigmoid(gate)
        slope = sigma * (1.0 + gate * (1.0 - sigma))
        grad_gate = (grad_hidden * up * slope).astype(bf16)
        grad_up = (grad_hidden * gate * sigma).astype(bf16)
        grad_both = jnp.concatenate([grad_gate, grad_up], axis=1)
        return grad_both, dot(grad_both, ffn_w, 1, 1).reshape(len(rows), seqs, slot, width)

    def norm_back(grad_norm, values, scale_rows, gain):
        unit = values * scale_rows
        e = grad_norm * gain
        return scale_rows * (e - unit * jnp.mean(e * unit, axis=-1, keepdims=True))

    (near, far), _ = window([(own_rows, LINE, 1), (own_rows, LINE, 2)])
    (last,), first = window([(far, LINE, 1)], backward((own_rows, near, far), *kept[0][:2]))
    back = [first, backward((last,), *kept[1][:2])]
    part = [y for x in back for y in x[1]]
    passing = swap(part[3].astype(bf16), LINE, 1)
    grad_both = jnp.concatenate([x[0] for x in back])
    grad_ffn = jnp.concatenate([x.reshape(-1, width) for x in (own_rows, near, far, last)])
    part, grad_both, hidden = tie(part, grad_both, hidden)
    grad_down = dot(hidden, grad_ffn, 0, 0).astype(bf16).reshape(nb, -1, width)
    passing, grad_down, normed_mlp = tie(passing, grad_down, normed_mlp)
    grad_down = summed(grad_down)
    grad_ffn_w = dot(normed_mlp, grad_both, 0, 0).astype(bf16)
    grad_ffn_w = grad_ffn_w.reshape(nh, 4, cores, drow, -1).transpose(0, 2, 1, 3, 4)
    shares = grad_ffn_w.reshape(nb, 4 * drow, -1)
    got, (shares, loss) = window(rest_moves([x.astype(bf16) for x in part], passing), (shares, loss))
    grad_ffn_w = summed(shares)
    loss = jnp.sum(loss[:, 0, 0]) / (width * count)
    grad_resid = grad_res + norm_back(plus(part[0], got), residual, scale_two, gain_mlp)
    own_rows = grad_resid.astype(bf16)
    got, _ = window(over(own_rows, HEAD))
    sent, grad_out_w = call(
        functools.partial(mixed_back_kernel, hd, copies),
        ids,
        [own_rows] + got + [out_w, mixed],
        [piece(vw), jax.ShapeDtypeStruct((cores, 4, drow, width), bf16)],
        held(vw),
        room=10,
    )
    sent, out_got, _ = exchange(
        sent, far_moves=[(grad_out_w[k], "c", k) for k in range(1, cores)]
    )
    grad_out_w = plus(grad_out_w[0], out_got).astype(bf16)
    sent, grad_out_w = tie(sent, grad_out_w)
    out_got = [swap(grad_out_w[o], LINE, o) for o in range(1, 3)]
    grads_out = call(
        functools.partial(bwd_kernel, *geometry),
        ids,
        [tiles, res] + sent,
        piece(pw),
        [
            pltpu.VMEM((n, vw, sb), bf16),
            pltpu.VMEM((n, sb, fw), bf16),
            pltpu.VMEM((n, pw, sb), f32),
        ],
        room=14,
    )
    grads_out, out_got = tie(grads_out, out_got)
    grad_qkv, _, (grad_ffn_w,) = exchange(grads_out, far_beside=(grad_ffn_w,))
    grad_ffn_w = grad_ffn_w.reshape(4, drow, -1)
    ffn_pieces = [pick(grad_ffn_w, lax.axis_index(LINE) ^ o) for o in range(4)]
    grad_qkv_w, own_back, attn_back = call(
        functools.partial(qkv_back_kernel, hd, copies, fw, vw),
        ids,
        grad_qkv + [normed_attn, qkv_w],
        [jax.ShapeDtypeStruct((cores, 4, nh, drow, hd * pw), bf16), own_part, sent_part],
        taken(pw) + [pltpu.VMEM((hd * pw, seqs * lanes), bf16)],
        room=14,
    )
    row_moves = [(attn_back[o - 1], HEAD, o) for o in range(1, 4)]
    got, _ = window([(grad_qkv_w[k], "c", k) for k in range(1, cores)])
    grad_qkv_w = plus(grad_qkv_w[0], got).astype(bf16)
    (passing, ffn_2, *row_got), _ = window(
        [by_way(grad_qkv_w), (ffn_pieces[2], LINE, 2)] + row_moves[:2]
    )
    (got_1, got_2, last, ffn_3), _ = window(
        rest_moves(grad_qkv_w, passing) + [row_moves[2], (ffn_pieces[3], LINE, 3)]
    )
    row_got = row_got + [last]
    grad_qkv_w = plus(grad_qkv_w[0], [got_1, got_2]).astype(bf16)
    (*got, ffn_1, out_last), _ = window(
        turn_moves(grad_qkv_w, HEAD) + [(ffn_pieces[1], LINE, 1), (grad_out_w[3], LINE, 3)]
    )
    out_got = out_got + [out_last]
    grad_down, got = tie(grad_down, got)
    rows_f32 = lambda w: jax.ShapeDtypeStruct(w.shape, f32)
    one = jax.ShapeDtypeStruct((drow, 1), f32)
    gg, gu, gain_sum_two = call(
        functools.partial(feed_kernel, nh, run),
        ids,
        [ffn_pieces[0], ffn_1, ffn_2, ffn_3, w_gate, w_up],
        [rows_f32(w_gate), rows_f32(w_up), one],
        [pltpu.VMEM((4, drow, 2 * ffl), bf16)],
    )
    gq, gk, gv, gain_sum_one = call(
        functools.partial(heads_kernel, nh, hd * fw, hd * vw),
        ids,
        [pick(grad_qkv_w, h)] + got + [w_query, w_key, w_value],
        [rows_f32(w_query), rows_f32(w_key), rows_f32(w_value), one],
        [pltpu.VMEM((4, drow, hd * pw), bf16)],
    )
    grad_out_w = plus(grad_out_w[0], out_got)
    grad_in = plus(own_back, row_got)
    grad_tokens = grad_resid + norm_back(grad_in, tokens_f, scale_one, gain_attn)

    def gain_grad(total, gain):
        at = lax.axis_index(AXES) * drow
        return total[:, 0] / lax.dynamic_slice(gain, (at,), (drow,))

    return (
        full.astype(bf16),
        loss,
        grad_tokens,
        gq,
        gk,
        gv,
        grad_out_w.astype(f32),
        gg,
        gu,
        grad_down.astype(f32),
        gain_grad(gain_sum_one, gain_attn),
        gain_grad(gain_sum_two, gain_mlp),
    )


def solution(mesh):
    parts = Mesh(mesh.devices.reshape(mesh.shape["head"], 4, -1), AXES)
    rows, slots = P(AXES, None), P(None, AXES, None)
    return jax.shard_map(
        shards,
        mesh=parts,
        in_specs=(slots,) * 3 + (P(),) * 3 + (rows,) * 7,
        out_specs=(slots, P(), slots) + (rows,) * 7 + (P(AXES),) * 2,
        check_vma=False,
    )
```

profile of v0, /device:TPU:0, one launch (start us, length us, event | category | flops | bytes accessed | tf_op | source)
XLA Modules:
  0.0 503.6 jit_solution(14505020666766685392)
XLA Ops:
  41.2 5.0 collective-permute-done.7
  52.4 5.3 %collective-permute-done.6.x2 = bf16[2,64,1792]{2,1,0:T(8,128)(2,1)S(1)} collective-permute-done((bf16[2,64,1792]{2,1,0:T(8,128)(2,1)S(1)}, bf16[2,64,1792]{2,1,0:T(8,128)(2,1)S(1)}, u32[]{:S(2)}, u32[]{:S(2)}) %collective-permute-start.6) | collective-permute-done | bytes 458784 | tf_op jit(solution)/shard_map/ppermute | solution.py:23
  61.0 7.2 %collective-permute-done.11 = bf16[56,1792]{1,0:T(8,128)(2,1)S(1)} collective-permute-done((bf16[56,1792]{1,0:T(8,128)(2,1)}, bf16[56,1792]{1,0:T(8,128)(2,1)S(1)}, u32[]{:S(2)}, u32[]{:S(2)}) %collective-permute-start.11) | collective-permute-done | bytes 200736 | tf_op jit(solution)/shard_map/ppermute | solution.py:23
  70.9 5.4 %collective-permute-done.14 = bf16[56,1792]{1,0:T(8,128)(2,1)S(1)} collective-permute-done((bf16[56,1792]{1,0:T(8,128)(2,1)S(1)}, bf16[56,1792]{1,0:T(8,128)(2,1)S(1)}, u32[]{:S(2)}, u32[]{:S(2)}) %collective-permute-start.14) | collective-permute-done | bytes 200736 | tf_op jit(solution)/shard_map/ppermute | solution.py:23
  90.4 5.5 %collective-permute-done.17.got2 = bf16[2,144,256]{2,1,0:T(8,128)(2,1)S(1)} collective-permute-done((bf16[2,144,256]{2,1,0:T(8,128)(2,1)S(1)}, bf16[2,144,256]{2,1,0:T(8,128)(2,1)S(1)}, u32[]{:S(2)}, u32[]{:S(2)}) %collective-permute-start.17) | collective-permute-done | bytes 147488 | tf_op jit(solution)/shard_map/ppermute | solution.py:23
  102.8 7.7 %shard_map.222 = (bf16[4,144,512]{2,1,0:T(8,128)(2,1)S(1)}, f32[4,512,128]{2,1,0:T(8,128)S(1)}, bf16[2,4,112,256]{3,2,1,0:T(8,128)(2,1)S(1)}) custom-call(s32[3]{0:T(128)S(1)} %pad_add_fusion.ids, bf16[2,144,256]{2,1,0:T(8,128)(2,1)S(1)} %get-tuple-element.391.got0, bf16[2,144,256]{2,1,0:T(8,128)(2,1)S(1)} %copy-done.30, ...), custom_call_target="tpu_custom_call" | custom-call | tf_op jit(solution)/shard_map/pallas_call | solution.py:360
  121.8 8.0 %collective-permute-done.23.g2 = bf16[2,112,256]{2,1,0:T(8,128)(2,1)S(1)} collective-permute-done((bf16[2,112,256]{2,1,0:T(8,128)(2,1)S(1)}, bf16[2,112,256]{2,1,0:T(8,128)(2,1)S(1)}, u32[]{:S(2)}, u32[]{:S(2)}) %collective-permute-start.23) | collective-permute-done | bytes 114720 | tf_op jit(solution)/shard_map/ppermute | solution.py:23
  132.5 4.0 collective-permute-start.25
  138.1 11.5 %collective-permute-done.25 = bf16[2,64,1792]{2,1,0:T(8,128)(2,1)S(1)} collective-permute-done((bf16[2,64,1792]{2,1,0:T(8,128)(2,1)S(1)}, bf16[2,64,1792]{2,1,0:T(8,128)(2,1)S(1)}, u32[]{:S(2)}, u32[]{:S(2)}) %collective-permute-start.25) | collective-permute-done | bytes 458784 | tf_op jit(solution)/shard_map/ppermute | solution.py:23
  149.6 17.3 %collective-permute-done.27 = bf16[2,64,1792]{2,1,0:T(8,128)(2,1)S(1)} collective-permute-done((bf16[2,64,1792]{2,1,0:T(8,128)(2,1)S(1)}, bf16[2,64,1792]{2,1,0:T(8,128)(2,1)S(1)}, u32[]{:S(2)}, u32[]{:S(2)}) %collective-permute-start.27) | collective-permute-done | bytes 458784 | tf_op jit(solution)/shard_map/ppermute | solution.py:23
  173.0 9.2 %all-gather.5.cloned.1.call-done = bf16[8,4,56,2432]{3,2,1,0:T(8,128)(2,1)} async-done(((bf16[1,4,56,2432]{3,2,1,0:T(8,128)(2,1)}), bf16[8,4,56,2432]{3,2,1,0:T(8,128)(2,1)}) %all-gather.5.cloned.1.call-update) | async-done | bytes 8716304 | tf_op jit(solution)/shard_map/all_gather | solution.py:405
  182.2 7.6 %copy.72 = bf16[4,4,2,56,2432]{4,3,2,1,0:T(8,128)(2,1)} copy(bf16[4,4,2,56,2432]{4,3,1,2,0:T(8,128)(2,1)} %bitcast.277) | data formatting | bytes 17432576 | tf_op jit(solution)/shard_map/transpose | solution.py:473
  191.9 6.9 %fusion.9 = f32[384,2432]{1,0:T(8,128)S(1)} fusion(bf16[1792,2432]{1,0:T(8,128)(2,1)} %bitcast.268, bf16[128,1792]{1,0:T(8,128)(2,1)} %bitcast.63, bf16[128,1792]{1,0:T(8,128)(2,1)} %bitcast.62, bf16[128,1792]{1,0:T(8,128)(2,1)} %bitcast.61), kind=kOutput, calls=%fused_computation.22 | convolution fusion | flops 3351183360 | bytes 13828096 | tf_op jit(solution)/shard_map/dot_general | solution.py:18
  204.7 9.2 %collective-permute-done.30 = bf16[2,64,1792]{2,1,0:T(8,128)(2,1)S(1)} collective-permute-done((bf16[2,64,1792]{2,1,0:T(8,128)(2,1)}, bf16[2,64,1792]{2,1,0:T(8,128)(2,1)S(1)}, u32[]{:S(2)}, u32[]{:S(2)}) %collective-permute-start.30) | collective-permute-done | bytes 458784 | tf_op jit(solution)/shard_map/ppermute | solution.py:23
  219.1 9.2 %collective-permute-done.31 = bf16[2,64,1792]{2,1,0:T(8,128)(2,1)S(1)} collective-permute-done((bf16[2,64,1792]{2,1,0:T(8,128)(2,1)S(1)}, bf16[2,64,1792]{2,1,0:T(8,128)(2,1)S(1)}, u32[]{:S(2)}, u32[]{:S(2)}) %collective-permute-start.31) | collective-permute-done | bytes 458784 | tf_op jit(solution)/shard_map/ppermute | solution.py:23
  233.0 16.5 %collective-permute-done.32 = bf16[2,64,1792]{2,1,0:T(8,128)(2,1)} collective-permute-done((bf16[2,64,1792]{2,1,0:T(8,128)(2,1)}, bf16[2,64,1792]{2,1,0:T(8,128)(2,1)}, u32[]{:S(2)}, u32[]{:S(2)}) %collective-permute-start.32) | collective-permute-done | bytes 458784 | tf_op jit(solution)/shard_map/ppermute | solution.py:23
  265.3 9.9 %collective-permute-done.34 = bf16[2,64,1792]{2,1,0:T(8,128)(2,1)} collective-permute-done((bf16[2,64,1792]{2,1,0:T(8,128)(2,1)}, bf16[2,64,1792]{2,1,0:T(8,128)(2,1)}, u32[]{:S(2)}, u32[]{:S(2)}) %collective-permute-start.34) | collective-permute-done | bytes 458784 | tf_op jit(solution)/shard_map/ppermute | solution.py:23
  278.8 4.8 fusion.15
  286.6 3.7 fusion.77
  299.9 5.8 %convolution_convert_fusion.1 = bf16[1216,1792]{1,0:T(8,128)(2,1)} fusion(bf16[512,1216]{1,0:T(8,128)(2,1)S(1)} %copy-done.71, bf16[128,1792]{1,0:T(8,128)(2,1)S(1)} %bitcast.301, bf16[128,1792]{1,0:T(8,128)(2,1)} %bitcast.76, bf16[128,1792]{1,0:T(8,128)(2,1)} %bitcast.75, bf16[128,1792]{1,0:T(8,128)(2,1)} %bitcast.74), kind=kOutput, calls=%fused_computation.1 | convolution fusion | flops 2240888832 | bytes 7438336 | tf_op jit(solution)/shard_map/dot_general | solution.py:18
  305.7 8.4 %collective-permute-done.37 = bf16[2,64,1792]{2,1,0:T(8,128)(2,1)S(1)} collective-permute-done((bf16[2,64,1792]{2,1,0:T(8,128)(2,1)S(1)}, bf16[2,64,1792]{2,1,0:T(8,128)(2,1)S(1)}, u32[]{:S(2)}, u32[]{:S(2)}) %collective-permute-start.37) | collective-permute-done | bytes 458784 | tf_op jit(solution)/shard_map/ppermute | solution.py:23
  316.3 10.8 %convolution_convert_fusion = bf16[1792,2432]{1,0:T(8,128)(2,1)} fusion(bf16[512,1792]{1,0:T(8,128)(2,1)} %pad_maximum_fusion.2, bf16[512,2432]{1,0:T(8,128)(2,1)} %pad_maximum_fusion), kind=kOutput, calls=%fused_computation | convolution fusion | flops 4467097600 | bytes 13041664 | tf_op jit(solution)/shard_map/dot_general | solution.py:18
  327.1 7.6 %copy.77 = bf16[4,4,2,56,2432]{4,3,1,2,0:T(8,128)(2,1)} copy(bf16[4,4,2,56,2432]{4,3,2,1,0:T(8,128)(2,1)} %bitcast.278) | data formatting | bytes 17432576 | tf_op jit(solution)/shard_map/reshape | solution.py:537
  344.1 6.6 %collective-permute-done.40.x1 = bf16[2,64,1792]{2,1,0:T(8,128)(2,1)S(1)} collective-permute-done((bf16[2,64,1792]{2,1,0:T(8,128)(2,1)S(1)}, bf16[2,64,1792]{2,1,0:T(8,128)(2,1)S(1)}, u32[]{:S(2)}, u32[]{:S(2)}) %collective-permute-start.40) | collective-permute-done | bytes 458784 | tf_op jit(solution)/shard_map/ppermute | solution.py:23
  350.7 8.1 %collective-permute-done.41.x2 = bf16[2,64,1792]{2,1,0:T(8,128)(2,1)S(1)} collective-permute-done((bf16[2,64,1792]{2,1,0:T(8,128)(2,1)S(1)}, bf16[2,64,1792]{2,1,0:T(8,128)(2,1)S(1)}, u32[]{:S(2)}, u32[]{:S(2)}) %collective-permute-start.41) | collective-permute-done | bytes 458784 | tf_op jit(solution)/shard_map/ppermute | solution.py:23
  372.2 4.2 collective-permute-done.45.got2
  382.3 13.0 %shard_map.225 = bf16[2,4,144,256]{3,2,1,0:T(8,128)(2,1)S(1)} custom-call(s32[3]{0:T(128)S(1)} %pad_add_fusion.ids, bf16[4,144,512]{2,1,0:T(8,128)(2,1)S(1)} %copy-done.21, f32[4,512,128]{2,1,0:T(8,128)S(1)} %get-tuple-element.275.res, bf16[2,112,256]{2,1,0:T(8,128)(2,1)S(1)} %get-tuple-element.293.got0, bf16[2,112,256]{2,1,0:T(8,128)(2,1)} %collective-permute-done.44.got1, ...), custom_call_target="tpu_custom_call" | custom-call | tf_op jit(solution)/shard_map/pallas_call | solution.py:360
  405.2 7.9 %collective-permute-done.52.g2 = bf16[2,144,256]{2,1,0:T(8,128)(2,1)S(1)} collective-permute-done((bf16[2,144,256]{2,1,0:T(8,128)(2,1)S(1)}, bf16[2,144,256]{2,1,0:T(8,128)(2,1)S(1)}, u32[]{:S(2)}, u32[]{:S(2)}) %collective-permute-start.52) | collective-permute-done | bytes 147488 | tf_op jit(solution)/shard_map/ppermute | solution.py:23
  417.8 3.7 shard_map.226
  429.8 12.7 %collective-permute-done.55 = bf16[4,56,576]{2,1,0:T(8,128)(2,1)S(1)} collective-permute-done((bf16[4,56,576]{2,1,0:T(8,128)(2,1)S(1)}, bf16[4,56,576]{2,1,0:T(8,128)(2,1)S(1)}, u32[]{:S(2)}, u32[]{:S(2)}) %collective-permute-start.55) | collective-permute-done | bytes 258080 | tf_op jit(solution)/shard_map/ppermute | solution.py:23
  451.6 11.3 %collective-permute-done.59 = bf16[4,56,576]{2,1,0:T(8,128)(2,1)} collective-permute-done((bf16[4,56,576]{2,1,0:T(8,128)(2,1)S(1)}, bf16[4,56,576]{2,1,0:T(8,128)(2,1)}, u32[]{:S(2)}, u32[]{:S(2)}) %collective-permute-start.59) | collective-permute-done | bytes 258080 | tf_op jit(solution)/shard_map/ppermute | solution.py:23
  463.0 8.7 %collective-permute-done.60 = bf16[4,56,576]{2,1,0:T(8,128)(2,1)} collective-permute-done((bf16[4,56,576]{2,1,0:T(8,128)(2,1)}, bf16[4,56,576]{2,1,0:T(8,128)(2,1)}, u32[]{:S(2)}, u32[]{:S(2)}) %collective-permute-start.60) | collective-permute-done | bytes 258080 | tf_op jit(solution)/shard_map/ppermute | solution.py:23
  (423 shorter events, 223.1 us)
Async XLA Ops:
  7.2 88.7 %all-gather.9.cloned.1.call-start = ((), (), s32[]{:S(2)}) async-start(), calls=%async_computation.6 | async-start | bytes 4902912 | tf_op jit(solution)/shard_map/all_gather | solution.py:405
  7.9 174.2 %all-gather.5.cloned.1.call-start = ((), (), s32[]{:S(2)}) async-start(), calls=%async_computation.2 | async-start | bytes 9805824 | tf_op jit(solution)/shard_map/all_gather | solution.py:405
  13.0 15.5 %collective-permute-start.3 = (bf16[56,2432]{1,0:T(8,128)(2,1)S(1)}, bf16[56,2432]{1,0:T(8,128)(2,1)}, u32[]{:S(2)}, u32[]{:S(2)}) collective-permute-start(bf16[56,2432]{1,0:T(8,128)(2,1)S(1)} %get-tuple-element.184), channel_id=1, source_target_pairs={{0,2},{2,0},{4,6},{6,4},{1,3},{3,1},{5,7},{7,5},{8,10},{10,8},{12,... | collective-permute-start | bytes 817160 | tf_op jit(solution)/shard_map/ppermute | solution.py:23
  16.1 14.8 %collective-permute-start.4 = (bf16[56,2432]{1,0:T(8,128)(2,1)S(1)}, bf16[56,2432]{1,0:T(8,128)(2,1)S(1)}, u32[]{:S(2)}, u32[]{:S(2)}) collective-permute-start(bf16[56,2432]{1,0:T(8,128)(2,1)S(1)} %get-tuple-element.185), channel_id=1, source_target_pairs={{0,4},{2,6},{4,0},{6,2},{1,5},{3,7},{5,1},{7,3},{8,12},{10,14},{12... | collective-permute-start | bytes 817160 | tf_op jit(solution)/shard_map/ppermute | solution.py:23
  32.4 20.0 %collective-permute-start.5 = (bf16[2,64,1792]{2,1,0:T(8,128)(2,1)S(1)}, bf16[2,64,1792]{2,1,0:T(8,128)(2,1)S(1)}, u32[]{:S(2)}, u32[]{:S(2)}) collective-permute-start(bf16[2,64,1792]{2,1,0:T(8,128)(2,1)S(1)} %fusion.24.x0), channel_id=1, source_target_pairs={{0,8},{8,0},{16,24},{24,16},{1,9},{9,1},{17,25},{25,17},{2,10},{10... | collective-permute-start | bytes 1376264 | tf_op jit(solution)/shard_map/ppermute | solution.py:23
  34.0 23.7 %collective-permute-start.6 = (bf16[2,64,1792]{2,1,0:T(8,128)(2,1)S(1)}, bf16[2,64,1792]{2,1,0:T(8,128)(2,1)S(1)}, u32[]{:S(2)}, u32[]{:S(2)}) collective-permute-start(bf16[2,64,1792]{2,1,0:T(8,128)(2,1)S(1)} %fusion.24.x0), channel_id=1, source_target_pairs={{0,16},{8,24},{16,0},{24,8},{1,17},{9,25},{17,1},{25,9},{2,18},{10... | collective-permute-start | bytes 1376264 | tf_op jit(solution)/shard_map/ppermute | solution.py:23
  81.2 14.6 %collective-permute-start.19 = (bf16[4,56,1792]{2,1,0:T(8,128)(2,1)}, bf16[4,56,1792]{2,1,0:T(8,128)(2,1)}, u32[]{:S(2)}, u32[]{:S(2)}) collective-permute-start(bf16[4,56,1792]{2,1,0:T(8,128)(2,1)} %bitcast_dynamic-update-slice_fusion.11), channel_id=1, source_target_pairs={{0,1},{1,0},{2,3},{3,2},{4,5},{5,4},{6,7},{7,6},{8,9},{9,8},{10,11... | collective-permute-start | bytes 2408456 | tf_op jit(solution)/shard_map/ppermute | solution.py:23
  95.9 16.2 %collective-permute-start.20 = (bf16[56,2432]{1,0:T(8,128)(2,1)}, bf16[56,2432]{1,0:T(8,128)(2,1)S(1)}, u32[]{:S(2)}, u32[]{:S(2)}) collective-permute-start(bf16[56,2432]{1,0:T(8,128)(2,1)} %get-tuple-element.220), channel_id=1, source_target_pairs={{0,6},{2,4},{4,2},{6,0},{1,7},{3,5},{5,3},{7,1},{8,14},{10,12},{12... | collective-permute-start | bytes 817160 | tf_op jit(solution)/shard_map/ppermute | solution.py:23
  112.9 221.8 %all-gather.7.cloned.1.call-start = ((), (), s32[]{:S(2)}) async-start(), calls=%async_computation.3 | async-start | bytes 1081344 | tf_op jit(solution)/shard_map/all_gather | solution.py:506
  132.5 17.1 %collective-permute-start.25 = (bf16[2,64,1792]{2,1,0:T(8,128)(2,1)S(1)}, bf16[2,64,1792]{2,1,0:T(8,128)(2,1)S(1)}, u32[]{:S(2)}, u32[]{:S(2)}) collective-permute-start(bf16[2,64,1792]{2,1,0:T(8,128)(2,1)S(1)} %get-tuple-element.231), channel_id=1, source_target_pairs={{0,8},{8,0},{16,24},{24,16},{1,9},{9,1},{17,25},{25,17},{2,10},{10... | collective-permute-start | bytes 1376264 | tf_op jit(solution)/shard_map/ppermute | solution.py:23
  136.5 30.4 %collective-permute-start.27 = (bf16[2,64,1792]{2,1,0:T(8,128)(2,1)S(1)}, bf16[2,64,1792]{2,1,0:T(8,128)(2,1)S(1)}, u32[]{:S(2)}, u32[]{:S(2)}) collective-permute-start(bf16[2,64,1792]{2,1,0:T(8,128)(2,1)S(1)} %get-tuple-element.233), channel_id=1, source_target_pairs={{0,24},{8,16},{16,8},{24,0},{1,25},{9,17},{17,9},{25,1},{2,26},{10... | collective-permute-start | bytes 1376264 | tf_op jit(solution)/shard_map/ppermute | solution.py:23
  169.2 20.6 %collective-permute-start.28 = (bf16[2,64,1792]{2,1,0:T(8,128)(2,1)}, bf16[2,64,1792]{2,1,0:T(8,128)(2,1)}, u32[]{:S(2)}, u32[]{:S(2)}) collective-permute-start(bf16[2,64,1792]{2,1,0:T(8,128)(2,1)} %multiply_convert_fusion.3), channel_id=1, source_target_pairs={{0,2},{2,0},{4,6},{6,4},{1,3},{3,1},{5,7},{7,5},{8,10},{10,8},{12,... | collective-permute-start | bytes 1376264 | tf_op jit(solution)/shard_map/ppermute | solution.py:23
  172.4 19.5 %collective-permute-start.29 = (bf16[2,64,1792]{2,1,0:T(8,128)(2,1)}, bf16[2,64,1792]{2,1,0:T(8,128)(2,1)}, u32[]{:S(2)}, u32[]{:S(2)}) collective-permute-start(bf16[2,64,1792]{2,1,0:T(8,128)(2,1)} %multiply_convert_fusion.3), channel_id=1, source_target_pairs={{0,4},{2,6},{4,0},{6,2},{1,5},{3,7},{5,1},{7,3},{8,12},{10,14},{12... | collective-permute-start | bytes 1376264 | tf_op jit(solution)/shard_map/ppermute | solution.py:23
  229.2 20.3 %collective-permute-start.32 = (bf16[2,64,1792]{2,1,0:T(8,128)(2,1)}, bf16[2,64,1792]{2,1,0:T(8,128)(2,1)}, u32[]{:S(2)}, u32[]{:S(2)}) collective-permute-start(bf16[2,64,1792]{2,1,0:T(8,128)(2,1)} %slice_bitcast_fusion.6), channel_id=1, source_target_pairs={{0,2},{2,0},{4,6},{6,4},{1,3},{3,1},{5,7},{7,5},{8,10},{10,8},{12,... | collective-permute-start | bytes 1376264 | tf_op jit(solution)/shard_map/ppermute | solution.py:23
  230.9 21.8 %collective-permute-start.33 = (bf16[2,64,1792]{2,1,0:T(8,128)(2,1)}, bf16[2,64,1792]{2,1,0:T(8,128)(2,1)}, u32[]{:S(2)}, u32[]{:S(2)}) collective-permute-start(bf16[2,64,1792]{2,1,0:T(8,128)(2,1)} %fusion.31), channel_id=1, source_target_pairs={{0,4},{2,6},{4,0},{6,2},{1,5},{3,7},{5,1},{7,3},{8,12},{10,14},{12... | collective-permute-start | bytes 1376264 | tf_op jit(solution)/shard_map/ppermute | solution.py:23
  257.5 17.7 %collective-permute-start.34 = (bf16[2,64,1792]{2,1,0:T(8,128)(2,1)}, bf16[2,64,1792]{2,1,0:T(8,128)(2,1)}, u32[]{:S(2)}, u32[]{:S(2)}) collective-permute-start(bf16[2,64,1792]{2,1,0:T(8,128)(2,1)} %fusion.72), channel_id=1, source_target_pairs={{0,2},{2,0},{4,6},{6,4},{1,3},{3,1},{5,7},{7,5},{8,10},{10,8},{12,... | collective-permute-start | bytes 1376264 | tf_op jit(solution)/shard_map/ppermute | solution.py:23
  257.5 20.8 %collective-permute-start.35 = (bf16[2,64,1792]{2,1,0:T(8,128)(2,1)}, bf16[2,64,1792]{2,1,0:T(8,128)(2,1)}, u32[]{:S(2)}, u32[]{:S(2)}) collective-permute-start(bf16[2,64,1792]{2,1,0:T(8,128)(2,1)} %fusion.72), channel_id=1, source_target_pairs={{0,4},{2,6},{4,0},{6,2},{1,5},{3,7},{5,1},{7,3},{8,12},{10,14},{12... | collective-permute-start | bytes 1376264 | tf_op jit(solution)/shard_map/ppermute | solution.py:23
  265.1 149.3 %reduce-scatter.3.cloned.1.call-start = ((), (), s32[]{:S(2)}) async-start(), calls=%async_computation.4 | async-start | bytes 9805824 | tf_op jit(solution)/shard_map/reduce_scatter | solution.py:408
  298.3 15.8 %collective-permute-start.37 = (bf16[2,64,1792]{2,1,0:T(8,128)(2,1)S(1)}, bf16[2,64,1792]{2,1,0:T(8,128)(2,1)S(1)}, u32[]{:S(2)}, u32[]{:S(2)}) collective-permute-start(bf16[2,64,1792]{2,1,0:T(8,128)(2,1)S(1)} %bitcast.295), channel_id=1, source_target_pairs={{0,2},{2,0},{4,6},{6,4},{1,3},{3,1},{5,7},{7,5},{8,10},{10,8},{12,... | collective-permute-start | bytes 1376264 | tf_op jit(solution)/shard_map/ppermute | solution.py:23
  316.1 18.6 %collective-permute-start.38 = (bf16[2,64,1792]{2,1,0:T(8,128)(2,1)}, bf16[2,64,1792]{2,1,0:T(8,128)(2,1)}, u32[]{:S(2)}, u32[]{:S(2)}) collective-permute-start(bf16[2,64,1792]{2,1,0:T(8,128)(2,1)} %get-tuple-element.266), channel_id=1, source_target_pairs={{0,2},{2,0},{4,6},{6,4},{1,3},{3,1},{5,7},{7,5},{8,10},{10,8},{12,... | collective-permute-start | bytes 1376264 | tf_op jit(solution)/shard_map/ppermute | solution.py:23
  316.2 18.5 %collective-permute-start.39 = (bf16[2,64,1792]{2,1,0:T(8,128)(2,1)S(1)}, bf16[2,64,1792]{2,1,0:T(8,128)(2,1)}, u32[]{:S(2)}, u32[]{:S(2)}) collective-permute-start(bf16[2,64,1792]{2,1,0:T(8,128)(2,1)S(1)} %add_convert_fusion), channel_id=1, source_target_pairs={{0,4},{2,6},{4,0},{6,2},{1,5},{3,7},{5,1},{7,3},{8,12},{10,14},{12... | collective-permute-start | bytes 1376264 | tf_op jit(solution)/shard_map/ppermute | solution.py:23
  334.7 151.4 %reduce-scatter.5.cloned.1.call-start = ((), (), s32[]{:S(2)}) async-start(), calls=%async_computation.5 | async-start | bytes 4902912 | tf_op jit(solution)/shard_map/reduce_scatter | solution.py:408
  340.6 18.2 %collective-permute-start.41 = (bf16[2,64,1792]{2,1,0:T(8,128)(2,1)S(1)}, bf16[2,64,1792]{2,1,0:T(8,128)(2,1)S(1)}, u32[]{:S(2)}, u32[]{:S(2)}) collective-permute-start(bf16[2,64,1792]{2,1,0:T(8,128)(2,1)S(1)} %get-tuple-element.278.x0), channel_id=1, source_target_pairs={{0,16},{8,24},{16,0},{24,8},{1,17},{9,25},{17,1},{25,9},{2,18},{10... | collective-permute-start | bytes 1376264 | tf_op jit(solution)/shard_map/ppermute | solution.py:23
  340.6 18.2 %collective-permute-start.42 = (bf16[2,64,1792]{2,1,0:T(8,128)(2,1)S(1)}, bf16[2,64,1792]{2,1,0:T(8,128)(2,1)S(1)}, u32[]{:S(2)}, u32[]{:S(2)}) collective-permute-start(bf16[2,64,1792]{2,1,0:T(8,128)(2,1)S(1)} %get-tuple-element.278.x0), channel_id=1, source_target_pairs={{0,24},{8,16},{16,8},{24,0},{1,25},{9,17},{17,9},{25,1},{2,26},{10... | collective-permute-start | bytes 1376264 | tf_op jit(solution)/shard_map/ppermute | solution.py:23
  378.7 16.5 %collective-permute-start.48 = (bf16[56,1792]{1,0:T(8,128)(2,1)S(1)}, bf16[56,1792]{1,0:T(8,128)(2,1)S(1)}, u32[]{:S(2)}, u32[]{:S(2)}) collective-permute-start(bf16[56,1792]{1,0:T(8,128)(2,1)S(1)} %get-tuple-element.383), channel_id=1, source_target_pairs={{0,2},{2,0},{4,6},{6,4},{1,3},{3,1},{5,7},{7,5},{8,10},{10,8},{12,... | collective-permute-start | bytes 602120 | tf_op jit(solution)/shard_map/ppermute | solution.py:23
  425.0 17.6 %collective-permute-start.57 = (bf16[2,64,1792]{2,1,0:T(8,128)(2,1)S(1)}, bf16[2,64,1792]{2,1,0:T(8,128)(2,1)S(1)}, u32[]{:S(2)}, u32[]{:S(2)}) collective-permute-start(bf16[2,64,1792]{2,1,0:T(8,128)(2,1)S(1)} %get-tuple-element.312), channel_id=1, source_target_pairs={{0,8},{8,0},{16,24},{24,16},{1,9},{9,1},{17,25},{25,17},{2,10},{10... | collective-permute-start | bytes 1376264 | tf_op jit(solution)/shard_map/ppermute | solution.py:23
  427.3 15.3 %collective-permute-start.58 = (bf16[2,64,1792]{2,1,0:T(8,128)(2,1)S(1)}, bf16[2,64,1792]{2,1,0:T(8,128)(2,1)S(1)}, u32[]{:S(2)}, u32[]{:S(2)}) collective-permute-start(bf16[2,64,1792]{2,1,0:T(8,128)(2,1)S(1)} %get-tuple-element.313), channel_id=1, source_target_pairs={{0,16},{8,24},{16,0},{24,8},{1,17},{9,25},{17,1},{25,9},{2,18},{10... | collective-permute-start | bytes 1376264 | tf_op jit(solution)/shard_map/ppermute | solution.py:23
  427.3 15.3 %collective-permute-start.56 = (bf16[56,2432]{1,0:T(8,128)(2,1)S(1)}, bf16[56,2432]{1,0:T(8,128)(2,1)S(1)}, u32[]{:S(2)}, u32[]{:S(2)}) collective-permute-start(bf16[56,2432]{1,0:T(8,128)(2,1)S(1)} %get-tuple-element.311), channel_id=1, source_target_pairs={{0,4},{2,6},{4,0},{6,2},{1,5},{3,7},{5,1},{7,3},{8,12},{10,14},{12... | collective-permute-start | bytes 817160 | tf_op jit(solution)/shard_map/ppermute | solution.py:23
  443.5 28.2 %collective-permute-start.61 = (bf16[2,64,1792]{2,1,0:T(8,128)(2,1)}, bf16[2,64,1792]{2,1,0:T(8,128)(2,1)}, u32[]{:S(2)}, u32[]{:S(2)}) collective-permute-start(bf16[2,64,1792]{2,1,0:T(8,128)(2,1)} %get-tuple-element.319), channel_id=1, source_target_pairs={{0,24},{8,16},{16,8},{24,0},{1,25},{9,17},{17,9},{25,1},{2,26},{10... | collective-permute-start | bytes 1376264 | tf_op jit(solution)/shard_map/ppermute | solution.py:23
  445.0 26.6 %collective-permute-start.62 = (bf16[56,2432]{1,0:T(8,128)(2,1)}, bf16[56,2432]{1,0:T(8,128)(2,1)S(1)}, u32[]{:S(2)}, u32[]{:S(2)}) collective-permute-start(bf16[56,2432]{1,0:T(8,128)(2,1)} %get-tuple-element.320), channel_id=1, source_target_pairs={{0,6},{2,4},{4,2},{6,0},{1,7},{3,5},{5,3},{7,1},{8,14},{10,12},{12... | collective-permute-start | bytes 817160 | tf_op jit(solution)/shard_map/ppermute | solution.py:23
  448.1 14.8 %collective-permute-start.59 = (bf16[4,56,576]{2,1,0:T(8,128)(2,1)S(1)}, bf16[4,56,576]{2,1,0:T(8,128)(2,1)}, u32[]{:S(2)}, u32[]{:S(2)}) collective-permute-start(bf16[4,56,576]{2,1,0:T(8,128)(2,1)S(1)} %get-tuple-element.317), channel_id=1, source_target_pairs={{0,2},{2,0},{4,6},{6,4},{1,3},{3,1},{5,7},{7,5},{8,10},{10,8},{12,... | collective-permute-start | bytes 774152 | tf_op jit(solution)/shard_map/ppermute | solution.py:23
  448.2 23.4 %collective-permute-start.60 = (bf16[4,56,576]{2,1,0:T(8,128)(2,1)}, bf16[4,56,576]{2,1,0:T(8,128)(2,1)}, u32[]{:S(2)}, u32[]{:S(2)}) collective-permute-start(bf16[4,56,576]{2,1,0:T(8,128)(2,1)} %fusion.37), channel_id=1, source_target_pairs={{0,4},{2,6},{4,0},{6,2},{1,5},{3,7},{5,1},{7,3},{8,12},{10,14},{12... | collective-permute-start | bytes 774152 | tf_op jit(solution)/shard_map/ppermute | solution.py:23
  (133 other events, 1231.2 us)
Sparse Core Ops, SparseCore 0:
  9.9 51.2 all-gather.8
  113.0 69.1 all-gather.4
  265.2 54.7 all-gather.6
  334.8 73.0 reduce-scatter.2
  411.2 64.9 reduce-scatter.4
where the time goes:
time: 512 us; the launch traced here: 504 us
  waiting for transfers between devices  225 us (44%)
  starting transfers between devices  82.6 us (16%)
  local copies, waits for them, and re-layouts  59.4 us (12%)
  other arithmetic  43.3 us (8%)
  matrix products  40.1 us (8%)
  Pallas kernels  35.8 us (7%)
  between operations  17.9 us (3%)
    ppermute x68, waiting for transfers between devices, swap(): return lax.ppermute(x, axis, [(i, i ^ o) for i in range(n)])  215 us
    ppermute x68, starting transfers between devices, swap(): return lax.ppermute(x, axis, [(i, i ^ o) for i in range(n)])  81.7 us
    dot_general x10, matrix products, dot(): lax.dot_general(a, b, (((ca,), (cb,)), ((), ())), preferred_element_type=...  40.1 us
    pallas_call x9, Pallas kernels, call(): pl.pallas_call(body, out_shape=outs, in_specs=[pl.BlockSpec(memory_space=...  35.8 us
    unnamed x184, local copies, waits for them, and re-layouts  17.8 us
    dynamic_update_slice x20, local copies, waits for them, and re-layouts, in_place(): whole = lax.dynamic_update_index_in_dim(whole, x, me ^ o, 0)  12.1 us
  transfers between devices with their start and end apart: 73, of which 38 were waited for; matrix products, arithmetic and copies ran while one was open for 20% of the time, Pallas kernels for 6%

commit v1 on v0

--- a/solution.py
+++ b/solution.py
@@ -288,7 +288,9 @@
         grad[(k % cores) ^ c, (k // cores) ^ z] = total[k * drow : (k + 1) * drow].astype(bf16)
 
 
-def qkv_back_kernel(hd, copies, fw, vw, ids, g0, g1, g2, g3, x, w, grad, own, send, pieces, cols):
+def qkv_back_kernel(
+    hd, copies, fw, vw, ids, g0, g1, g2, g3, x0, x1, x2, x3, w, grad, own, send, pieces, cols
+):
     cores, pw, lanes = g0.shape
     seqs, slot = own.shape[:2]
     z, c = ids[2], ids[1] % cores
@@ -307,6 +309,7 @@
         own[s] = part[:slot]
         for o in range(1, 4):
             send[o - 1, s] = part[o * slot : (o + 1) * slot].astype(bf16)
+    x = jnp.concatenate([rows_of((x0, x1, x2, x3), s) for s in range(seqs)], axis=0)
     drow, half = grad.shape[3], x.shape[1] // 2
     for i in range(2):
         total = dot(x[:, i * half : (i + 1) * half], rows, 0, 0)
@@ -316,8 +319,13 @@
             grad[(at % cores) ^ c, (at // cores % 4) ^ z, at // (4 * cores)] = block
 
 
-def cut_kernel(nh, run, ids, gate, up, out):
-    z = ids[2]
+def cut_kernel(nh, run, ids, gate, up, wq, wk, wv, out, heads):
+    h, z = ids[0], ids[2]
+    qw, vw = wq.shape[1] // nh, wv.shape[1] // nh
+    for k in range(nh):
+        parts = [wq[:, k * qw : (k + 1) * qw], wk[:, k * qw : (k + 1) * qw]]
+        parts.append(wv[:, k * vw : (k + 1) * vw])
+        heads[k ^ h] = jnp.concatenate([x.astype(f32) for x in parts], axis=1).astype(bf16)
     for zz in range(4):
         parts = []
         for w in (gate, up):
@@ -398,19 +406,23 @@
     n = nb * slot * nh // sb
     ids = jnp.stack([h, b, lax.axis_index(LINE)]).astype(jnp.int32)
 
-    def columns(ws):
-        return jnp.concatenate([w.reshape(drow, nh, -1).transpose(1, 0, 2) for w in ws], axis=2)
-
     def gathered(x):
         return lax.all_gather(x[None], CROSS, axis=0, tiled=True)
 
     def summed(shares):
         return lax.psum_scatter(shares, CROSS, scatter_dimension=0)
 
-    qkv_cols = columns((w_query, w_key, w_value))
     run = w_gate.shape[1] // (4 * nh)
-    feed = jax.ShapeDtypeStruct((4, drow, 2 * ffl), bf16)
-    ffn_cols = call(functools.partial(cut_kernel, nh, run), ids, [w_gate, w_up], feed, [])
+    ffn_cols, qkv_cols = call(
+        functools.partial(cut_kernel, nh, run),
+        ids,
+        [w_gate, w_up, w_query, w_key, w_value],
+        [
+            jax.ShapeDtypeStruct((4, drow, 2 * ffl), bf16),
+            jax.ShapeDtypeStruct((nh, drow, hd * pw), bf16),
+        ],
+        [],
+    )
 
     place = (h * nb + b) * slot + lax.broadcasted_iota(jnp.int32, (seqs, slot), 1)
     valid = (place < lengths[:, None]).astype(f32)[..., None]
@@ -420,21 +432,23 @@
     scale_one = rms_scale(tokens_f)
     own_rows = (tokens_f * scale_one * gain_attn).astype(bf16)
     (*got, ffn_1, ffn_2), (own_rows,) = window(
-        turn_moves(qkv_cols, HEAD) + [(ffn_cols[1], LINE, 1), (ffn_cols[2], LINE, 2)], (own_rows,)
-    )
-    qkv_cols = turned(qkv_cols, got, HEAD)
+        return_moves(qkv_cols, HEAD) + [(ffn_cols[1], LINE, 1), (ffn_cols[2], LINE, 2)], (own_rows,)
+    )
+    qkv_cols = in_place([qkv_cols[0]] + got, h)
     (row_1, row_2, qkv_near, qkv_far), _ = window(
         [(own_rows, HEAD, 1), (own_rows, HEAD, 2), (qkv_cols, LINE, 1), (qkv_cols, LINE, 2)]
     )
-    (row_3, qkv_last, out_near, out_far), _ = window(
-        [(own_rows, HEAD, 3), (qkv_far, LINE, 1), (w_out, LINE, 1), (w_out, LINE, 2)]
+    (row_3, qkv_last, ffn_3), _ = window(
+        [(own_rows, HEAD, 3), (qkv_far, LINE, 1), (ffn_cols[3], LINE, 3)]
     )
     attn_rows = [own_rows, row_1, row_2, row_3]
     qkv_w = line_whole([qkv_cols, qkv_near, qkv_far, qkv_last])
-    (*got, out_last), _ = window(over(qkv_w, "c") + [(out_far, LINE, 1)])
+    got, (ffn_cols,) = window(
+        over(qkv_w, "c"), (line_whole([ffn_cols[0], ffn_1, ffn_2, ffn_3]),)
+    )
+    ffn_w = gathered(ffn_cols)
+    ffn_w = ffn_w.reshape(nh, cores, 4, drow, -1).transpose(0, 2, 1, 3, 4).reshape(width, -1)
     qkv_w = core_end(qkv_w, got).transpose(2, 0, 1, 3, 4).reshape(width, -1)
-    out_w = line_whole([w_out, out_near, out_far, out_last])
-    normed_attn = jnp.concatenate(attn_rows, axis=1).reshape(-1, width)
     geometry = (nh, nb, slot, sb)
     piece = lambda rows: jax.ShapeDtypeStruct((cores, 4, rows, lanes), bf16)
     held = lambda rows: [pltpu.VMEM((pairs, rows, lanes), bf16)]
@@ -449,13 +463,9 @@
         held(pw),
         room=10,
     )
-    pieces, out_w = tie(pieces, out_w)
-    sent, got, (ffn_last, down_w) = exchange(
-        pieces, far_moves=over(out_w, "c"), far_beside=(ffn_cols[3], gathered(w_down))
-    )
+    sent, _, (down_w, w_out_late) = exchange(pieces, far_beside=(gathered(w_down), w_out))
     down_w = down_w.reshape(-1, width)
-    ffn_3 = swap(ffn_last, LINE, 3)
-    out_w = core_end(out_w, got).reshape(-1, width)
+    out_near, out_far = swap(w_out_late, LINE, 1), swap(w_out_late, LINE, 2)
     tiles, res, mixed_out = call(
         functools.partial(fwd_kernel, *geometry),
         ids,
@@ -468,18 +478,20 @@
         [pltpu.VMEM((n, sb, 128), bf16)],
         room=14,
     )
-    mixed_out, ffn_3 = tie(mixed_out, ffn_3)
-    ffn_w = gathered(line_whole([ffn_cols[0], ffn_1, ffn_2, ffn_3]))
-    ffn_w = ffn_w.reshape(nh, cores, 4, drow, -1).transpose(0, 2, 1, 3, 4).reshape(width, -1)
+    mixed_out, out_near, out_far = tie(mixed_out, out_near, out_far)
+    mixed_got, (out_last,), _ = exchange(mixed_out, far_moves=[(out_far, LINE, 1)])
+    out_w = line_whole([w_out, out_near, out_far, out_last])
+    got, (out_w,) = window(over(out_w, "c"), (out_w,))
+    out_w = core_end(out_w, got).reshape(-1, width)
     mixed, attn_own, attn_part = call(
         functools.partial(out_kernel, hd, copies),
         ids,
-        exchange(mixed_out)[0] + [out_w],
+        mixed_got + [out_w],
         [jax.ShapeDtypeStruct((hd * vw, seqs * lanes), bf16), own_part, sent_part],
         taken(vw),
         room=10,
     )
-    got, _ = window([(attn_part[o - 1], HEAD, o) for o in range(1, 4)])
+    got, (ffn_w,) = window([(attn_part[o - 1], HEAD, o) for o in range(1, 4)], (ffn_w,))
     residual = tokens_f + plus(attn_own, got)
 
     scale_two = rms_scale(residual)
@@ -492,9 +504,9 @@
         part = dot(hidden, down_w, 1, 0).reshape(len(rows), seqs, slot, width)
         return gate, up, hidden, part
 
-    (near, far), (ffn_w,) = window([(own_rows, LINE, 1), (own_rows, LINE, 2)], (ffn_w,))
-    (last,), first = window([(far, LINE, 1)], forward(own_rows, near, far))
-    kept = [first, forward(last)]
+    (near, far), first = window([(own_rows, LINE, 1), (own_rows, LINE, 2)], forward(own_rows))
+    (last,), second = window([(far, LINE, 1)], forward(near, far))
+    kept = [first, second, forward(last)]
     part = [y for x in kept for y in x[3]]
     normed_mlp = jnp.concatenate([x.reshape(-1, width) for x in (own_rows, near, far, last)])
     hidden = jnp.concatenate([x[2] for x in kept])
@@ -522,9 +534,11 @@
         e = grad_norm * gain
         return scale_rows * (e - unit * jnp.mean(e * unit, axis=-1, keepdims=True))
 
-    (near, far), _ = window([(own_rows, LINE, 1), (own_rows, LINE, 2)])
-    (last,), first = window([(far, LINE, 1)], backward((own_rows, near, far), *kept[0][:2]))
-    back = [first, backward((last,), *kept[1][:2])]
+    (near, far), first = window(
+        [(own_rows, LINE, 1), (own_rows, LINE, 2)], backward((own_rows,), *kept[0][:2])
+    )
+    (last,), second = window([(far, LINE, 1)], backward((near, far), *kept[1][:2]))
+    back = [first, second, backward((last,), *kept[2][:2])]
     part = [y for x in back for y in x[1]]
     passing = swap(part[3].astype(bf16), LINE, 1)
     grad_both = jnp.concatenate([x[0] for x in back])
@@ -555,7 +569,7 @@
     )
     grad_out_w = plus(grad_out_w[0], out_got).astype(bf16)
     sent, grad_out_w = tie(sent, grad_out_w)
-    out_got = [swap(grad_out_w[o], LINE, o) for o in range(1, 3)]
+    out_got = [swap(grad_out_w[o], LINE, o) for o in range(1, 4)]
     grads_out = call(
         functools.partial(bwd_kernel, *geometry),
         ids,
@@ -570,31 +584,29 @@
     )
     grads_out, out_got = tie(grads_out, out_got)
     grad_qkv, _, (grad_ffn_w,) = exchange(grads_out, far_beside=(grad_ffn_w,))
-    grad_ffn_w = grad_ffn_w.reshape(4, drow, -1)
-    ffn_pieces = [pick(grad_ffn_w, lax.axis_index(LINE) ^ o) for o in range(4)]
     grad_qkv_w, own_back, attn_back = call(
         functools.partial(qkv_back_kernel, hd, copies, fw, vw),
         ids,
-        grad_qkv + [normed_attn, qkv_w],
+        grad_qkv + attn_rows + [qkv_w],
         [jax.ShapeDtypeStruct((cores, 4, nh, drow, hd * pw), bf16), own_part, sent_part],
         taken(pw) + [pltpu.VMEM((hd * pw, seqs * lanes), bf16)],
         room=14,
     )
+    grad_qkv_w, grad_ffn_w = tie(grad_qkv_w, grad_ffn_w)
+    grad_ffn_w = grad_ffn_w.reshape(4, drow, -1)
+    ffn_pieces = [pick(grad_ffn_w, lax.axis_index(LINE) ^ o) for o in range(4)]
     row_moves = [(attn_back[o - 1], HEAD, o) for o in range(1, 4)]
     got, _ = window([(grad_qkv_w[k], "c", k) for k in range(1, cores)])
     grad_qkv_w = plus(grad_qkv_w[0], got).astype(bf16)
     (passing, ffn_2, *row_got), _ = window(
         [by_way(grad_qkv_w), (ffn_pieces[2], LINE, 2)] + row_moves[:2]
     )
-    (got_1, got_2, last, ffn_3), _ = window(
-        rest_moves(grad_qkv_w, passing) + [row_moves[2], (ffn_pieces[3], LINE, 3)]
+    (got_1, got_2, last, ffn_1), _ = window(
+        rest_moves(grad_qkv_w, passing) + [row_moves[2], (ffn_pieces[1], LINE, 1)]
     )
     row_got = row_got + [last]
     grad_qkv_w = plus(grad_qkv_w[0], [got_1, got_2]).astype(bf16)
-    (*got, ffn_1, out_last), _ = window(
-        turn_moves(grad_qkv_w, HEAD) + [(ffn_pieces[1], LINE, 1), (grad_out_w[3], LINE, 3)]
-    )
-    out_got = out_got + [out_last]
+    (*got, ffn_3), _ = window(turn_moves(grad_qkv_w, HEAD) + [(ffn_pieces[3], LINE, 3)])
     grad_down, got = tie(grad_down, got)
     rows_f32 = lambda w: jax.ShapeDtypeStruct(w.shape, f32)
     one = jax.ShapeDtypeStruct((drow, 1), f32)

time: 512 us -> 479 us (0.936)
  the two profiles are of different devices: /device:TPU:0 before, /device:TPU:8 now
where the time goes in v1:
time: 479 us; the launch traced here: 471 us
  waiting for transfers between devices  197 us (41%)
  starting transfers between devices  85.5 us (18%)
  local copies, waits for them, and re-layouts  50 us (10%)
  matrix products  48.9 us (10%)
  other arithmetic  36.5 us (8%)
  Pallas kernels  35.6 us (7%)
  between operations  17.6 us (4%)
    ppermute x68, waiting for transfers between devices, swap(): return lax.ppermute(x, axis, [(i, i ^ o) for i in range(n)])  196 us
    ppermute x68, starting transfers between devices, swap(): return lax.ppermute(x, axis, [(i, i ^ o) for i in range(n)])  85.3 us
    dot_general x14, matrix products, dot(): lax.dot_general(a, b, (((ca,), (cb,)), ((), ())), preferred_element_type=...  48.9 us
    pallas_call x9, Pallas kernels, call(): pl.pallas_call(body, out_shape=outs, in_specs=[pl.BlockSpec(memory_space=...  35.6 us
    unnamed x174, local copies, waits for them, and re-layouts  20.3 us
  transfers between devices with their start and end apart: 73, of which 51 were waited for; matrix products, arithmetic and copies ran while one was open for 22% of the time, Pallas kernels for 7%

profile of v1, /device:TPU:8, one launch (start us, length us, event | category | flops | bytes accessed | tf_op | source)
XLA Modules:
  0.0 471.2 jit_solution(17974937397306954660)
XLA Ops:
  37.4 6.3 %collective-permute-done.7 = bf16[4,56,576]{2,1,0:T(8,128)(2,1)S(1)} collective-permute-done((bf16[4,56,576]{2,1,0:T(8,128)(2,1)S(1)}, bf16[4,56,576]{2,1,0:T(8,128)(2,1)S(1)}, u32[]{:S(2)}, u32[]{:S(2)}) %collective-permute-start.7) | collective-permute-done | bytes 258080 | tf_op jit(solution)/shard_map/ppermute | solution.py:23
  50.5 3.6 collective-permute-done.6.x2
  57.7 4.4 collective-permute-done.10
  62.1 3.8 collective-permute-done.11
  83.5 6.7 %collective-permute-done.15.got2 = bf16[2,144,256]{2,1,0:T(8,128)(2,1)S(1)} collective-permute-done((bf16[2,144,256]{2,1,0:T(8,128)(2,1)S(1)}, bf16[2,144,256]{2,1,0:T(8,128)(2,1)S(1)}, u32[]{:S(2)}, u32[]{:S(2)}) %collective-permute-start.15) | collective-permute-done | bytes 147488 | tf_op jit(solution)/shard_map/ppermute | solution.py:23
  99.8 7.9 %shard_map.222 = (bf16[4,144,512]{2,1,0:T(8,128)(2,1)S(1)}, f32[4,512,128]{2,1,0:T(8,128)S(1)}, bf16[2,4,112,256]{3,2,1,0:T(8,128)(2,1)S(1)}) custom-call(s32[3]{0:T(128)S(1)} %pad_add_fusion.ids, bf16[2,144,256]{2,1,0:T(8,128)(2,1)S(1)} %get-tuple-element.409.got0, bf16[2,144,256]{2,1,0:T(8,128)(2,1)S(1)} %collective-permute-done.14.got1, ...), custom_call_target="tpu_custom_call" | custom-call | tf_op jit(solution)/shard_map/pallas_call | solution.py:368
  113.1 6.7 %collective-permute-done.20.g1 = bf16[2,112,256]{2,1,0:T(8,128)(2,1)S(1)} collective-permute-done((bf16[2,112,256]{2,1,0:T(8,128)(2,1)S(1)}, bf16[2,112,256]{2,1,0:T(8,128)(2,1)S(1)}, u32[]{:S(2)}, u32[]{:S(2)}) %collective-permute-start.20) | collective-permute-done | bytes 114720 | tf_op jit(solution)/shard_map/ppermute | solution.py:23
  134.4 7.5 %copy.66 = bf16[4,4,2,56,2432]{4,3,2,1,0:T(8,128)(2,1)} copy(bf16[4,4,2,56,2432]{4,3,1,2,0:T(8,128)(2,1)} %bitcast.284) | data formatting | bytes 17432576 | tf_op jit(solution)/shard_map/transpose | solution.py:450
  143.2 10.8 %collective-permute-done.26 = bf16[2,64,1792]{2,1,0:T(8,128)(2,1)} collective-permute-done((bf16[2,64,1792]{2,1,0:T(8,128)(2,1)}, bf16[2,64,1792]{2,1,0:T(8,128)(2,1)}, u32[]{:S(2)}, u32[]{:S(2)}) %collective-permute-start.26) | collective-permute-done | bytes 458784 | tf_op jit(solution)/shard_map/ppermute | solution.py:23
  159.9 5.0 %fusion.70 = f32[128,2432]{1,0:T(8,128)S(1)} fusion(bf16[128,1792]{1,0:T(8,128)(2,1)S(1)} %bitcast.288, bf16[1792,2432]{1,0:T(8,128)(2,1)} %bitcast.266), kind=kOutput, calls=%fused_computation.211 | convolution fusion | flops 1115684864 | bytes 10420224 | tf_op jit(solution)/shard_map/dot_general | solution.py:18
  166.9 10.4 %collective-permute-done.28 = bf16[2,64,1792]{2,1,0:T(8,128)(2,1)S(1)} collective-permute-done((bf16[2,64,1792]{2,1,0:T(8,128)(2,1)S(1)}, bf16[2,64,1792]{2,1,0:T(8,128)(2,1)S(1)}, u32[]{:S(2)}, u32[]{:S(2)}) %collective-permute-start.28) | collective-permute-done | bytes 458784 | tf_op jit(solution)/shard_map/ppermute | solution.py:23
  193.7 9.4 %collective-permute-done.31 = bf16[2,64,1792]{2,1,0:T(8,128)(2,1)S(1)} collective-permute-done((bf16[2,64,1792]{2,1,0:T(8,128)(2,1)S(1)}, bf16[2,64,1792]{2,1,0:T(8,128)(2,1)S(1)}, u32[]{:S(2)}, u32[]{:S(2)}) %collective-permute-start.31) | collective-permute-done | bytes 458784 | tf_op jit(solution)/shard_map/ppermute | solution.py:23
  203.8 6.3 %collective-permute-start.33 = (bf16[2,64,1792]{2,1,0:T(8,128)(2,1)S(1)}, bf16[2,64,1792]{2,1,0:T(8,128)(2,1)S(1)}, u32[]{:S(2)}, u32[]{:S(2)}) collective-permute-start(bf16[2,64,1792]{2,1,0:T(8,128)(2,1)S(1)} %fusion.27), channel_id=1, source_target_pairs={{0,4},{2,6},{4,0},{6,2},{1,5},{3,7},{5,1},{7,3},{8,12},{10,14},{12... | collective-permute-start | bytes 1376264 | tf_op jit(solution)/shard_map/ppermute | solution.py:23
  213.1 6.0 %collective-permute-done.32 = bf16[2,64,1792]{2,1,0:T(8,128)(2,1)S(1)} collective-permute-done((bf16[2,64,1792]{2,1,0:T(8,128)(2,1)S(1)}, bf16[2,64,1792]{2,1,0:T(8,128)(2,1)S(1)}, u32[]{:S(2)}, u32[]{:S(2)}) %collective-permute-start.32) | collective-permute-done | bytes 458784 | tf_op jit(solution)/shard_map/ppermute | solution.py:23
  219.1 4.6 collective-permute-done.33
  231.5 4.0 fusion.73
  236.1 7.2 %fusion.74 = f32[128,1792]{1,0:T(8,128)} fusion(bf16[128,2432]{1,0:T(8,128)(2,1)S(1)} %pad_maximum_fusion.4, bf16[1792,2432]{1,0:T(8,128)(2,1)} %bitcast.267), kind=kOutput, calls=%fused_computation.215 | convolution fusion | flops 1115684864 | bytes 10256384 | tf_op jit(solution)/shard_map/dot_general | solution.py:18
  263.9 5.8 %convolution_convert_fusion.1 = bf16[1216,1792]{1,0:T(8,128)(2,1)} fusion(bf16[512,1216]{1,0:T(8,128)(2,1)S(1)} %copy-done.64, bf16[128,1792]{1,0:T(8,128)(2,1)S(1)} %bitcast.309, bf16[128,1792]{1,0:T(8,128)(2,1)} %bitcast.77, bf16[128,1792]{1,0:T(8,128)(2,1)} %bitcast.76, bf16[128,1792]{1,0:T(8,128)(2,1)} %bitcast.73), kind=kOutput, calls=%fused_computation.1 | convolution fusion | flops 2240888832 | bytes 7438336 | tf_op jit(solution)/shard_map/dot_general | solution.py:18
  275.5 10.9 %convolution_convert_fusion = bf16[1792,2432]{1,0:T(8,128)(2,1)} fusion(bf16[512,1792]{1,0:T(8,128)(2,1)} %pad_maximum_fusion.1, bf16[512,2432]{1,0:T(8,128)(2,1)} %pad_maximum_fusion), kind=kOutput, calls=%fused_computation | convolution fusion | flops 4467097600 | bytes 13041664 | tf_op jit(solution)/shard_map/dot_general | solution.py:18
  286.3 7.5 %copy.73 = bf16[4,4,2,56,2432]{4,3,1,2,0:T(8,128)(2,1)} copy(bf16[4,4,2,56,2432]{4,3,2,1,0:T(8,128)(2,1)} %bitcast.285) | data formatting | bytes 17432576 | tf_op jit(solution)/shard_map/reshape | solution.py:551
  305.2 10.0 %collective-permute-done.40.x1 = bf16[2,64,1792]{2,1,0:T(8,128)(2,1)S(1)} collective-permute-done((bf16[2,64,1792]{2,1,0:T(8,128)(2,1)S(1)}, bf16[2,64,1792]{2,1,0:T(8,128)(2,1)S(1)}, u32[]{:S(2)}, u32[]{:S(2)}) %collective-permute-start.40) | collective-permute-done | bytes 458784 | tf_op jit(solution)/shard_map/ppermute | solution.py:23
  315.2 6.3 %collective-permute-done.42.x3 = bf16[2,64,1792]{2,1,0:T(8,128)(2,1)S(1)} collective-permute-done((bf16[2,64,1792]{2,1,0:T(8,128)(2,1)S(1)}, bf16[2,64,1792]{2,1,0:T(8,128)(2,1)S(1)}, u32[]{:S(2)}, u32[]{:S(2)}) %collective-permute-start.42) | collective-permute-done | bytes 458784 | tf_op jit(solution)/shard_map/ppermute | solution.py:23
  332.1 6.6 %collective-permute-done.45.got2 = bf16[2,112,256]{2,1,0:T(8,128)(2,1)S(1)} collective-permute-done((bf16[2,112,256]{2,1,0:T(8,128)(2,1)}, bf16[2,112,256]{2,1,0:T(8,128)(2,1)S(1)}, u32[]{:S(2)}, u32[]{:S(2)}) %collective-permute-start.45) | collective-permute-done | bytes 114720 | tf_op jit(solution)/shard_map/ppermute | solution.py:23
  346.8 12.6 %shard_map.225 = bf16[2,4,144,256]{3,2,1,0:T(8,128)(2,1)S(1)} custom-call(s32[3]{0:T(128)S(1)} %copy-done.38, bf16[4,144,512]{2,1,0:T(8,128)(2,1)S(1)} %copy-done.22, f32[4,512,128]{2,1,0:T(8,128)S(1)} %copy-done.16, bf16[2,112,256]{2,1,0:T(8,128)(2,1)S(1)} %get-tuple-element.304.got0, bf16[2,112,256]{2,1,0:T(8,128)(2,1)S(1)} %collective-permute-done.44.got1, ...), custom_call_target="tpu_custom_call" | custom-call | tf_op jit(solution)/shard_map/pallas_call | solution.py:368
  360.3 3.6 collective-permute-done.50
  372.4 6.9 %collective-permute-done.53.g2 = bf16[2,144,256]{2,1,0:T(8,128)(2,1)S(1)} collective-permute-done((bf16[2,144,256]{2,1,0:T(8,128)(2,1)S(1)}, bf16[2,144,256]{2,1,0:T(8,128)(2,1)S(1)}, u32[]{:S(2)}, u32[]{:S(2)}) %collective-permute-start.53) | collective-permute-done | bytes 147488 | tf_op jit(solution)/shard_map/ppermute | solution.py:23
  387.0 3.7 shard_map.226
  402.2 9.6 %collective-permute-done.56 = bf16[4,56,576]{2,1,0:T(8,128)(2,1)S(1)} collective-permute-done((bf16[4,56,576]{2,1,0:T(8,128)(2,1)S(1)}, bf16[4,56,576]{2,1,0:T(8,128)(2,1)S(1)}, u32[]{:S(2)}, u32[]{:S(2)}) %collective-permute-start.56) | collective-permute-done | bytes 258080 | tf_op jit(solution)/shard_map/ppermute | solution.py:23
  411.8 4.9 %collective-permute-done.58 = bf16[2,64,1792]{2,1,0:T(8,128)(2,1)S(1)} collective-permute-done((bf16[2,64,1792]{2,1,0:T(8,128)(2,1)}, bf16[2,64,1792]{2,1,0:T(8,128)(2,1)S(1)}, u32[]{:S(2)}, u32[]{:S(2)}) %collective-permute-start.58) | collective-permute-done | bytes 458784 | tf_op jit(solution)/shard_map/ppermute | solution.py:23
  427.2 8.4 %collective-permute-done.60 = bf16[4,56,576]{2,1,0:T(8,128)(2,1)S(1)} collective-permute-done((bf16[4,56,576]{2,1,0:T(8,128)(2,1)S(1)}, bf16[4,56,576]{2,1,0:T(8,128)(2,1)S(1)}, u32[]{:S(2)}, u32[]{:S(2)}) %collective-permute-start.60) | collective-permute-done | bytes 258080 | tf_op jit(solution)/shard_map/ppermute | solution.py:23
  435.6 3.5 collective-permute-done.61
  450.6 4.5 collective-permute-done.67.p3
  (409 shorter events, 238.4 us)
Async XLA Ops:
  7.2 86.9 %all-gather.8.cloned.1.call-start = ((), (), s32[]{:S(2)}) async-start(), calls=%async_computation.5 | async-start | bytes 4902912 | tf_op jit(solution)/shard_map/all_gather | solution.py:410
  7.9 126.5 %all-gather.10.cloned.1.call-start = ((), (), s32[]{:S(2)}) async-start(), calls=%async_computation.6 | async-start | bytes 9805824 | tf_op jit(solution)/shard_map/all_gather | solution.py:410
  15.6 15.2 %collective-permute-start.4 = (bf16[56,2432]{1,0:T(8,128)(2,1)S(1)}, bf16[56,2432]{1,0:T(8,128)(2,1)S(1)}, u32[]{:S(2)}, u32[]{:S(2)}) collective-permute-start(bf16[56,2432]{1,0:T(8,128)(2,1)S(1)} %get-tuple-element.193), channel_id=1, source_target_pairs={{0,4},{2,6},{4,0},{6,2},{1,5},{3,7},{5,1},{7,3},{8,12},{10,14},{12... | collective-permute-start | bytes 817160 | tf_op jit(solution)/shard_map/ppermute | solution.py:23
  30.9 19.6 %collective-permute-start.5 = (bf16[2,64,1792]{2,1,0:T(8,128)(2,1)S(1)}, bf16[2,64,1792]{2,1,0:T(8,128)(2,1)S(1)}, u32[]{:S(2)}, u32[]{:S(2)}) collective-permute-start(bf16[2,64,1792]{2,1,0:T(8,128)(2,1)S(1)} %fusion.12.x0), channel_id=1, source_target_pairs={{0,8},{8,0},{16,24},{24,16},{1,9},{9,1},{17,25},{25,17},{2,10},{10... | collective-permute-start | bytes 1376264 | tf_op jit(solution)/shard_map/ppermute | solution.py:23
  32.4 21.6 %collective-permute-start.6 = (bf16[2,64,1792]{2,1,0:T(8,128)(2,1)S(1)}, bf16[2,64,1792]{2,1,0:T(8,128)(2,1)S(1)}, u32[]{:S(2)}, u32[]{:S(2)}) collective-permute-start(bf16[2,64,1792]{2,1,0:T(8,128)(2,1)S(1)} %fusion.12.x0), channel_id=1, source_target_pairs={{0,16},{8,24},{16,0},{24,8},{1,17},{9,25},{17,1},{25,9},{2,18},{10... | collective-permute-start | bytes 1376264 | tf_op jit(solution)/shard_map/ppermute | solution.py:23
  69.7 226.1 %all-gather.6.cloned.1.call-start = ((), (), s32[]{:S(2)}) async-start(), calls=%async_computation.2 | async-start | bytes 1081344 | tf_op jit(solution)/shard_map/all_gather | solution.py:518
  79.6 13.8 %collective-permute-start.16 = (bf16[2,144,256]{2,1,0:T(8,128)(2,1)S(1)}, bf16[2,144,256]{2,1,0:T(8,128)(2,1)S(1)}, u32[]{:S(2)}, u32[]{:S(2)}) collective-permute-start(bf16[2,144,256]{2,1,0:T(8,128)(2,1)S(1)} %get-tuple-element.217), channel_id=1, source_target_pairs={{0,6},{2,4},{4,2},{6,0},{1,7},{3,5},{5,3},{7,1},{8,14},{10,12},{12... | collective-permute-start | bytes 442376 | tf_op jit(solution)/shard_map/ppermute | solution.py:23
  128.3 14.9 %collective-permute-start.25 = (bf16[2,64,1792]{2,1,0:T(8,128)(2,1)}, bf16[2,64,1792]{2,1,0:T(8,128)(2,1)}, u32[]{:S(2)}, u32[]{:S(2)}) collective-permute-start(bf16[2,64,1792]{2,1,0:T(8,128)(2,1)} %get-tuple-element.238), channel_id=1, source_target_pairs={{0,8},{8,0},{16,24},{24,16},{1,9},{9,1},{17,25},{25,17},{2,10},{10... | collective-permute-start | bytes 1376264 | tf_op jit(solution)/shard_map/ppermute | solution.py:23
  131.6 22.4 %collective-permute-start.26 = (bf16[2,64,1792]{2,1,0:T(8,128)(2,1)}, bf16[2,64,1792]{2,1,0:T(8,128)(2,1)}, u32[]{:S(2)}, u32[]{:S(2)}) collective-permute-start(bf16[2,64,1792]{2,1,0:T(8,128)(2,1)} %get-tuple-element.239), channel_id=1, source_target_pairs={{0,16},{8,24},{16,0},{24,8},{1,17},{9,25},{17,1},{25,9},{2,18},{10... | collective-permute-start | bytes 1376264 | tf_op jit(solution)/shard_map/ppermute | solution.py:23
  131.6 22.4 %collective-permute-start.27 = (bf16[2,64,1792]{2,1,0:T(8,128)(2,1)}, bf16[2,64,1792]{2,1,0:T(8,128)(2,1)}, u32[]{:S(2)}, u32[]{:S(2)}) collective-permute-start(bf16[2,64,1792]{2,1,0:T(8,128)(2,1)} %get-tuple-element.240), channel_id=1, source_target_pairs={{0,24},{8,16},{16,8},{24,0},{1,25},{9,17},{17,9},{25,1},{2,26},{10... | collective-permute-start | bytes 1376264 | tf_op jit(solution)/shard_map/ppermute | solution.py:23
  156.1 21.2 %collective-permute-start.28 = (bf16[2,64,1792]{2,1,0:T(8,128)(2,1)S(1)}, bf16[2,64,1792]{2,1,0:T(8,128)(2,1)S(1)}, u32[]{:S(2)}, u32[]{:S(2)}) collective-permute-start(bf16[2,64,1792]{2,1,0:T(8,128)(2,1)S(1)} %multiply_convert_fusion.3), channel_id=1, source_target_pairs={{0,2},{2,0},{4,6},{6,4},{1,3},{3,1},{5,7},{7,5},{8,10},{10,8},{12,... | collective-permute-start | bytes 1376264 | tf_op jit(solution)/shard_map/ppermute | solution.py:23
  158.9 20.4 %collective-permute-start.29 = (bf16[2,64,1792]{2,1,0:T(8,128)(2,1)S(1)}, bf16[2,64,1792]{2,1,0:T(8,128)(2,1)S(1)}, u32[]{:S(2)}, u32[]{:S(2)}) collective-permute-start(bf16[2,64,1792]{2,1,0:T(8,128)(2,1)S(1)} %multiply_convert_fusion.3), channel_id=1, source_target_pairs={{0,4},{2,6},{4,0},{6,2},{1,5},{3,7},{5,1},{7,3},{8,12},{10,14},{12... | collective-permute-start | bytes 1376264 | tf_op jit(solution)/shard_map/ppermute | solution.py:23
  203.2 15.9 %collective-permute-start.32 = (bf16[2,64,1792]{2,1,0:T(8,128)(2,1)S(1)}, bf16[2,64,1792]{2,1,0:T(8,128)(2,1)S(1)}, u32[]{:S(2)}, u32[]{:S(2)}) collective-permute-start(bf16[2,64,1792]{2,1,0:T(8,128)(2,1)S(1)} %slice_bitcast_fusion.5), channel_id=1, source_target_pairs={{0,2},{2,0},{4,6},{6,4},{1,3},{3,1},{5,7},{7,5},{8,10},{10,8},{12,... | collective-permute-start | bytes 1376264 | tf_op jit(solution)/shard_map/ppermute | solution.py:23
  203.8 19.9 %collective-permute-start.33 = (bf16[2,64,1792]{2,1,0:T(8,128)(2,1)S(1)}, bf16[2,64,1792]{2,1,0:T(8,128)(2,1)S(1)}, u32[]{:S(2)}, u32[]{:S(2)}) collective-permute-start(bf16[2,64,1792]{2,1,0:T(8,128)(2,1)S(1)} %fusion.27), channel_id=1, source_target_pairs={{0,4},{2,6},{4,0},{6,2},{1,5},{3,7},{5,1},{7,3},{8,12},{10,14},{12... | collective-permute-start | bytes 1376264 | tf_op jit(solution)/shard_map/ppermute | solution.py:23
  226.7 16.5 %collective-permute-start.34 = (bf16[2,64,1792]{2,1,0:T(8,128)(2,1)}, bf16[2,64,1792]{2,1,0:T(8,128)(2,1)}, u32[]{:S(2)}, u32[]{:S(2)}) collective-permute-start(bf16[2,64,1792]{2,1,0:T(8,128)(2,1)} %fusion.67), channel_id=1, source_target_pairs={{0,2},{2,0},{4,6},{6,4},{1,3},{3,1},{5,7},{7,5},{8,10},{10,8},{12,... | collective-permute-start | bytes 1376264 | tf_op jit(solution)/shard_map/ppermute | solution.py:23
  227.0 17.4 %collective-permute-start.35 = (bf16[2,64,1792]{2,1,0:T(8,128)(2,1)}, bf16[2,64,1792]{2,1,0:T(8,128)(2,1)}, u32[]{:S(2)}, u32[]{:S(2)}) collective-permute-start(bf16[2,64,1792]{2,1,0:T(8,128)(2,1)} %fusion.67), channel_id=1, source_target_pairs={{0,4},{2,6},{4,0},{6,2},{1,5},{3,7},{5,1},{7,3},{8,12},{10,14},{12... | collective-permute-start | bytes 1376264 | tf_op jit(solution)/shard_map/ppermute | solution.py:23
  231.5 151.5 %reduce-scatter.3.cloned.1.call-start = ((), (), s32[]{:S(2)}) async-start(), calls=%async_computation.3 | async-start | bytes 9805824 | tf_op jit(solution)/shard_map/reduce_scatter | solution.py:413
  272.4 21.4 %collective-permute-start.38 = (bf16[2,64,1792]{2,1,0:T(8,128)(2,1)}, bf16[2,64,1792]{2,1,0:T(8,128)(2,1)}, u32[]{:S(2)}, u32[]{:S(2)}) collective-permute-start(bf16[2,64,1792]{2,1,0:T(8,128)(2,1)} %get-tuple-element.277), channel_id=1, source_target_pairs={{0,2},{2,0},{4,6},{6,4},{1,3},{3,1},{5,7},{7,5},{8,10},{10,8},{12,... | collective-permute-start | bytes 1376264 | tf_op jit(solution)/shard_map/ppermute | solution.py:23
  274.2 21.6 %collective-permute-start.39 = (bf16[2,64,1792]{2,1,0:T(8,128)(2,1)S(1)}, bf16[2,64,1792]{2,1,0:T(8,128)(2,1)}, u32[]{:S(2)}, u32[]{:S(2)}) collective-permute-start(bf16[2,64,1792]{2,1,0:T(8,128)(2,1)S(1)} %add_convert_fusion), channel_id=1, source_target_pairs={{0,4},{2,6},{4,0},{6,2},{1,5},{3,7},{5,1},{7,3},{8,12},{10,14},{12... | collective-permute-start | bytes 1376264 | tf_op jit(solution)/shard_map/ppermute | solution.py:23
  295.8 159.3 %reduce-scatter.5.cloned.1.call-start = ((), (), s32[]{:S(2)}) async-start(), calls=%async_computation.4 | async-start | bytes 4902912 | tf_op jit(solution)/shard_map/reduce_scatter | solution.py:413
  302.8 18.7 %collective-permute-start.42 = (bf16[2,64,1792]{2,1,0:T(8,128)(2,1)S(1)}, bf16[2,64,1792]{2,1,0:T(8,128)(2,1)S(1)}, u32[]{:S(2)}, u32[]{:S(2)}) collective-permute-start(bf16[2,64,1792]{2,1,0:T(8,128)(2,1)S(1)} %get-tuple-element.289.x0), channel_id=1, source_target_pairs={{0,24},{8,16},{16,8},{24,0},{1,25},{9,17},{17,9},{25,1},{2,26},{10... | collective-permute-start | bytes 1376264 | tf_op jit(solution)/shard_map/ppermute | solution.py:23
  326.3 15.3 %collective-permute-start.47 = (bf16[4,56,1792]{2,1,0:T(8,128)(2,1)}, bf16[4,56,1792]{2,1,0:T(8,128)(2,1)}, u32[]{:S(2)}, u32[]{:S(2)}) collective-permute-start(bf16[4,56,1792]{2,1,0:T(8,128)(2,1)} %slice_bitcast_fusion.3), channel_id=1, source_target_pairs={{0,1},{1,0},{2,3},{3,2},{4,5},{5,4},{6,7},{7,6},{8,9},{9,8},{10,11... | collective-permute-start | bytes 2408456 | tf_op jit(solution)/shard_map/ppermute | solution.py:23
  343.2 16.2 %collective-permute-start.48 = (bf16[56,1792]{1,0:T(8,128)(2,1)S(1)}, bf16[56,1792]{1,0:T(8,128)(2,1)S(1)}, u32[]{:S(2)}, u32[]{:S(2)}) collective-permute-start(bf16[56,1792]{1,0:T(8,128)(2,1)S(1)} %get-tuple-element.401), channel_id=1, source_target_pairs={{0,2},{2,0},{4,6},{6,4},{1,3},{3,1},{5,7},{7,5},{8,10},{10,8},{12,... | collective-permute-start | bytes 602120 | tf_op jit(solution)/shard_map/ppermute | solution.py:23
  343.3 17.0 %collective-permute-start.49 = (bf16[56,1792]{1,0:T(8,128)(2,1)S(1)}, bf16[56,1792]{1,0:T(8,128)(2,1)S(1)}, u32[]{:S(2)}, u32[]{:S(2)}) collective-permute-start(bf16[56,1792]{1,0:T(8,128)(2,1)S(1)} %get-tuple-element.400), channel_id=1, source_target_pairs={{0,4},{2,6},{4,0},{6,2},{1,5},{3,7},{5,1},{7,3},{8,12},{10,14},{12... | collective-permute-start | bytes 602120 | tf_op jit(solution)/shard_map/ppermute | solution.py:23
  346.3 17.6 %collective-permute-start.50 = (bf16[56,1792]{1,0:T(8,128)(2,1)S(1)}, bf16[56,1792]{1,0:T(8,128)(2,1)S(1)}, u32[]{:S(2)}, u32[]{:S(2)}) collective-permute-start(bf16[56,1792]{1,0:T(8,128)(2,1)S(1)} %get-tuple-element.399), channel_id=1, source_target_pairs={{0,6},{2,4},{4,2},{6,0},{1,7},{3,5},{5,3},{7,1},{8,14},{10,12},{12... | collective-permute-start | bytes 602120 | tf_op jit(solution)/shard_map/ppermute | solution.py:23
  394.6 22.1 %collective-permute-start.58 = (bf16[2,64,1792]{2,1,0:T(8,128)(2,1)}, bf16[2,64,1792]{2,1,0:T(8,128)(2,1)S(1)}, u32[]{:S(2)}, u32[]{:S(2)}) collective-permute-start(bf16[2,64,1792]{2,1,0:T(8,128)(2,1)} %get-tuple-element.325), channel_id=1, source_target_pairs={{0,8},{8,0},{16,24},{24,16},{1,9},{9,1},{17,25},{25,17},{2,10},{10... | collective-permute-start | bytes 1376264 | tf_op jit(solution)/shard_map/ppermute | solution.py:23
  395.6 22.5 %collective-permute-start.59 = (bf16[2,64,1792]{2,1,0:T(8,128)(2,1)}, bf16[2,64,1792]{2,1,0:T(8,128)(2,1)S(1)}, u32[]{:S(2)}, u32[]{:S(2)}) collective-permute-start(bf16[2,64,1792]{2,1,0:T(8,128)(2,1)} %get-tuple-element.326), channel_id=1, source_target_pairs={{0,16},{8,24},{16,0},{24,8},{1,17},{9,25},{17,1},{25,9},{2,18},{10... | collective-permute-start | bytes 1376264 | tf_op jit(solution)/shard_map/ppermute | solution.py:23
  397.0 14.8 %collective-permute-start.57 = (bf16[56,2432]{1,0:T(8,128)(2,1)}, bf16[56,2432]{1,0:T(8,128)(2,1)S(1)}, u32[]{:S(2)}, u32[]{:S(2)}) collective-permute-start(bf16[56,2432]{1,0:T(8,128)(2,1)} %get-tuple-element.324), channel_id=1, source_target_pairs={{0,4},{2,6},{4,0},{6,2},{1,5},{3,7},{5,1},{7,3},{8,12},{10,14},{12... | collective-permute-start | bytes 817160 | tf_op jit(solution)/shard_map/ppermute | solution.py:23
  398.0 13.8 %collective-permute-start.56 = (bf16[4,56,576]{2,1,0:T(8,128)(2,1)S(1)}, bf16[4,56,576]{2,1,0:T(8,128)(2,1)S(1)}, u32[]{:S(2)}, u32[]{:S(2)}) collective-permute-start(bf16[4,56,576]{2,1,0:T(8,128)(2,1)S(1)} %get-tuple-element.323), channel_id=1, source_target_pairs={{0,2},{2,0},{4,6},{6,4},{1,3},{3,1},{5,7},{7,5},{8,10},{10,8},{12,... | collective-permute-start | bytes 774152 | tf_op jit(solution)/shard_map/ppermute | solution.py:23
  420.0 21.7 %collective-permute-start.62 = (bf16[2,64,1792]{2,1,0:T(8,128)(2,1)}, bf16[2,64,1792]{2,1,0:T(8,128)(2,1)S(1)}, u32[]{:S(2)}, u32[]{:S(2)}) collective-permute-start(bf16[2,64,1792]{2,1,0:T(8,128)(2,1)} %get-tuple-element.332), channel_id=1, source_target_pairs={{0,24},{8,16},{16,8},{24,0},{1,25},{9,17},{17,9},{25,1},{2,26},{10... | collective-permute-start | bytes 1376264 | tf_op jit(solution)/shard_map/ppermute | solution.py:23
  422.1 16.9 %collective-permute-start.61 = (bf16[4,56,576]{2,1,0:T(8,128)(2,1)S(1)}, bf16[4,56,576]{2,1,0:T(8,128)(2,1)S(1)}, u32[]{:S(2)}, u32[]{:S(2)}) collective-permute-start(bf16[4,56,576]{2,1,0:T(8,128)(2,1)S(1)} %fusion.33), channel_id=1, source_target_pairs={{0,4},{2,6},{4,0},{6,2},{1,5},{3,7},{5,1},{7,3},{8,12},{10,14},{12... | collective-permute-start | bytes 774152 | tf_op jit(solution)/shard_map/ppermute | solution.py:23
  425.1 16.5 %collective-permute-start.63 = (bf16[56,2432]{1,0:T(8,128)(2,1)}, bf16[56,2432]{1,0:T(8,128)(2,1)S(1)}, u32[]{:S(2)}, u32[]{:S(2)}) collective-permute-start(bf16[56,2432]{1,0:T(8,128)(2,1)} %get-tuple-element.333), channel_id=1, source_target_pairs={{0,2},{2,0},{4,6},{6,4},{1,3},{3,1},{5,7},{7,5},{8,10},{10,8},{12,... | collective-permute-start | bytes 817160 | tf_op jit(solution)/shard_map/ppermute | solution.py:23
  (128 other events, 1461.7 us)
Sparse Core Ops, SparseCore 0:
  9.9 56.8 all-gather.7
  69.8 56.1 all-gather.9
  231.6 57.5 all-gather.5
  295.9 73.6 reduce-scatter.2
  373.0 71.9 reduce-scatter.4

commit v2 on v1

--- a/solution.py
+++ b/solution.py
@@ -71,11 +71,12 @@
     return [(blocks[1], LINE, 1), (far, LINE, 2)]
 
 
-def exchange(pieces, far_moves=(), far_beside=()):
-    got, _ = window([(pieces[k], "c", k) for k in range(1, pieces.shape[0])])
+def exchange(pieces, far_moves=(), far_beside=(), near_beside=()):
+    got, near_beside = window([(pieces[k], "c", k) for k in range(1, pieces.shape[0])], near_beside)
     near = jnp.stack([pieces[0]] + got, axis=1)
+    far_moves = far_moves(*near_beside) if callable(far_moves) else far_moves
     got, far_beside = window([(near[o], LINE, o) for o in range(1, 4)] + list(far_moves), far_beside)
-    return [near[0]] + got[:3], got[3:], far_beside
+    return [near[0]] + got[:3], got[3:], far_beside + near_beside
 
 
 def in_place(got, me):
@@ -116,16 +117,23 @@
     return ((b ^ (sub * cps + lane // slot)) * slot) + lane % slot
 
 
-def flip(x):
-    return jnp.transpose(x.astype(f32)).astype(bf16)
-
-
-def kernel_sum(score):
-    lifted = score + 4.0
-    return lifted * lifted * (1.0 / 32.0) + 0.5
-
-
-def fwd_kernel(nh, nb, slot, sb, ids, got0, got1, got2, got3, tiles, res, out, vrow):
+def flip(x, factor=1.0):
+    return jnp.transpose(x.astype(f32) * factor).astype(bf16)
+
+
+def lifted(qrow, kcol):
+    return dot(qrow, kcol, 1, 0) + 1.0
+
+
+def repeat(lo, hi, step, value):
+    if hi - lo <= 4:
+        for i in range(lo, hi):
+            value = step(i, value)
+        return value
+    return lax.fori_loop(lo, hi, step, value)
+
+
+def fwd_kernel(nh, nb, slot, sb, ids, got0, got1, got2, got3, tiles, res, out, vrow, back):
     got, cores = (got0, got1, got2, got3), nb // 4
     nsub, cps = nb * slot // sb, sb // slot
     h, b = ids[0], ids[1]
@@ -141,35 +149,35 @@
         vrow[i] = jnp.transpose(vv).astype(bf16)
         return c
 
-    lax.fori_loop(0, nh * nsub, rows_of, 0)
-
-    for oh in range(nh):
-        hq = h ^ oh
+    repeat(0, nh * nsub, rows_of, 0)
+
+    for hq in range(nh):
         for sub in range(nsub):
             iq = hq * nsub + sub
-            qrow = flip(tiles[iq, 0:16, :])
+            qrow = flip(tiles[iq, 0:16, :], 0.25)
             pos_q = positions(b, sub, cps, slot, 0, sb)
 
             def step(ik, acc, masked):
-                w = kernel_sum(dot(qrow, tiles[ik, 16:32, :], 1, 0))
+                u = lifted(qrow, tiles[ik, 16:32, :])
+                w = u * u + 1.0
                 if masked:
                     pos_k = positions(b, ik - hq * nsub, cps, slot, 1, sb)
                     w = jnp.where(pos_q >= pos_k, w, 0.0)
                 return acc + dot(w.astype(bf16), vrow[ik], 1, 0)
 
-            acc = lax.fori_loop(
-                0, hq * nsub, functools.partial(step, masked=False), jnp.zeros((sb, 128), f32)
-            )
-            acc = lax.fori_loop(hq * nsub, (hq + 1) * nsub, functools.partial(step, masked=True), acc)
+            acc = jnp.zeros((sb, 128), f32)
+            acc = repeat(0, hq * nsub, functools.partial(step, masked=False), acc)
+            acc = repeat(hq * nsub, (hq + 1) * nsub, functools.partial(step, masked=True), acc)
             den = acc[:, 112:113]
             mixed = acc / den
             lane = lax.broadcasted_iota(jnp.int32, (sb, 128), 1)
             res[iq] = jnp.where(lane == 112, den, mixed)
-            back = jnp.transpose(mixed)[0:112].astype(bf16)
-            for c in range(cps):
-                o = sub * cps + c
-                piece = back[:, c * slot : (c + 1) * slot]
-                out[o % cores, o // cores, :, oh * slot : (oh + 1) * slot] = piece
+            back[iq] = jnp.transpose(mixed)[0:112].astype(bf16)
+    for oh in range(nh):
+        for o in range(nb):
+            lo = (o % cps) * slot
+            piece = back[(h ^ oh) * nsub + o // cps, :, lo : lo + slot]
+            out[o % cores, o // cores, :, oh * slot : (oh + 1) * slot] = piece
 
 
 def bwd_kernel(nh, nb, slot, sb, ids, tiles, res, got0, got1, got2, got3, out, gt, krow, acc):
@@ -188,27 +196,26 @@
         acc[i] = jnp.zeros((144, sb), f32)
         return c
 
-    lax.fori_loop(0, nh * nsub, rows_of, 0)
-
-    for oh in range(nh):
-        hq = h ^ oh
+    repeat(0, nh * nsub, rows_of, 0)
+
+    for hq in range(nh):
         for sub in range(nsub):
             iq = hq * nsub + sub
             qcol = tiles[iq, 0:16, :]
-            qrow = flip(qcol)
+            qrow = flip(qcol, 0.25)
             gcol = gt[iq]
             grow = jnp.transpose(gcol.astype(f32))
             kept = res[iq]
             rden = 1.0 / kept[:, 112:113]
+            rquarter = rden * 0.5
             delta = jnp.sum(grow * kept[:, 0:112], axis=1, keepdims=True)
             grow = grow.astype(bf16)
             pos_q = positions(b, sub, cps, slot, 0, sb)
 
             def step(ik, dq, masked):
-                lifted = dot(qrow, tiles[ik, 16:32, :], 1, 0) + 4.0
-                g = (dot(grow, tiles[ik, 32:144, :], 1, 0) - delta) * rden
-                p = (lifted * lifted * (1.0 / 32.0) + 0.5) * rden
-                ds = g * lifted * (1.0 / 16.0)
+                u = lifted(qrow, tiles[ik, 16:32, :])
+                p = (u * u + 1.0) * rden
+                ds = (dot(grow, tiles[ik, 32:144, :], 1, 0) - delta) * rquarter * u
                 if masked:
                     pos_k = positions(b, ik - hq * nsub, cps, slot, 1, sb)
                     keep = pos_q >= pos_k
@@ -219,10 +226,9 @@
                 acc[ik, 16:32, :] += dot(qcol, ds, 1, 0)
                 return dq + dot(ds, krow[ik], 1, 0)
 
-            dq = lax.fori_loop(
-                0, hq * nsub, functools.partial(step, masked=False), jnp.zeros((sb, 16), f32)
-            )
-            dq = lax.fori_loop(hq * nsub, (hq + 1) * nsub, functools.partial(step, masked=True), dq)
+            dq = jnp.zeros((sb, 16), f32)
+            dq = repeat(0, hq * nsub, functools.partial(step, masked=False), dq)
+            dq = repeat(hq * nsub, (hq + 1) * nsub, functools.partial(step, masked=True), dq)
             acc[iq, 0:16, :] = jnp.transpose(dq)
     for oh in range(nh):
         for o in range(nb):
@@ -361,7 +367,7 @@
     total[...] = sums[0] + sums[1] + sums[2]
 
 
-def call(body, ids, arrays, outs, scratch, room=6):
+def call(body, ids, arrays, outs, scratch, room=12):
     vmem = pl.BlockSpec(memory_space=pltpu.VMEM)
     held = list(arrays) + jax.tree.leaves(outs) + list(scratch)
     held = sum(math.prod(x.shape[:-1]) * max(x.shape[-1], 128) * x.dtype.itemsize for x in held)
@@ -461,7 +467,7 @@
         attn_rows + [qkv_w],
         piece(pw),
         held(pw),
-        room=10,
+        room=36,
     )
     sent, _, (down_w, w_out_late) = exchange(pieces, far_beside=(gathered(w_down), w_out))
     down_w = down_w.reshape(-1, width)
@@ -475,11 +481,14 @@
             jax.ShapeDtypeStruct((n, sb, 128), f32),
             piece(vw),
         ],
-        [pltpu.VMEM((n, sb, 128), bf16)],
-        room=14,
-    )
-    mixed_out, out_near, out_far = tie(mixed_out, out_near, out_far)
-    mixed_got, (out_last,), _ = exchange(mixed_out, far_moves=[(out_far, LINE, 1)])
+        [pltpu.VMEM((n, sb, 128), bf16), pltpu.VMEM((n, vw, sb), bf16)],
+        room=36,
+    )
+    mixed_got, (out_last,), (out_near, out_far) = exchange(
+        mixed_out,
+        far_moves=lambda near, far: [(far, LINE, 1)],
+        near_beside=(out_near, out_far),
+    )
     out_w = line_whole([w_out, out_near, out_far, out_last])
     got, (out_w,) = window(over(out_w, "c"), (out_w,))
     out_w = core_end(out_w, got).reshape(-1, width)
@@ -489,7 +498,7 @@
         mixed_got + [out_w],
         [jax.ShapeDtypeStruct((hd * vw, seqs * lanes), bf16), own_part, sent_part],
         taken(vw),
-        room=10,
+        room=36,
     )
     got, (ffn_w,) = window([(attn_part[o - 1], HEAD, o) for o in range(1, 4)], (ffn_w,))
     residual = tokens_f + plus(attn_own, got)
@@ -562,14 +571,14 @@
         [own_rows] + got + [out_w, mixed],
         [piece(vw), jax.ShapeDtypeStruct((cores, 4, drow, width), bf16)],
         held(vw),
-        room=10,
+        room=36,
     )
     sent, out_got, _ = exchange(
         sent, far_moves=[(grad_out_w[k], "c", k) for k in range(1, cores)]
     )
     grad_out_w = plus(grad_out_w[0], out_got).astype(bf16)
     sent, grad_out_w = tie(sent, grad_out_w)
-    out_got = [swap(grad_out_w[o], LINE, o) for o in range(1, 4)]
+    out_got = [swap(grad_out_w[o], LINE, o) for o in range(1, 3)]
     grads_out = call(
         functools.partial(bwd_kernel, *geometry),
         ids,
@@ -580,7 +589,7 @@
             pltpu.VMEM((n, sb, fw), bf16),
             pltpu.VMEM((n, pw, sb), f32),
         ],
-        room=14,
+        room=36,
     )
     grads_out, out_got = tie(grads_out, out_got)
     grad_qkv, _, (grad_ffn_w,) = exchange(grads_out, far_beside=(grad_ffn_w,))
@@ -590,7 +599,7 @@
         grad_qkv + attn_rows + [qkv_w],
         [jax.ShapeDtypeStruct((cores, 4, nh, drow, hd * pw), bf16), own_part, sent_part],
         taken(pw) + [pltpu.VMEM((hd * pw, seqs * lanes), bf16)],
-        room=14,
+        room=36,
     )
     grad_qkv_w, grad_ffn_w = tie(grad_qkv_w, grad_ffn_w)
     grad_ffn_w = grad_ffn_w.reshape(4, drow, -1)
@@ -598,9 +607,10 @@
     row_moves = [(attn_back[o - 1], HEAD, o) for o in range(1, 4)]
     got, _ = window([(grad_qkv_w[k], "c", k) for k in range(1, cores)])
     grad_qkv_w = plus(grad_qkv_w[0], got).astype(bf16)
-    (passing, ffn_2, *row_got), _ = window(
-        [by_way(grad_qkv_w), (ffn_pieces[2], LINE, 2)] + row_moves[:2]
-    )
+    (passing, ffn_2, out_last, *row_got), _ = window(
+        [by_way(grad_qkv_w), (ffn_pieces[2], LINE, 2), (grad_out_w[3], LINE, 3)] + row_moves[:2]
+    )
+    out_got = out_got + [out_last]
     (got_1, got_2, last, ffn_1), _ = window(
         rest_moves(grad_qkv_w, passing) + [row_moves[2], (ffn_pieces[1], LINE, 1)]
     )

time: 479 us -> 459 us (0.958)
  the two profiles are of different devices: /device:TPU:8 before, /device:TPU:0 now
where the time goes in v2:
time: 459 us; the launch traced here: 453 us
  waiting for transfers between devices  208 us (45%)
  starting transfers between devices  75.6 us (16%)
  matrix products  49.1 us (11%)
  local copies, waits for them, and re-layouts  38.7 us (8%)
  other arithmetic  34.9 us (8%)
  Pallas kernels  29.6 us (6%)
  between operations  17.7 us (4%)
    ppermute x68, waiting for transfers between devices, swap(): return lax.ppermute(x, axis, [(i, i ^ o) for i in range(n)])  207 us
    ppermute x68, starting transfers between devices, swap(): return lax.ppermute(x, axis, [(i, i ^ o) for i in range(n)])  74.8 us
    dot_general x14, matrix products, dot(): lax.dot_general(a, b, (((ca,), (cb,)), ((), ())), preferred_element_type=...  49.1 us
    pallas_call x9, Pallas kernels, call(): pl.pallas_call(body, out_shape=outs, in_specs=[pl.BlockSpec(memory_space=...  29.6 us
    unnamed x138, local copies, waits for them, and re-layouts  9.2 us
  transfers between devices with their start and end apart: 73, of which 42 were waited for; matrix products, arithmetic and copies ran while one was open for 23% of the time, Pallas kernels for 6%

profile of v2, /device:TPU:0, one launch (start us, length us, event | category | flops | bytes accessed | tf_op | source)
XLA Modules:
  0.0 453.3 jit_solution(9469506176841094678)
XLA Ops:
  41.2 7.4 %collective-permute-done.7 = bf16[4,56,576]{2,1,0:T(8,128)(2,1)S(1)} collective-permute-done((bf16[4,56,576]{2,1,0:T(8,128)(2,1)S(1)}, bf16[4,56,576]{2,1,0:T(8,128)(2,1)S(1)}, u32[]{:S(2)}, u32[]{:S(2)}) %collective-permute-start.7) | collective-permute-done | bytes 258080 | tf_op jit(solution)/shard_map/ppermute | solution.py:23
  48.6 3.7 collective-permute-done.8
  55.3 5.6 %collective-permute-done.6.x2 = bf16[2,64,1792]{2,1,0:T(8,128)(2,1)S(1)} collective-permute-done((bf16[2,64,1792]{2,1,0:T(8,128)(2,1)S(1)}, bf16[2,64,1792]{2,1,0:T(8,128)(2,1)S(1)}, u32[]{:S(2)}, u32[]{:S(2)}) %collective-permute-start.6) | collective-permute-done | bytes 458784 | tf_op jit(solution)/shard_map/ppermute | solution.py:23
  62.1 8.4 %collective-permute-done.10 = bf16[4,56,576]{2,1,0:T(8,128)(2,1)S(1)} collective-permute-done((bf16[4,56,576]{2,1,0:T(8,128)(2,1)S(1)}, bf16[4,56,576]{2,1,0:T(8,128)(2,1)S(1)}, u32[]{:S(2)}, u32[]{:S(2)}) %collective-permute-start.10) | collective-permute-done | bytes 258080 | tf_op jit(solution)/shard_map/ppermute | solution.py:23
  88.3 8.1 %collective-permute-done.15.got2 = bf16[2,144,256]{2,1,0:T(8,128)(2,1)S(1)} collective-permute-done((bf16[2,144,256]{2,1,0:T(8,128)(2,1)S(1)}, bf16[2,144,256]{2,1,0:T(8,128)(2,1)S(1)}, u32[]{:S(2)}, u32[]{:S(2)}) %collective-permute-start.15) | collective-permute-done | bytes 147488 | tf_op jit(solution)/shard_map/ppermute | solution.py:23
  99.2 4.8 %shard_map.222 = (bf16[4,144,512]{2,1,0:T(8,128)(2,1)S(1)}, f32[4,512,128]{2,1,0:T(8,128)S(1)}, bf16[2,4,112,256]{3,2,1,0:T(8,128)(2,1)S(1)}) custom-call(s32[3]{0:T(128)S(1)} %pad_add_fusion.ids, bf16[2,144,256]{2,1,0:T(8,128)(2,1)S(1)} %get-tuple-element.411.got0, bf16[2,144,256]{2,1,0:T(8,128)(2,1)S(1)} %collective-permute-done.14.got1, ...), custom_call_target="tpu_custom_call" | custom-call | tf_op jit(solution)/shard_map/pallas_call | solution.py:374
  106.3 4.0 collective-permute-done.19
  115.0 8.4 %collective-permute-done.20.g1 = bf16[2,112,256]{2,1,0:T(8,128)(2,1)S(1)} collective-permute-done((bf16[2,112,256]{2,1,0:T(8,128)(2,1)S(1)}, bf16[2,112,256]{2,1,0:T(8,128)(2,1)S(1)}, u32[]{:S(2)}, u32[]{:S(2)}) %collective-permute-start.20) | collective-permute-done | bytes 114720 | tf_op jit(solution)/shard_map/ppermute | solution.py:23
  135.2 7.6 %copy.66 = bf16[4,4,2,56,2432]{4,3,2,1,0:T(8,128)(2,1)} copy(bf16[4,4,2,56,2432]{4,3,1,2,0:T(8,128)(2,1)} %bitcast.284) | data formatting | bytes 17432576 | tf_op jit(solution)/shard_map/transpose | solution.py:456
  143.9 10.9 %collective-permute-done.26 = bf16[2,64,1792]{2,1,0:T(8,128)(2,1)} collective-permute-done((bf16[2,64,1792]{2,1,0:T(8,128)(2,1)}, bf16[2,64,1792]{2,1,0:T(8,128)(2,1)}, u32[]{:S(2)}, u32[]{:S(2)}) %collective-permute-start.26) | collective-permute-done | bytes 458784 | tf_op jit(solution)/shard_map/ppermute | solution.py:23
  159.7 5.0 %fusion.70 = f32[128,2432]{1,0:T(8,128)S(1)} fusion(bf16[128,1792]{1,0:T(8,128)(2,1)S(1)} %bitcast.288, bf16[1792,2432]{1,0:T(8,128)(2,1)} %bitcast.266), kind=kOutput, calls=%fused_computation.211 | convolution fusion | flops 1115684864 | bytes 10420224 | tf_op jit(solution)/shard_map/dot_general | solution.py:18
  167.1 9.9 %collective-permute-done.28 = bf16[2,64,1792]{2,1,0:T(8,128)(2,1)S(1)} collective-permute-done((bf16[2,64,1792]{2,1,0:T(8,128)(2,1)S(1)}, bf16[2,64,1792]{2,1,0:T(8,128)(2,1)S(1)}, u32[]{:S(2)}, u32[]{:S(2)}) %collective-permute-start.28) | collective-permute-done | bytes 458784 | tf_op jit(solution)/shard_map/ppermute | solution.py:23
  192.6 15.2 %collective-permute-done.31 = bf16[2,64,1792]{2,1,0:T(8,128)(2,1)S(1)} collective-permute-done((bf16[2,64,1792]{2,1,0:T(8,128)(2,1)S(1)}, bf16[2,64,1792]{2,1,0:T(8,128)(2,1)S(1)}, u32[]{:S(2)}, u32[]{:S(2)}) %collective-permute-start.31) | collective-permute-done | bytes 458784 | tf_op jit(solution)/shard_map/ppermute | solution.py:23
  210.7 8.2 %collective-permute-done.32 = bf16[2,64,1792]{2,1,0:T(8,128)(2,1)S(1)} collective-permute-done((bf16[2,64,1792]{2,1,0:T(8,128)(2,1)S(1)}, bf16[2,64,1792]{2,1,0:T(8,128)(2,1)S(1)}, u32[]{:S(2)}, u32[]{:S(2)}) %collective-permute-start.32) | collective-permute-done | bytes 458784 | tf_op jit(solution)/shard_map/ppermute | solution.py:23
  218.9 6.2 %collective-permute-done.33 = bf16[2,64,1792]{2,1,0:T(8,128)(2,1)S(1)} collective-permute-done((bf16[2,64,1792]{2,1,0:T(8,128)(2,1)S(1)}, bf16[2,64,1792]{2,1,0:T(8,128)(2,1)S(1)}, u32[]{:S(2)}, u32[]{:S(2)}) %collective-permute-start.33) | collective-permute-done | bytes 458784 | tf_op jit(solution)/shard_map/ppermute | solution.py:23
  230.0 4.0 fusion.73
  234.5 7.1 %fusion.74 = f32[128,1792]{1,0:T(8,128)} fusion(bf16[128,2432]{1,0:T(8,128)(2,1)S(1)} %pad_maximum_fusion.4, bf16[1792,2432]{1,0:T(8,128)(2,1)} %bitcast.267), kind=kOutput, calls=%fused_computation.215 | convolution fusion | flops 1115684864 | bytes 10256384 | tf_op jit(solution)/shard_map/dot_general | solution.py:18
  262.4 5.8 %convolution_convert_fusion.1 = bf16[1216,1792]{1,0:T(8,128)(2,1)} fusion(bf16[512,1216]{1,0:T(8,128)(2,1)S(1)} %copy-done.46, bf16[128,1792]{1,0:T(8,128)(2,1)S(1)} %bitcast.309, bf16[128,1792]{1,0:T(8,128)(2,1)} %bitcast.77, bf16[128,1792]{1,0:T(8,128)(2,1)} %bitcast.76, bf16[128,1792]{1,0:T(8,128)(2,1)} %bitcast.73), kind=kOutput, calls=%fused_computation.1 | convolution fusion | flops 2240888832 | bytes 7438336 | tf_op jit(solution)/shard_map/dot_general | solution.py:18
  275.1 10.9 %convolution_convert_fusion = bf16[1792,2432]{1,0:T(8,128)(2,1)} fusion(bf16[512,1792]{1,0:T(8,128)(2,1)} %pad_maximum_fusion.1, bf16[512,2432]{1,0:T(8,128)(2,1)} %pad_maximum_fusion), kind=kOutput, calls=%fused_computation | convolution fusion | flops 4467097600 | bytes 13041664 | tf_op jit(solution)/shard_map/dot_general | solution.py:18
  286.0 7.5 %copy.73 = bf16[4,4,2,56,2432]{4,3,1,2,0:T(8,128)(2,1)} copy(bf16[4,4,2,56,2432]{4,3,2,1,0:T(8,128)(2,1)} %bitcast.285) | data formatting | bytes 17432576 | tf_op jit(solution)/shard_map/reshape | solution.py:560
  302.8 10.0 %collective-permute-done.40.x1 = bf16[2,64,1792]{2,1,0:T(8,128)(2,1)S(1)} collective-permute-done((bf16[2,64,1792]{2,1,0:T(8,128)(2,1)S(1)}, bf16[2,64,1792]{2,1,0:T(8,128)(2,1)S(1)}, u32[]{:S(2)}, u32[]{:S(2)}) %collective-permute-start.40) | collective-permute-done | bytes 458784 | tf_op jit(solution)/shard_map/ppermute | solution.py:23
  312.7 8.6 %collective-permute-done.42.x3 = bf16[2,64,1792]{2,1,0:T(8,128)(2,1)S(1)} collective-permute-done((bf16[2,64,1792]{2,1,0:T(8,128)(2,1)S(1)}, bf16[2,64,1792]{2,1,0:T(8,128)(2,1)S(1)}, u32[]{:S(2)}, u32[]{:S(2)}) %collective-permute-start.42) | collective-permute-done | bytes 458784 | tf_op jit(solution)/shard_map/ppermute | solution.py:23
  326.0 4.2 collective-permute-start.45
  331.1 8.0 %collective-permute-done.45.got2 = bf16[2,112,256]{2,1,0:T(8,128)(2,1)S(1)} collective-permute-done((bf16[2,112,256]{2,1,0:T(8,128)(2,1)S(1)}, bf16[2,112,256]{2,1,0:T(8,128)(2,1)S(1)}, u32[]{:S(2)}, u32[]{:S(2)}) %collective-permute-start.45) | collective-permute-done | bytes 114720 | tf_op jit(solution)/shard_map/ppermute | solution.py:23
  344.7 8.3 %shard_map.225 = bf16[2,4,144,256]{3,2,1,0:T(8,128)(2,1)S(1)} custom-call(s32[3]{0:T(128)S(1)} %pad_add_fusion.ids, bf16[4,144,512]{2,1,0:T(8,128)(2,1)S(1)} %copy-done.20, f32[4,512,128]{2,1,0:T(8,128)S(1)} %copy-done.14, bf16[2,112,256]{2,1,0:T(8,128)(2,1)S(1)} %get-tuple-element.305.got0, bf16[2,112,256]{2,1,0:T(8,128)(2,1)S(1)} %collective-permute-done.44.got1, ...), custom_call_target="tpu_custom_call" | custom-call | tf_op jit(solution)/shard_map/pallas_call | solution.py:374
  361.5 4.0 collective-permute-done.51.g1
  365.4 6.0 %collective-permute-done.52.g2 = bf16[2,144,256]{2,1,0:T(8,128)(2,1)S(1)} collective-permute-done((bf16[2,144,256]{2,1,0:T(8,128)(2,1)S(1)}, bf16[2,144,256]{2,1,0:T(8,128)(2,1)S(1)}, u32[]{:S(2)}, u32[]{:S(2)}) %collective-permute-start.52) | collective-permute-done | bytes 147488 | tf_op jit(solution)/shard_map/ppermute | solution.py:23
  371.4 5.0 %shard_map.226 = (bf16[2,4,4,56,576]{4,3,2,1,0:T(8,128)(2,1)S(1)}, f32[2,64,1792]{2,1,0:T(8,128)S(1)}, bf16[3,2,64,1792]{3,2,1,0:T(8,128)(2,1)S(1)}) custom-call(s32[3]{0:T(128)S(1)} %pad_add_fusion.ids, bf16[2,144,256]{2,1,0:T(8,128)(2,1)S(1)} %get-tuple-element.405.g0, bf16[2,144,256]{2,1,0:T(8,128)(2,1)S(1)} %collective-permute-done.51.g1, ...), custom_call_target="tpu_custom_call" | custom-call | tf_op jit(solution)/shard_map/pallas_call | solution.py:374
  382.6 3.6 collective-permute-start.56
  389.8 14.4 %collective-permute-done.57 = bf16[56,1792]{1,0:T(8,128)(2,1)} collective-permute-done((bf16[56,1792]{1,0:T(8,128)(2,1)}, bf16[56,1792]{1,0:T(8,128)(2,1)}, u32[]{:S(2)}, u32[]{:S(2)}) %collective-permute-start.57) | collective-permute-done | bytes 200736 | tf_op jit(solution)/shard_map/ppermute | solution.py:23
  415.0 10.0 %collective-permute-done.60 = bf16[4,56,576]{2,1,0:T(8,128)(2,1)S(1)} collective-permute-done((bf16[4,56,576]{2,1,0:T(8,128)(2,1)}, bf16[4,56,576]{2,1,0:T(8,128)(2,1)S(1)}, u32[]{:S(2)}, u32[]{:S(2)}) %collective-permute-start.60) | collective-permute-done | bytes 258080 | tf_op jit(solution)/shard_map/ppermute | solution.py:23
  425.0 3.7 collective-permute-done.63.p1
  (373 shorter events, 201.1 us)
Async XLA Ops:
  7.2 89.3 %all-gather.8.cloned.1.call-start = ((), (), s32[]{:S(2)}) async-start(), calls=%async_computation.5 | async-start | bytes 4902912 | tf_op jit(solution)/shard_map/all_gather | solution.py:416
  7.9 127.3 %all-gather.10.cloned.1.call-start = ((), (), s32[]{:S(2)}) async-start(), calls=%async_computation.6 | async-start | bytes 9805824 | tf_op jit(solution)/shard_map/all_gather | solution.py:416
  15.2 15.9 %collective-permute-start.3 = (bf16[56,2432]{1,0:T(8,128)(2,1)S(1)}, bf16[56,2432]{1,0:T(8,128)(2,1)S(1)}, u32[]{:S(2)}, u32[]{:S(2)}) collective-permute-start(bf16[56,2432]{1,0:T(8,128)(2,1)S(1)} %get-tuple-element.193), channel_id=1, source_target_pairs={{0,2},{2,0},{4,6},{6,4},{1,3},{3,1},{5,7},{7,5},{8,10},{10,8},{12,... | collective-permute-start | bytes 817160 | tf_op jit(solution)/shard_map/ppermute | solution.py:23
  18.2 14.8 %collective-permute-start.4 = (bf16[56,2432]{1,0:T(8,128)(2,1)S(1)}, bf16[56,2432]{1,0:T(8,128)(2,1)S(1)}, u32[]{:S(2)}, u32[]{:S(2)}) collective-permute-start(bf16[56,2432]{1,0:T(8,128)(2,1)S(1)} %get-tuple-element.194), channel_id=1, source_target_pairs={{0,4},{2,6},{4,0},{6,2},{1,5},{3,7},{5,1},{7,3},{8,12},{10,14},{12... | collective-permute-start | bytes 817160 | tf_op jit(solution)/shard_map/ppermute | solution.py:23
  34.9 20.4 %collective-permute-start.5 = (bf16[2,64,1792]{2,1,0:T(8,128)(2,1)S(1)}, bf16[2,64,1792]{2,1,0:T(8,128)(2,1)S(1)}, u32[]{:S(2)}, u32[]{:S(2)}) collective-permute-start(bf16[2,64,1792]{2,1,0:T(8,128)(2,1)S(1)} %fusion.12.x0), channel_id=1, source_target_pairs={{0,8},{8,0},{16,24},{24,16},{1,9},{9,1},{17,25},{25,17},{2,10},{10... | collective-permute-start | bytes 1376264 | tf_op jit(solution)/shard_map/ppermute | solution.py:23
  36.4 24.5 %collective-permute-start.6 = (bf16[2,64,1792]{2,1,0:T(8,128)(2,1)S(1)}, bf16[2,64,1792]{2,1,0:T(8,128)(2,1)S(1)}, u32[]{:S(2)}, u32[]{:S(2)}) collective-permute-start(bf16[2,64,1792]{2,1,0:T(8,128)(2,1)S(1)} %fusion.12.x0), channel_id=1, source_target_pairs={{0,16},{8,24},{16,0},{24,8},{1,17},{9,25},{17,1},{25,9},{2,18},{10... | collective-permute-start | bytes 1376264 | tf_op jit(solution)/shard_map/ppermute | solution.py:23
  38.4 13.9 %collective-permute-start.8 = (bf16[4,56,576]{2,1,0:T(8,128)(2,1)S(1)}, bf16[4,56,576]{2,1,0:T(8,128)(2,1)S(1)}, u32[]{:S(2)}, u32[]{:S(2)}) collective-permute-start(bf16[4,56,576]{2,1,0:T(8,128)(2,1)S(1)} %bitcast_dynamic-update-slice_fusion.15), channel_id=1, source_target_pairs={{0,4},{2,6},{4,0},{6,2},{1,5},{3,7},{5,1},{7,3},{8,12},{10,14},{12... | collective-permute-start | bytes 774152 | tf_op jit(solution)/shard_map/ppermute | solution.py:23
  74.2 219.8 %all-gather.6.cloned.1.call-start = ((), (), s32[]{:S(2)}) async-start(), calls=%async_computation.2 | async-start | bytes 1081344 | tf_op jit(solution)/shard_map/all_gather | solution.py:527
  129.5 14.4 %collective-permute-start.25 = (bf16[2,64,1792]{2,1,0:T(8,128)(2,1)}, bf16[2,64,1792]{2,1,0:T(8,128)(2,1)S(1)}, u32[]{:S(2)}, u32[]{:S(2)}) collective-permute-start(bf16[2,64,1792]{2,1,0:T(8,128)(2,1)} %get-tuple-element.239), channel_id=1, source_target_pairs={{0,8},{8,0},{16,24},{24,16},{1,9},{9,1},{17,25},{25,17},{2,10},{10... | collective-permute-start | bytes 1376264 | tf_op jit(solution)/shard_map/ppermute | solution.py:23
  132.4 22.4 %collective-permute-start.26 = (bf16[2,64,1792]{2,1,0:T(8,128)(2,1)}, bf16[2,64,1792]{2,1,0:T(8,128)(2,1)}, u32[]{:S(2)}, u32[]{:S(2)}) collective-permute-start(bf16[2,64,1792]{2,1,0:T(8,128)(2,1)} %get-tuple-element.240), channel_id=1, source_target_pairs={{0,16},{8,24},{16,0},{24,8},{1,17},{9,25},{17,1},{25,9},{2,18},{10... | collective-permute-start | bytes 1376264 | tf_op jit(solution)/shard_map/ppermute | solution.py:23
  132.9 21.9 %collective-permute-start.27 = (bf16[2,64,1792]{2,1,0:T(8,128)(2,1)S(1)}, bf16[2,64,1792]{2,1,0:T(8,128)(2,1)}, u32[]{:S(2)}, u32[]{:S(2)}) collective-permute-start(bf16[2,64,1792]{2,1,0:T(8,128)(2,1)S(1)} %get-tuple-element.241), channel_id=1, source_target_pairs={{0,24},{8,16},{16,8},{24,0},{1,25},{9,17},{17,9},{25,1},{2,26},{10... | collective-permute-start | bytes 1376264 | tf_op jit(solution)/shard_map/ppermute | solution.py:23
  156.8 20.2 %collective-permute-start.28 = (bf16[2,64,1792]{2,1,0:T(8,128)(2,1)S(1)}, bf16[2,64,1792]{2,1,0:T(8,128)(2,1)S(1)}, u32[]{:S(2)}, u32[]{:S(2)}) collective-permute-start(bf16[2,64,1792]{2,1,0:T(8,128)(2,1)S(1)} %multiply_convert_fusion.3), channel_id=1, source_target_pairs={{0,2},{2,0},{4,6},{6,4},{1,3},{3,1},{5,7},{7,5},{8,10},{10,8},{12,... | collective-permute-start | bytes 1376264 | tf_op jit(solution)/shard_map/ppermute | solution.py:23
  158.1 22.2 %collective-permute-start.29 = (bf16[2,64,1792]{2,1,0:T(8,128)(2,1)S(1)}, bf16[2,64,1792]{2,1,0:T(8,128)(2,1)S(1)}, u32[]{:S(2)}, u32[]{:S(2)}) collective-permute-start(bf16[2,64,1792]{2,1,0:T(8,128)(2,1)S(1)} %multiply_convert_fusion.3), channel_id=1, source_target_pairs={{0,4},{2,6},{4,0},{6,2},{1,5},{3,7},{5,1},{7,3},{8,12},{10,14},{12... | collective-permute-start | bytes 1376264 | tf_op jit(solution)/shard_map/ppermute | solution.py:23
  191.9 15.8 %collective-permute-start.31 = (bf16[2,64,1792]{2,1,0:T(8,128)(2,1)S(1)}, bf16[2,64,1792]{2,1,0:T(8,128)(2,1)S(1)}, u32[]{:S(2)}, u32[]{:S(2)}) collective-permute-start(bf16[2,64,1792]{2,1,0:T(8,128)(2,1)S(1)} %convolution_convert_fusion.2), channel_id=1, source_target_pairs={{0,2},{2,0},{4,6},{6,4},{1,3},{3,1},{5,7},{7,5},{8,10},{10,8},{12,... | collective-permute-start | bytes 1376264 | tf_op jit(solution)/shard_map/ppermute | solution.py:23
  208.0 17.1 %collective-permute-start.33 = (bf16[2,64,1792]{2,1,0:T(8,128)(2,1)S(1)}, bf16[2,64,1792]{2,1,0:T(8,128)(2,1)S(1)}, u32[]{:S(2)}, u32[]{:S(2)}) collective-permute-start(bf16[2,64,1792]{2,1,0:T(8,128)(2,1)S(1)} %fusion.27), channel_id=1, source_target_pairs={{0,4},{2,6},{4,0},{6,2},{1,5},{3,7},{5,1},{7,3},{8,12},{10,14},{12... | collective-permute-start | bytes 1376264 | tf_op jit(solution)/shard_map/ppermute | solution.py:23
  228.1 15.8 %collective-permute-start.34 = (bf16[2,64,1792]{2,1,0:T(8,128)(2,1)}, bf16[2,64,1792]{2,1,0:T(8,128)(2,1)}, u32[]{:S(2)}, u32[]{:S(2)}) collective-permute-start(bf16[2,64,1792]{2,1,0:T(8,128)(2,1)} %fusion.67), channel_id=1, source_target_pairs={{0,2},{2,0},{4,6},{6,4},{1,3},{3,1},{5,7},{7,5},{8,10},{10,8},{12,... | collective-permute-start | bytes 1376264 | tf_op jit(solution)/shard_map/ppermute | solution.py:23
  228.1 17.2 %collective-permute-start.35 = (bf16[2,64,1792]{2,1,0:T(8,128)(2,1)}, bf16[2,64,1792]{2,1,0:T(8,128)(2,1)}, u32[]{:S(2)}, u32[]{:S(2)}) collective-permute-start(bf16[2,64,1792]{2,1,0:T(8,128)(2,1)} %fusion.67), channel_id=1, source_target_pairs={{0,4},{2,6},{4,0},{6,2},{1,5},{3,7},{5,1},{7,3},{8,12},{10,14},{12... | collective-permute-start | bytes 1376264 | tf_op jit(solution)/shard_map/ppermute | solution.py:23
  229.4 142.0 %reduce-scatter.3.cloned.1.call-start = ((), (), s32[]{:S(2)}) async-start(), calls=%async_computation.3 | async-start | bytes 9805824 | tf_op jit(solution)/shard_map/reduce_scatter | solution.py:419
  272.6 21.4 %collective-permute-start.38 = (bf16[2,64,1792]{2,1,0:T(8,128)(2,1)}, bf16[2,64,1792]{2,1,0:T(8,128)(2,1)}, u32[]{:S(2)}, u32[]{:S(2)}) collective-permute-start(bf16[2,64,1792]{2,1,0:T(8,128)(2,1)} %get-tuple-element.278), channel_id=1, source_target_pairs={{0,2},{2,0},{4,6},{6,4},{1,3},{3,1},{5,7},{7,5},{8,10},{10,8},{12,... | collective-permute-start | bytes 1376264 | tf_op jit(solution)/shard_map/ppermute | solution.py:23
  272.7 21.3 %collective-permute-start.39 = (bf16[2,64,1792]{2,1,0:T(8,128)(2,1)S(1)}, bf16[2,64,1792]{2,1,0:T(8,128)(2,1)}, u32[]{:S(2)}, u32[]{:S(2)}) collective-permute-start(bf16[2,64,1792]{2,1,0:T(8,128)(2,1)S(1)} %add_convert_fusion), channel_id=1, source_target_pairs={{0,4},{2,6},{4,0},{6,2},{1,5},{3,7},{5,1},{7,3},{8,12},{10,14},{12... | collective-permute-start | bytes 1376264 | tf_op jit(solution)/shard_map/ppermute | solution.py:23
  294.0 143.8 %reduce-scatter.5.cloned.1.call-start = ((), (), s32[]{:S(2)}) async-start(), calls=%async_computation.4 | async-start | bytes 4902912 | tf_op jit(solution)/shard_map/reduce_scatter | solution.py:419
  301.2 20.2 %collective-permute-start.42 = (bf16[2,64,1792]{2,1,0:T(8,128)(2,1)S(1)}, bf16[2,64,1792]{2,1,0:T(8,128)(2,1)S(1)}, u32[]{:S(2)}, u32[]{:S(2)}) collective-permute-start(bf16[2,64,1792]{2,1,0:T(8,128)(2,1)S(1)} %get-tuple-element.290.x0), channel_id=1, source_target_pairs={{0,24},{8,16},{16,8},{24,0},{1,25},{9,17},{17,9},{25,1},{2,26},{10... | collective-permute-start | bytes 1376264 | tf_op jit(solution)/shard_map/ppermute | solution.py:23
  357.5 13.9 %collective-permute-start.52 = (bf16[2,144,256]{2,1,0:T(8,128)(2,1)S(1)}, bf16[2,144,256]{2,1,0:T(8,128)(2,1)S(1)}, u32[]{:S(2)}, u32[]{:S(2)}) collective-permute-start(bf16[2,144,256]{2,1,0:T(8,128)(2,1)S(1)} %get-tuple-element.312), channel_id=1, source_target_pairs={{0,4},{2,6},{4,0},{6,2},{1,5},{3,7},{5,1},{7,3},{8,12},{10,14},{12... | collective-permute-start | bytes 442376 | tf_op jit(solution)/shard_map/ppermute | solution.py:23
  380.8 23.4 %collective-permute-start.58 = (bf16[2,64,1792]{2,1,0:T(8,128)(2,1)}, bf16[2,64,1792]{2,1,0:T(8,128)(2,1)S(1)}, u32[]{:S(2)}, u32[]{:S(2)}) collective-permute-start(bf16[2,64,1792]{2,1,0:T(8,128)(2,1)} %get-tuple-element.327), channel_id=1, source_target_pairs={{0,8},{8,0},{16,24},{24,16},{1,9},{9,1},{17,25},{25,17},{2,10},{10... | collective-permute-start | bytes 1376264 | tf_op jit(solution)/shard_map/ppermute | solution.py:23
  381.1 23.1 %collective-permute-start.59 = (bf16[2,64,1792]{2,1,0:T(8,128)(2,1)}, bf16[2,64,1792]{2,1,0:T(8,128)(2,1)}, u32[]{:S(2)}, u32[]{:S(2)}) collective-permute-start(bf16[2,64,1792]{2,1,0:T(8,128)(2,1)} %get-tuple-element.328), channel_id=1, source_target_pairs={{0,16},{8,24},{16,0},{24,8},{1,17},{9,25},{17,1},{25,9},{2,18},{10... | collective-permute-start | bytes 1376264 | tf_op jit(solution)/shard_map/ppermute | solution.py:23
  382.6 21.7 %collective-permute-start.56 = (bf16[56,2432]{1,0:T(8,128)(2,1)}, bf16[56,2432]{1,0:T(8,128)(2,1)S(1)}, u32[]{:S(2)}, u32[]{:S(2)}) collective-permute-start(bf16[56,2432]{1,0:T(8,128)(2,1)} %get-tuple-element.325), channel_id=1, source_target_pairs={{0,4},{2,6},{4,0},{6,2},{1,5},{3,7},{5,1},{7,3},{8,12},{10,14},{12... | collective-permute-start | bytes 817160 | tf_op jit(solution)/shard_map/ppermute | solution.py:23
  386.1 18.1 %collective-permute-start.55 = (bf16[4,56,576]{2,1,0:T(8,128)(2,1)S(1)}, bf16[4,56,576]{2,1,0:T(8,128)(2,1)}, u32[]{:S(2)}, u32[]{:S(2)}) collective-permute-start(bf16[4,56,576]{2,1,0:T(8,128)(2,1)S(1)} %get-tuple-element.324), channel_id=1, source_target_pairs={{0,2},{2,0},{4,6},{6,4},{1,3},{3,1},{5,7},{7,5},{8,10},{10,8},{12,... | collective-permute-start | bytes 774152 | tf_op jit(solution)/shard_map/ppermute | solution.py:23
  386.1 18.1 %collective-permute-start.57 = (bf16[56,1792]{1,0:T(8,128)(2,1)}, bf16[56,1792]{1,0:T(8,128)(2,1)}, u32[]{:S(2)}, u32[]{:S(2)}) collective-permute-start(bf16[56,1792]{1,0:T(8,128)(2,1)} %get-tuple-element.326), channel_id=1, source_target_pairs={{0,6},{2,4},{4,2},{6,0},{1,7},{3,5},{5,3},{7,1},{8,14},{10,12},{12... | collective-permute-start | bytes 602120 | tf_op jit(solution)/shard_map/ppermute | solution.py:23
  405.3 23.4 %collective-permute-start.62 = (bf16[2,64,1792]{2,1,0:T(8,128)(2,1)}, bf16[2,64,1792]{2,1,0:T(8,128)(2,1)S(1)}, u32[]{:S(2)}, u32[]{:S(2)}) collective-permute-start(bf16[2,64,1792]{2,1,0:T(8,128)(2,1)} %get-tuple-element.334), channel_id=1, source_target_pairs={{0,24},{8,16},{16,8},{24,0},{1,25},{9,17},{17,9},{25,1},{2,26},{10... | collective-permute-start | bytes 1376264 | tf_op jit(solution)/shard_map/ppermute | solution.py:23
  407.6 17.4 %collective-permute-start.60 = (bf16[4,56,576]{2,1,0:T(8,128)(2,1)}, bf16[4,56,576]{2,1,0:T(8,128)(2,1)S(1)}, u32[]{:S(2)}, u32[]{:S(2)}) collective-permute-start(bf16[4,56,576]{2,1,0:T(8,128)(2,1)} %get-tuple-element.332), channel_id=1, source_target_pairs={{0,2},{2,0},{4,6},{6,4},{1,3},{3,1},{5,7},{7,5},{8,10},{10,8},{12,... | collective-permute-start | bytes 774152 | tf_op jit(solution)/shard_map/ppermute | solution.py:23
  410.9 14.1 %collective-permute-start.61 = (bf16[4,56,576]{2,1,0:T(8,128)(2,1)S(1)}, bf16[4,56,576]{2,1,0:T(8,128)(2,1)S(1)}, u32[]{:S(2)}, u32[]{:S(2)}) collective-permute-start(bf16[4,56,576]{2,1,0:T(8,128)(2,1)S(1)} %fusion.33), channel_id=1, source_target_pairs={{0,4},{2,6},{4,0},{6,2},{1,5},{3,7},{5,1},{7,3},{8,12},{10,14},{12... | collective-permute-start | bytes 774152 | tf_op jit(solution)/shard_map/ppermute | solution.py:23
  410.9 17.8 %collective-permute-start.63 = (bf16[56,2432]{1,0:T(8,128)(2,1)}, bf16[56,2432]{1,0:T(8,128)(2,1)S(1)}, u32[]{:S(2)}, u32[]{:S(2)}) collective-permute-start(bf16[56,2432]{1,0:T(8,128)(2,1)} %get-tuple-element.335), channel_id=1, source_target_pairs={{0,2},{2,0},{4,6},{6,4},{1,3},{3,1},{5,7},{7,5},{8,10},{10,8},{12,... | collective-permute-start | bytes 817160 | tf_op jit(solution)/shard_map/ppermute | solution.py:23
  (110 other events, 958.5 us)
Sparse Core Ops, SparseCore 0:
  9.9 53.6 all-gather.7
  74.4 57.3 all-gather.9
  229.6 59.8 all-gather.5
  294.2 75.2 reduce-scatter.2
  372.8 61.4 reduce-scatter.4

commit v3 on v2

--- a/solution.py
+++ b/solution.py
@@ -578,7 +578,7 @@
     )
     grad_out_w = plus(grad_out_w[0], out_got).astype(bf16)
     sent, grad_out_w = tie(sent, grad_out_w)
-    out_got = [swap(grad_out_w[o], LINE, o) for o in range(1, 3)]
+    *out_got, out_last = [swap(grad_out_w[o], LINE, o) for o in range(1, 4)]
     grads_out = call(
         functools.partial(bwd_kernel, *geometry),
         ids,
@@ -592,7 +592,7 @@
         room=36,
     )
     grads_out, out_got = tie(grads_out, out_got)
-    grad_qkv, _, (grad_ffn_w,) = exchange(grads_out, far_beside=(grad_ffn_w,))
+    grad_qkv, _, (grad_ffn_w, out_last) = exchange(grads_out, far_beside=(grad_ffn_w, out_last))
     grad_qkv_w, own_back, attn_back = call(
         functools.partial(qkv_back_kernel, hd, copies, fw, vw),
         ids,
@@ -607,17 +607,16 @@
     row_moves = [(attn_back[o - 1], HEAD, o) for o in range(1, 4)]
     got, _ = window([(grad_qkv_w[k], "c", k) for k in range(1, cores)])
     grad_qkv_w = plus(grad_qkv_w[0], got).astype(bf16)
-    (passing, ffn_2, out_last, *row_got), _ = window(
-        [by_way(grad_qkv_w), (ffn_pieces[2], LINE, 2), (grad_out_w[3], LINE, 3)] + row_moves[:2]
+    (passing, ffn_2, *row_got), _ = window(
+        [by_way(grad_qkv_w), (ffn_pieces[2], LINE, 2)] + row_moves[:2]
     )
     out_got = out_got + [out_last]
-    (got_1, got_2, last, ffn_1), _ = window(
-        rest_moves(grad_qkv_w, passing) + [row_moves[2], (ffn_pieces[1], LINE, 1)]
-    )
+    (got_1, got_2, last), _ = window(rest_moves(grad_qkv_w, passing) + [row_moves[2]])
     row_got = row_got + [last]
     grad_qkv_w = plus(grad_qkv_w[0], [got_1, got_2]).astype(bf16)
-    (*got, ffn_3), _ = window(turn_moves(grad_qkv_w, HEAD) + [(ffn_pieces[3], LINE, 3)])
-    grad_down, got = tie(grad_down, got)
+    (*got, ffn_1, ffn_3), _ = window(
+        turn_moves(grad_qkv_w, HEAD) + [(ffn_pieces[1], LINE, 1), (ffn_pieces[3], LINE, 3)]
+    )
     rows_f32 = lambda w: jax.ShapeDtypeStruct(w.shape, f32)
     one = jax.ShapeDtypeStruct((drow, 1), f32)
     gg, gu, gain_sum_two = call(
@@ -634,6 +633,7 @@
         [rows_f32(w_query), rows_f32(w_key), rows_f32(w_value), one],
         [pltpu.VMEM((4, drow, hd * pw), bf16)],
     )
+    grad_down, gq, gg = tie(grad_down, gq, gg)
     grad_out_w = plus(grad_out_w[0], out_got)
     grad_in = plus(own_back, row_got)
     grad_tokens = grad_resid + norm_back(grad_in, tokens_f, scale_one, gain_attn)

time: 459 us -> 454 us (0.989)
    unnamed x138 -> x142, local copies, waits for them, and re-layouts: 9.2 us -> 9.14 us
  transfers between devices with their start and end apart: 73 -> 73, of which waited for: 42 -> 44; matrix products, arithmetic and copies ran while one was open for 23% -> 23% of each run, Pallas kernels for 6% -> 7%
where the time goes in v3:
time: 454 us; the launch traced here: 450 us
  waiting for transfers between devices  208 us (46%)
  starting transfers between devices  73.2 us (16%)
  matrix products  49.2 us (11%)
  local copies, waits for them, and re-layouts  38 us (8%)
  other arithmetic  35.1 us (8%)
  Pallas kernels  29.6 us (7%)
  between operations  17.6 us (4%)
    ppermute x68, waiting for transfers between devices, swap(): return lax.ppermute(x, axis, [(i, i ^ o) for i in range(n)])  207 us
    ppermute x68, starting transfers between devices, swap(): return lax.ppermute(x, axis, [(i, i ^ o) for i in range(n)])  72.4 us
    dot_general x14, matrix products, dot(): lax.dot_general(a, b, (((ca,), (cb,)), ((), ())), preferred_element_type=...  49.2 us
    pallas_call x9, Pallas kernels, call(): pl.pallas_call(body, out_shape=outs, in_specs=[pl.BlockSpec(memory_space=...  29.6 us
    unnamed x142, local copies, waits for them, and re-layouts  9.14 us
  transfers between devices with their start and end apart: 73, of which 44 were waited for; matrix products, arithmetic and copies ran while one was open for 23% of the time, Pallas kernels for 7%

profile of v3, /device:TPU:0, one launch (start us, length us, event | category | flops | bytes accessed | tf_op | source)
XLA Modules:
  0.0 450.2 jit_solution(17933982170984000729)
XLA Ops:
  41.2 7.4 %collective-permute-done.7 = bf16[4,56,576]{2,1,0:T(8,128)(2,1)S(1)} collective-permute-done((bf16[4,56,576]{2,1,0:T(8,128)(2,1)S(1)}, bf16[4,56,576]{2,1,0:T(8,128)(2,1)S(1)}, u32[]{:S(2)}, u32[]{:S(2)}) %collective-permute-start.7) | collective-permute-done | bytes 258080 | tf_op jit(solution)/shard_map/ppermute | solution.py:23
  48.6 3.7 collective-permute-done.8
  55.3 5.6 %collective-permute-done.6.x2 = bf16[2,64,1792]{2,1,0:T(8,128)(2,1)S(1)} collective-permute-done((bf16[2,64,1792]{2,1,0:T(8,128)(2,1)S(1)}, bf16[2,64,1792]{2,1,0:T(8,128)(2,1)S(1)}, u32[]{:S(2)}, u32[]{:S(2)}) %collective-permute-start.6) | collective-permute-done | bytes 458784 | tf_op jit(solution)/shard_map/ppermute | solution.py:23
  62.1 8.4 %collective-permute-done.10 = bf16[4,56,576]{2,1,0:T(8,128)(2,1)S(1)} collective-permute-done((bf16[4,56,576]{2,1,0:T(8,128)(2,1)S(1)}, bf16[4,56,576]{2,1,0:T(8,128)(2,1)S(1)}, u32[]{:S(2)}, u32[]{:S(2)}) %collective-permute-start.10) | collective-permute-done | bytes 258080 | tf_op jit(solution)/shard_map/ppermute | solution.py:23
  88.3 8.1 %collective-permute-done.15.got2 = bf16[2,144,256]{2,1,0:T(8,128)(2,1)S(1)} collective-permute-done((bf16[2,144,256]{2,1,0:T(8,128)(2,1)S(1)}, bf16[2,144,256]{2,1,0:T(8,128)(2,1)S(1)}, u32[]{:S(2)}, u32[]{:S(2)}) %collective-permute-start.15) | collective-permute-done | bytes 147488 | tf_op jit(solution)/shard_map/ppermute | solution.py:23
  99.2 4.8 %shard_map.222 = (bf16[4,144,512]{2,1,0:T(8,128)(2,1)S(1)}, f32[4,512,128]{2,1,0:T(8,128)S(1)}, bf16[2,4,112,256]{3,2,1,0:T(8,128)(2,1)S(1)}) custom-call(s32[3]{0:T(128)S(1)} %pad_add_fusion.ids, bf16[2,144,256]{2,1,0:T(8,128)(2,1)S(1)} %get-tuple-element.407.got0, bf16[2,144,256]{2,1,0:T(8,128)(2,1)S(1)} %collective-permute-done.14.got1, ...), custom_call_target="tpu_custom_call" | custom-call | tf_op jit(solution)/shard_map/pallas_call | solution.py:374
  106.3 4.0 collective-permute-done.19
  115.0 8.4 %collective-permute-done.20.g1 = bf16[2,112,256]{2,1,0:T(8,128)(2,1)S(1)} collective-permute-done((bf16[2,112,256]{2,1,0:T(8,128)(2,1)S(1)}, bf16[2,112,256]{2,1,0:T(8,128)(2,1)S(1)}, u32[]{:S(2)}, u32[]{:S(2)}) %collective-permute-start.20) | collective-permute-done | bytes 114720 | tf_op jit(solution)/shard_map/ppermute | solution.py:23
  135.2 7.6 %copy.66 = bf16[4,4,2,56,2432]{4,3,2,1,0:T(8,128)(2,1)} copy(bf16[4,4,2,56,2432]{4,3,1,2,0:T(8,128)(2,1)} %bitcast.284) | data formatting | bytes 17432576 | tf_op jit(solution)/shard_map/transpose | solution.py:456
  143.9 10.9 %collective-permute-done.26 = bf16[2,64,1792]{2,1,0:T(8,128)(2,1)} collective-permute-done((bf16[2,64,1792]{2,1,0:T(8,128)(2,1)}, bf16[2,64,1792]{2,1,0:T(8,128)(2,1)}, u32[]{:S(2)}, u32[]{:S(2)}) %collective-permute-start.26) | collective-permute-done | bytes 458784 | tf_op jit(solution)/shard_map/ppermute | solution.py:23
  159.7 5.1 %fusion.70 = f32[128,2432]{1,0:T(8,128)S(1)} fusion(bf16[128,1792]{1,0:T(8,128)(2,1)S(1)} %bitcast.288, bf16[1792,2432]{1,0:T(8,128)(2,1)} %bitcast.266), kind=kOutput, calls=%fused_computation.211 | convolution fusion | flops 1115684864 | bytes 10420224 | tf_op jit(solution)/shard_map/dot_general | solution.py:18
  167.1 9.9 %collective-permute-done.28 = bf16[2,64,1792]{2,1,0:T(8,128)(2,1)S(1)} collective-permute-done((bf16[2,64,1792]{2,1,0:T(8,128)(2,1)S(1)}, bf16[2,64,1792]{2,1,0:T(8,128)(2,1)S(1)}, u32[]{:S(2)}, u32[]{:S(2)}) %collective-permute-start.28) | collective-permute-done | bytes 458784 | tf_op jit(solution)/shard_map/ppermute | solution.py:23
  192.6 15.1 %collective-permute-done.31 = bf16[2,64,1792]{2,1,0:T(8,128)(2,1)S(1)} collective-permute-done((bf16[2,64,1792]{2,1,0:T(8,128)(2,1)S(1)}, bf16[2,64,1792]{2,1,0:T(8,128)(2,1)S(1)}, u32[]{:S(2)}, u32[]{:S(2)}) %collective-permute-start.31) | collective-permute-done | bytes 458784 | tf_op jit(solution)/shard_map/ppermute | solution.py:23
  210.6 8.3 %collective-permute-done.32 = bf16[2,64,1792]{2,1,0:T(8,128)(2,1)S(1)} collective-permute-done((bf16[2,64,1792]{2,1,0:T(8,128)(2,1)S(1)}, bf16[2,64,1792]{2,1,0:T(8,128)(2,1)S(1)}, u32[]{:S(2)}, u32[]{:S(2)}) %collective-permute-start.32) | collective-permute-done | bytes 458784 | tf_op jit(solution)/shard_map/ppermute | solution.py:23
  218.8 6.2 %collective-permute-done.33 = bf16[2,64,1792]{2,1,0:T(8,128)(2,1)S(1)} collective-permute-done((bf16[2,64,1792]{2,1,0:T(8,128)(2,1)S(1)}, bf16[2,64,1792]{2,1,0:T(8,128)(2,1)S(1)}, u32[]{:S(2)}, u32[]{:S(2)}) %collective-permute-start.33) | collective-permute-done | bytes 458784 | tf_op jit(solution)/shard_map/ppermute | solution.py:23
  229.9 4.0 fusion.73
  234.4 7.1 %fusion.74 = f32[128,1792]{1,0:T(8,128)} fusion(bf16[128,2432]{1,0:T(8,128)(2,1)S(1)} %pad_maximum_fusion.4, bf16[1792,2432]{1,0:T(8,128)(2,1)} %bitcast.267), kind=kOutput, calls=%fused_computation.215 | convolution fusion | flops 1115684864 | bytes 10256384 | tf_op jit(solution)/shard_map/dot_general | solution.py:18
  262.4 5.9 %convolution_convert_fusion.1 = bf16[1216,1792]{1,0:T(8,128)(2,1)} fusion(bf16[512,1216]{1,0:T(8,128)(2,1)S(1)} %copy-done.46, bf16[128,1792]{1,0:T(8,128)(2,1)S(1)} %bitcast.309, bf16[128,1792]{1,0:T(8,128)(2,1)} %bitcast.77, bf16[128,1792]{1,0:T(8,128)(2,1)} %bitcast.76, bf16[128,1792]{1,0:T(8,128)(2,1)} %bitcast.73), kind=kOutput, calls=%fused_computation.1 | convolution fusion | flops 2240888832 | bytes 7438336 | tf_op jit(solution)/shard_map/dot_general | solution.py:18
  274.8 10.8 %convolution_convert_fusion = bf16[1792,2432]{1,0:T(8,128)(2,1)} fusion(bf16[512,1792]{1,0:T(8,128)(2,1)} %pad_maximum_fusion.1, bf16[512,2432]{1,0:T(8,128)(2,1)} %pad_maximum_fusion), kind=kOutput, calls=%fused_computation | convolution fusion | flops 4467097600 | bytes 13041664 | tf_op jit(solution)/shard_map/dot_general | solution.py:18
  285.6 7.5 %copy.73 = bf16[4,4,2,56,2432]{4,3,1,2,0:T(8,128)(2,1)} copy(bf16[4,4,2,56,2432]{4,3,2,1,0:T(8,128)(2,1)} %bitcast.285) | data formatting | bytes 17432576 | tf_op jit(solution)/shard_map/reshape | solution.py:560
  302.4 10.0 %collective-permute-done.40.x1 = bf16[2,64,1792]{2,1,0:T(8,128)(2,1)S(1)} collective-permute-done((bf16[2,64,1792]{2,1,0:T(8,128)(2,1)S(1)}, bf16[2,64,1792]{2,1,0:T(8,128)(2,1)S(1)}, u32[]{:S(2)}, u32[]{:S(2)}) %collective-permute-start.40) | collective-permute-done | bytes 458784 | tf_op jit(solution)/shard_map/ppermute | solution.py:23
  312.4 8.8 %collective-permute-done.42.x3 = bf16[2,64,1792]{2,1,0:T(8,128)(2,1)S(1)} collective-permute-done((bf16[2,64,1792]{2,1,0:T(8,128)(2,1)S(1)}, bf16[2,64,1792]{2,1,0:T(8,128)(2,1)S(1)}, u32[]{:S(2)}, u32[]{:S(2)}) %collective-permute-start.42) | collective-permute-done | bytes 458784 | tf_op jit(solution)/shard_map/ppermute | solution.py:23
  326.1 3.8 collective-permute-start.46
  332.2 5.2 %collective-permute-done.45.got2 = bf16[2,112,256]{2,1,0:T(8,128)(2,1)S(1)} collective-permute-done((bf16[2,112,256]{2,1,0:T(8,128)(2,1)S(1)}, bf16[2,112,256]{2,1,0:T(8,128)(2,1)S(1)}, u32[]{:S(2)}, u32[]{:S(2)}) %collective-permute-start.45) | collective-permute-done | bytes 114720 | tf_op jit(solution)/shard_map/ppermute | solution.py:23
  341.5 8.3 %shard_map.225 = bf16[2,4,144,256]{3,2,1,0:T(8,128)(2,1)S(1)} custom-call(s32[3]{0:T(128)S(1)} %pad_add_fusion.ids, bf16[4,144,512]{2,1,0:T(8,128)(2,1)S(1)} %copy-done.20, f32[4,512,128]{2,1,0:T(8,128)S(1)} %copy-done.14, bf16[2,112,256]{2,1,0:T(8,128)(2,1)S(1)} %get-tuple-element.303.got0, bf16[2,112,256]{2,1,0:T(8,128)(2,1)S(1)} %collective-permute-done.44.got1, ...), custom_call_target="tpu_custom_call" | custom-call | tf_op jit(solution)/shard_map/pallas_call | solution.py:374
  359.1 3.6 collective-permute-done.54
  362.7 4.1 collective-permute-done.51.g1
  366.8 6.7 %collective-permute-done.52.g2 = bf16[2,144,256]{2,1,0:T(8,128)(2,1)S(1)} collective-permute-done((bf16[2,144,256]{2,1,0:T(8,128)(2,1)S(1)}, bf16[2,144,256]{2,1,0:T(8,128)(2,1)S(1)}, u32[]{:S(2)}, u32[]{:S(2)}) %collective-permute-start.52) | collective-permute-done | bytes 147488 | tf_op jit(solution)/shard_map/ppermute | solution.py:23
  373.6 5.0 %shard_map.226 = (bf16[2,4,4,56,576]{4,3,2,1,0:T(8,128)(2,1)S(1)}, f32[2,64,1792]{2,1,0:T(8,128)S(1)}, bf16[3,2,64,1792]{3,2,1,0:T(8,128)(2,1)S(1)}) custom-call(s32[3]{0:T(128)S(1)} %pad_add_fusion.ids, bf16[2,144,256]{2,1,0:T(8,128)(2,1)S(1)} %get-tuple-element.401.g0, bf16[2,144,256]{2,1,0:T(8,128)(2,1)S(1)} %collective-permute-done.51.g1, ...), custom_call_target="tpu_custom_call" | custom-call | tf_op jit(solution)/shard_map/pallas_call | solution.py:374
  385.5 3.9 collective-permute-start.57
  391.6 10.4 %collective-permute-done.56 = bf16[4,56,576]{2,1,0:T(8,128)(2,1)} collective-permute-done((bf16[4,56,576]{2,1,0:T(8,128)(2,1)}, bf16[4,56,576]{2,1,0:T(8,128)(2,1)}, u32[]{:S(2)}, u32[]{:S(2)}) %collective-permute-start.56) | collective-permute-done | bytes 258080 | tf_op jit(solution)/shard_map/ppermute | solution.py:23
  409.0 8.1 %collective-permute-done.60 = bf16[4,56,576]{2,1,0:T(8,128)(2,1)S(1)} collective-permute-done((bf16[4,56,576]{2,1,0:T(8,128)(2,1)S(1)}, bf16[4,56,576]{2,1,0:T(8,128)(2,1)S(1)}, u32[]{:S(2)}, u32[]{:S(2)}) %collective-permute-start.60) | collective-permute-done | bytes 258080 | tf_op jit(solution)/shard_map/ppermute | solution.py:23
  (377 shorter events, 205.9 us)
Async XLA Ops:
  7.2 89.2 %all-gather.8.cloned.1.call-start = ((), (), s32[]{:S(2)}) async-start(), calls=%async_computation.5 | async-start | bytes 4902912 | tf_op jit(solution)/shard_map/all_gather | solution.py:416
  7.9 127.3 %all-gather.10.cloned.1.call-start = ((), (), s32[]{:S(2)}) async-start(), calls=%async_computation.6 | async-start | bytes 9805824 | tf_op jit(solution)/shard_map/all_gather | solution.py:416
  15.2 15.9 %collective-permute-start.3 = (bf16[56,2432]{1,0:T(8,128)(2,1)S(1)}, bf16[56,2432]{1,0:T(8,128)(2,1)S(1)}, u32[]{:S(2)}, u32[]{:S(2)}) collective-permute-start(bf16[56,2432]{1,0:T(8,128)(2,1)S(1)} %get-tuple-element.191), channel_id=1, source_target_pairs={{0,2},{2,0},{4,6},{6,4},{1,3},{3,1},{5,7},{7,5},{8,10},{10,8},{12,... | collective-permute-start | bytes 817160 | tf_op jit(solution)/shard_map/ppermute | solution.py:23
  18.2 14.8 %collective-permute-start.4 = (bf16[56,2432]{1,0:T(8,128)(2,1)S(1)}, bf16[56,2432]{1,0:T(8,128)(2,1)S(1)}, u32[]{:S(2)}, u32[]{:S(2)}) collective-permute-start(bf16[56,2432]{1,0:T(8,128)(2,1)S(1)} %get-tuple-element.192), channel_id=1, source_target_pairs={{0,4},{2,6},{4,0},{6,2},{1,5},{3,7},{5,1},{7,3},{8,12},{10,14},{12... | collective-permute-start | bytes 817160 | tf_op jit(solution)/shard_map/ppermute | solution.py:23
  34.9 20.4 %collective-permute-start.5 = (bf16[2,64,1792]{2,1,0:T(8,128)(2,1)S(1)}, bf16[2,64,1792]{2,1,0:T(8,128)(2,1)S(1)}, u32[]{:S(2)}, u32[]{:S(2)}) collective-permute-start(bf16[2,64,1792]{2,1,0:T(8,128)(2,1)S(1)} %fusion.12.x0), channel_id=1, source_target_pairs={{0,8},{8,0},{16,24},{24,16},{1,9},{9,1},{17,25},{25,17},{2,10},{10... | collective-permute-start | bytes 1376264 | tf_op jit(solution)/shard_map/ppermute | solution.py:23
  36.4 24.5 %collective-permute-start.6 = (bf16[2,64,1792]{2,1,0:T(8,128)(2,1)S(1)}, bf16[2,64,1792]{2,1,0:T(8,128)(2,1)S(1)}, u32[]{:S(2)}, u32[]{:S(2)}) collective-permute-start(bf16[2,64,1792]{2,1,0:T(8,128)(2,1)S(1)} %fusion.12.x0), channel_id=1, source_target_pairs={{0,16},{8,24},{16,0},{24,8},{1,17},{9,25},{17,1},{25,9},{2,18},{10... | collective-permute-start | bytes 1376264 | tf_op jit(solution)/shard_map/ppermute | solution.py:23
  38.4 13.9 %collective-permute-start.8 = (bf16[4,56,576]{2,1,0:T(8,128)(2,1)S(1)}, bf16[4,56,576]{2,1,0:T(8,128)(2,1)S(1)}, u32[]{:S(2)}, u32[]{:S(2)}) collective-permute-start(bf16[4,56,576]{2,1,0:T(8,128)(2,1)S(1)} %bitcast_dynamic-update-slice_fusion.15), channel_id=1, source_target_pairs={{0,4},{2,6},{4,0},{6,2},{1,5},{3,7},{5,1},{7,3},{8,12},{10,14},{12... | collective-permute-start | bytes 774152 | tf_op jit(solution)/shard_map/ppermute | solution.py:23
  74.2 219.4 %all-gather.6.cloned.1.call-start = ((), (), s32[]{:S(2)}) async-start(), calls=%async_computation.2 | async-start | bytes 1081344 | tf_op jit(solution)/shard_map/all_gather | solution.py:527
  82.7 13.8 %collective-permute-start.15 = (bf16[2,144,256]{2,1,0:T(8,128)(2,1)S(1)}, bf16[2,144,256]{2,1,0:T(8,128)(2,1)S(1)}, u32[]{:S(2)}, u32[]{:S(2)}) collective-permute-start(bf16[2,144,256]{2,1,0:T(8,128)(2,1)S(1)} %get-tuple-element.215), channel_id=1, source_target_pairs={{0,4},{2,6},{4,0},{6,2},{1,5},{3,7},{5,1},{7,3},{8,12},{10,14},{12... | collective-permute-start | bytes 442376 | tf_op jit(solution)/shard_map/ppermute | solution.py:23
  129.2 14.7 %collective-permute-start.25 = (bf16[2,64,1792]{2,1,0:T(8,128)(2,1)}, bf16[2,64,1792]{2,1,0:T(8,128)(2,1)S(1)}, u32[]{:S(2)}, u32[]{:S(2)}) collective-permute-start(bf16[2,64,1792]{2,1,0:T(8,128)(2,1)} %get-tuple-element.237), channel_id=1, source_target_pairs={{0,8},{8,0},{16,24},{24,16},{1,9},{9,1},{17,25},{25,17},{2,10},{10... | collective-permute-start | bytes 1376264 | tf_op jit(solution)/shard_map/ppermute | solution.py:23
  132.4 22.4 %collective-permute-start.26 = (bf16[2,64,1792]{2,1,0:T(8,128)(2,1)}, bf16[2,64,1792]{2,1,0:T(8,128)(2,1)}, u32[]{:S(2)}, u32[]{:S(2)}) collective-permute-start(bf16[2,64,1792]{2,1,0:T(8,128)(2,1)} %get-tuple-element.238), channel_id=1, source_target_pairs={{0,16},{8,24},{16,0},{24,8},{1,17},{9,25},{17,1},{25,9},{2,18},{10... | collective-permute-start | bytes 1376264 | tf_op jit(solution)/shard_map/ppermute | solution.py:23
  132.9 21.9 %collective-permute-start.27 = (bf16[2,64,1792]{2,1,0:T(8,128)(2,1)S(1)}, bf16[2,64,1792]{2,1,0:T(8,128)(2,1)}, u32[]{:S(2)}, u32[]{:S(2)}) collective-permute-start(bf16[2,64,1792]{2,1,0:T(8,128)(2,1)S(1)} %get-tuple-element.239), channel_id=1, source_target_pairs={{0,24},{8,16},{16,8},{24,0},{1,25},{9,17},{17,9},{25,1},{2,26},{10... | collective-permute-start | bytes 1376264 | tf_op jit(solution)/shard_map/ppermute | solution.py:23
  156.8 20.2 %collective-permute-start.28 = (bf16[2,64,1792]{2,1,0:T(8,128)(2,1)S(1)}, bf16[2,64,1792]{2,1,0:T(8,128)(2,1)S(1)}, u32[]{:S(2)}, u32[]{:S(2)}) collective-permute-start(bf16[2,64,1792]{2,1,0:T(8,128)(2,1)S(1)} %multiply_convert_fusion.3), channel_id=1, source_target_pairs={{0,2},{2,0},{4,6},{6,4},{1,3},{3,1},{5,7},{7,5},{8,10},{10,8},{12,... | collective-permute-start | bytes 1376264 | tf_op jit(solution)/shard_map/ppermute | solution.py:23
  158.1 22.2 %collective-permute-start.29 = (bf16[2,64,1792]{2,1,0:T(8,128)(2,1)S(1)}, bf16[2,64,1792]{2,1,0:T(8,128)(2,1)S(1)}, u32[]{:S(2)}, u32[]{:S(2)}) collective-permute-start(bf16[2,64,1792]{2,1,0:T(8,128)(2,1)S(1)} %multiply_convert_fusion.3), channel_id=1, source_target_pairs={{0,4},{2,6},{4,0},{6,2},{1,5},{3,7},{5,1},{7,3},{8,12},{10,14},{12... | collective-permute-start | bytes 1376264 | tf_op jit(solution)/shard_map/ppermute | solution.py:23
  191.9 15.8 %collective-permute-start.31 = (bf16[2,64,1792]{2,1,0:T(8,128)(2,1)S(1)}, bf16[2,64,1792]{2,1,0:T(8,128)(2,1)S(1)}, u32[]{:S(2)}, u32[]{:S(2)}) collective-permute-start(bf16[2,64,1792]{2,1,0:T(8,128)(2,1)S(1)} %convolution_convert_fusion.2), channel_id=1, source_target_pairs={{0,2},{2,0},{4,6},{6,4},{1,3},{3,1},{5,7},{7,5},{8,10},{10,8},{12,... | collective-permute-start | bytes 1376264 | tf_op jit(solution)/shard_map/ppermute | solution.py:23
  207.9 17.1 %collective-permute-start.33 = (bf16[2,64,1792]{2,1,0:T(8,128)(2,1)S(1)}, bf16[2,64,1792]{2,1,0:T(8,128)(2,1)S(1)}, u32[]{:S(2)}, u32[]{:S(2)}) collective-permute-start(bf16[2,64,1792]{2,1,0:T(8,128)(2,1)S(1)} %fusion.27), channel_id=1, source_target_pairs={{0,4},{2,6},{4,0},{6,2},{1,5},{3,7},{5,1},{7,3},{8,12},{10,14},{12... | collective-permute-start | bytes 1376264 | tf_op jit(solution)/shard_map/ppermute | solution.py:23
  228.1 15.8 %collective-permute-start.34 = (bf16[2,64,1792]{2,1,0:T(8,128)(2,1)}, bf16[2,64,1792]{2,1,0:T(8,128)(2,1)}, u32[]{:S(2)}, u32[]{:S(2)}) collective-permute-start(bf16[2,64,1792]{2,1,0:T(8,128)(2,1)} %fusion.67), channel_id=1, source_target_pairs={{0,2},{2,0},{4,6},{6,4},{1,3},{3,1},{5,7},{7,5},{8,10},{10,8},{12,... | collective-permute-start | bytes 1376264 | tf_op jit(solution)/shard_map/ppermute | solution.py:23
  228.1 17.3 %collective-permute-start.35 = (bf16[2,64,1792]{2,1,0:T(8,128)(2,1)}, bf16[2,64,1792]{2,1,0:T(8,128)(2,1)}, u32[]{:S(2)}, u32[]{:S(2)}) collective-permute-start(bf16[2,64,1792]{2,1,0:T(8,128)(2,1)} %fusion.67), channel_id=1, source_target_pairs={{0,4},{2,6},{4,0},{6,2},{1,5},{3,7},{5,1},{7,3},{8,12},{10,14},{12... | collective-permute-start | bytes 1376264 | tf_op jit(solution)/shard_map/ppermute | solution.py:23
  229.4 144.2 %reduce-scatter.3.cloned.1.call-start = ((), (), s32[]{:S(2)}) async-start(), calls=%async_computation.3 | async-start | bytes 9805824 | tf_op jit(solution)/shard_map/reduce_scatter | solution.py:419
  272.5 21.1 %collective-permute-start.38 = (bf16[2,64,1792]{2,1,0:T(8,128)(2,1)}, bf16[2,64,1792]{2,1,0:T(8,128)(2,1)}, u32[]{:S(2)}, u32[]{:S(2)}) collective-permute-start(bf16[2,64,1792]{2,1,0:T(8,128)(2,1)} %get-tuple-element.276), channel_id=1, source_target_pairs={{0,2},{2,0},{4,6},{6,4},{1,3},{3,1},{5,7},{7,5},{8,10},{10,8},{12,... | collective-permute-start | bytes 1376264 | tf_op jit(solution)/shard_map/ppermute | solution.py:23
  272.6 21.0 %collective-permute-start.39 = (bf16[2,64,1792]{2,1,0:T(8,128)(2,1)S(1)}, bf16[2,64,1792]{2,1,0:T(8,128)(2,1)}, u32[]{:S(2)}, u32[]{:S(2)}) collective-permute-start(bf16[2,64,1792]{2,1,0:T(8,128)(2,1)S(1)} %add_convert_fusion), channel_id=1, source_target_pairs={{0,4},{2,6},{4,0},{6,2},{1,5},{3,7},{5,1},{7,3},{8,12},{10,14},{12... | collective-permute-start | bytes 1376264 | tf_op jit(solution)/shard_map/ppermute | solution.py:23
  293.7 145.1 %reduce-scatter.5.cloned.1.call-start = ((), (), s32[]{:S(2)}) async-start(), calls=%async_computation.4 | async-start | bytes 4902912 | tf_op jit(solution)/shard_map/reduce_scatter | solution.py:419
  298.9 13.5 %collective-permute-start.40 = (bf16[2,64,1792]{2,1,0:T(8,128)(2,1)S(1)}, bf16[2,64,1792]{2,1,0:T(8,128)(2,1)S(1)}, u32[]{:S(2)}, u32[]{:S(2)}) collective-permute-start(bf16[2,64,1792]{2,1,0:T(8,128)(2,1)S(1)} %get-tuple-element.288.x0), channel_id=1, source_target_pairs={{0,8},{8,0},{16,24},{24,16},{1,9},{9,1},{17,25},{25,17},{2,10},{10... | collective-permute-start | bytes 1376264 | tf_op jit(solution)/shard_map/ppermute | solution.py:23
  302.1 19.1 %collective-permute-start.42 = (bf16[2,64,1792]{2,1,0:T(8,128)(2,1)S(1)}, bf16[2,64,1792]{2,1,0:T(8,128)(2,1)S(1)}, u32[]{:S(2)}, u32[]{:S(2)}) collective-permute-start(bf16[2,64,1792]{2,1,0:T(8,128)(2,1)S(1)} %get-tuple-element.288.x0), channel_id=1, source_target_pairs={{0,24},{8,16},{16,8},{24,0},{1,25},{9,17},{17,9},{25,1},{2,26},{10... | collective-permute-start | bytes 1376264 | tf_op jit(solution)/shard_map/ppermute | solution.py:23
  354.7 18.8 %collective-permute-start.52 = (bf16[2,144,256]{2,1,0:T(8,128)(2,1)S(1)}, bf16[2,144,256]{2,1,0:T(8,128)(2,1)S(1)}, u32[]{:S(2)}, u32[]{:S(2)}) collective-permute-start(bf16[2,144,256]{2,1,0:T(8,128)(2,1)S(1)} %get-tuple-element.310), channel_id=1, source_target_pairs={{0,4},{2,6},{4,0},{6,2},{1,5},{3,7},{5,1},{7,3},{8,12},{10,14},{12... | collective-permute-start | bytes 442376 | tf_op jit(solution)/shard_map/ppermute | solution.py:23
  357.6 16.0 %collective-permute-start.53 = (bf16[2,144,256]{2,1,0:T(8,128)(2,1)S(1)}, bf16[2,144,256]{2,1,0:T(8,128)(2,1)S(1)}, u32[]{:S(2)}, u32[]{:S(2)}) collective-permute-start(bf16[2,144,256]{2,1,0:T(8,128)(2,1)S(1)} %get-tuple-element.311), channel_id=1, source_target_pairs={{0,6},{2,4},{4,2},{6,0},{1,7},{3,5},{5,3},{7,1},{8,14},{10,12},{12... | collective-permute-start | bytes 442376 | tf_op jit(solution)/shard_map/ppermute | solution.py:23
  383.0 19.0 %collective-permute-start.58 = (bf16[2,64,1792]{2,1,0:T(8,128)(2,1)}, bf16[2,64,1792]{2,1,0:T(8,128)(2,1)S(1)}, u32[]{:S(2)}, u32[]{:S(2)}) collective-permute-start(bf16[2,64,1792]{2,1,0:T(8,128)(2,1)} %get-tuple-element.324), channel_id=1, source_target_pairs={{0,8},{8,0},{16,24},{24,16},{1,9},{9,1},{17,25},{25,17},{2,10},{10... | collective-permute-start | bytes 1376264 | tf_op jit(solution)/shard_map/ppermute | solution.py:23
  384.1 18.0 %collective-permute-start.59 = (bf16[2,64,1792]{2,1,0:T(8,128)(2,1)}, bf16[2,64,1792]{2,1,0:T(8,128)(2,1)}, u32[]{:S(2)}, u32[]{:S(2)}) collective-permute-start(bf16[2,64,1792]{2,1,0:T(8,128)(2,1)} %get-tuple-element.325), channel_id=1, source_target_pairs={{0,16},{8,24},{16,0},{24,8},{1,17},{9,25},{17,1},{25,9},{2,18},{10... | collective-permute-start | bytes 1376264 | tf_op jit(solution)/shard_map/ppermute | solution.py:23
  385.5 16.5 %collective-permute-start.57 = (bf16[56,2432]{1,0:T(8,128)(2,1)}, bf16[56,2432]{1,0:T(8,128)(2,1)S(1)}, u32[]{:S(2)}, u32[]{:S(2)}) collective-permute-start(bf16[56,2432]{1,0:T(8,128)(2,1)} %get-tuple-element.323), channel_id=1, source_target_pairs={{0,4},{2,6},{4,0},{6,2},{1,5},{3,7},{5,1},{7,3},{8,12},{10,14},{12... | collective-permute-start | bytes 817160 | tf_op jit(solution)/shard_map/ppermute | solution.py:23
  403.1 17.5 %collective-permute-start.62 = (bf16[2,64,1792]{2,1,0:T(8,128)(2,1)}, bf16[2,64,1792]{2,1,0:T(8,128)(2,1)S(1)}, u32[]{:S(2)}, u32[]{:S(2)}) collective-permute-start(bf16[2,64,1792]{2,1,0:T(8,128)(2,1)} %get-tuple-element.331), channel_id=1, source_target_pairs={{0,24},{8,16},{16,8},{24,0},{1,25},{9,17},{17,9},{25,1},{2,26},{10... | collective-permute-start | bytes 1376264 | tf_op jit(solution)/shard_map/ppermute | solution.py:23
  406.7 13.9 %collective-permute-start.61 = (bf16[4,56,576]{2,1,0:T(8,128)(2,1)S(1)}, bf16[4,56,576]{2,1,0:T(8,128)(2,1)S(1)}, u32[]{:S(2)}, u32[]{:S(2)}) collective-permute-start(bf16[4,56,576]{2,1,0:T(8,128)(2,1)S(1)} %fusion.33), channel_id=1, source_target_pairs={{0,4},{2,6},{4,0},{6,2},{1,5},{3,7},{5,1},{7,3},{8,12},{10,14},{12... | collective-permute-start | bytes 774152 | tf_op jit(solution)/shard_map/ppermute | solution.py:23
  421.0 13.8 %collective-permute-start.67 = (bf16[56,2432]{1,0:T(8,128)(2,1)S(1)}, bf16[56,2432]{1,0:T(8,128)(2,1)S(1)}, u32[]{:S(2)}, u32[]{:S(2)}) collective-permute-start(bf16[56,2432]{1,0:T(8,128)(2,1)S(1)} %copy-done.50), channel_id=1, source_target_pairs={{0,6},{2,4},{4,2},{6,0},{1,7},{3,5},{5,3},{7,1},{8,14},{10,12},{12... | collective-permute-start | bytes 817160 | tf_op jit(solution)/shard_map/ppermute | solution.py:23
  (112 other events, 1003.7 us)
Sparse Core Ops, SparseCore 0:
  9.9 53.6 all-gather.7
  74.4 57.3 all-gather.9
  229.5 59.9 all-gather.5
  293.8 73.5 reduce-scatter.2
  370.7 66.2 reduce-scatter.4

commit v4 on v3

--- a/solution.py
+++ b/solution.py
@@ -323,6 +323,14 @@
             at = i * (half // drow) + k
             block = total[k * drow : (k + 1) * drow].astype(bf16)
             grad[(at % cores) ^ c, (at // cores % 4) ^ z, at // (4 * cores)] = block
+
+
+def ffn_back_kernel(cores, ids, x, g, out):
+    heads, drow = out.shape[0], out.shape[3]
+    total = dot(x[...], g[...], 0, 0)
+    for k in range(heads * 4 * cores):
+        block = total[k * drow : (k + 1) * drow].astype(bf16)
+        out[k // (4 * cores), k % cores, k // cores % 4] = block
 
 
 def cut_kernel(nh, run, ids, gate, up, wq, wk, wv, out, heads):
@@ -556,9 +564,20 @@
     grad_down = dot(hidden, grad_ffn, 0, 0).astype(bf16).reshape(nb, -1, width)
     passing, grad_down, normed_mlp = tie(passing, grad_down, normed_mlp)
     grad_down = summed(grad_down)
-    grad_ffn_w = dot(normed_mlp, grad_both, 0, 0).astype(bf16)
-    grad_ffn_w = grad_ffn_w.reshape(nh, 4, cores, drow, -1).transpose(0, 2, 1, 3, 4)
-    shares = grad_ffn_w.reshape(nb, 4 * drow, -1)
+    rows, cols = normed_mlp.shape[0], grad_both.shape[1]
+    shares = pl.pallas_call(
+        functools.partial(ffn_back_kernel, cores),
+        grid=(2,),
+        out_shape=jax.ShapeDtypeStruct((nh, cores, 4, drow, cols), bf16),
+        in_specs=[
+            pl.BlockSpec(memory_space=pltpu.SMEM),
+            pl.BlockSpec((rows, width // 2), lambda i: (0, i)),
+            pl.BlockSpec((rows, cols), lambda i: (0, 0)),
+        ],
+        out_specs=pl.BlockSpec((nh // 2, cores, 4, drow, cols), lambda i: (i, 0, 0, 0, 0)),
+        compiler_params=pltpu.CompilerParams(vmem_limit_bytes=40 * 1024 * 1024),
+    )(ids, normed_mlp, grad_both)
+    shares = shares.reshape(nh * cores, 4 * drow, -1)
     got, (shares, loss) = window(rest_moves([x.astype(bf16) for x in part], passing), (shares, loss))
     grad_ffn_w = summed(shares)
     loss = jnp.sum(loss[:, 0, 0]) / (width * count)

time: 454 us -> 450 us (level)
  starting transfers between devices: 73.2 us -> 95.4 us
  waiting for transfers between devices: 208 us -> 192 us
  matrix products: 49.2 us -> 38.6 us
  Pallas kernels: 29.6 us -> 35.4 us
    ppermute x68, starting transfers between devices: 72.4 us -> 94.5 us  [swap(): return lax.ppermute(x, axis, [(i, i ^ o) for i in range(n)])]
    ppermute x68, waiting for transfers between devices: 207 us -> 191 us  [swap(): return lax.ppermute(x, axis, [(i, i ^ o) for i in range(n)])]
    dot_general x14 -> x13, matrix products: 49.2 us -> 38.6 us  [dot(): lax.dot_general(a, b, (((ca,), (cb,)), ((), ())), preferred_element_type=...]
    reshape x1 -> x0, local copies, waits for them, and re-layouts: 7.5 us -> none  [shards(): grad_ffn_w.reshape(nh, 4, cores, drow, -1).transpose(0, 2, 1, 3, 4)]
    pallas_call x0 -> x1, Pallas kernels: none -> 5.84 us  [shards(): pl.pallas_call(functools.partial(ffn_back_kernel, cores), grid=(2,), out_...]
    unnamed x142 -> x138, local copies, waits for them, and re-layouts: 9.14 us -> 14.8 us
  transfers between devices with their start and end apart: 73 -> 73, of which waited for: 44 -> 47; matrix products, arithmetic and copies ran while one was open for 23% -> 18% of each run, Pallas kernels for 7% -> 8%
where the time goes in v4:
time: 450 us; the launch traced here: 448 us
  waiting for transfers between devices  192 us (43%)
  starting transfers between devices  95.4 us (21%)
  matrix products  38.6 us (9%)
  local copies, waits for them, and re-layouts  36.7 us (8%)
  Pallas kernels  35.4 us (8%)
  other arithmetic  31.8 us (7%)
  between operations  17.6 us (4%)
    ppermute x68, waiting for transfers between devices, swap(): return lax.ppermute(x, axis, [(i, i ^ o) for i in range(n)])  191 us
    ppermute x68, starting transfers between devices, swap(): return lax.ppermute(x, axis, [(i, i ^ o) for i in range(n)])  94.5 us
    dot_general x13, matrix products, dot(): lax.dot_general(a, b, (((ca,), (cb,)), ((), ())), preferred_element_type=...  38.6 us
    pallas_call x9, Pallas kernels, call(): pl.pallas_call(body, out_shape=outs, in_specs=[pl.BlockSpec(memory_space=...  29.6 us
    unnamed x138, local copies, waits for them, and re-layouts  14.8 us
  transfers between devices with their start and end apart: 73, of which 47 were waited for; matrix products, arithmetic and copies ran while one was open for 18% of the time, Pallas kernels for 8%

profile of v4, /device:TPU:0, one launch (start us, length us, event | category | flops | bytes accessed | tf_op | source)
XLA Modules:
  0.0 447.8 jit_solution(17530868814239084352)
XLA Ops:
  40.4 6.7 %collective-permute-done.7 = bf16[4,56,576]{2,1,0:T(8,128)(2,1)S(1)} collective-permute-done((bf16[4,56,576]{2,1,0:T(8,128)(2,1)S(1)}, bf16[4,56,576]{2,1,0:T(8,128)(2,1)S(1)}, u32[]{:S(2)}, u32[]{:S(2)}) %collective-permute-start.7) | collective-permute-done | bytes 258080 | tf_op jit(solution)/shard_map/ppermute | solution.py:23
  47.0 3.8 collective-permute-done.8
  59.4 4.4 collective-permute-done.10
  81.6 3.8 collective-permute-done.14.got1
  85.4 7.4 %collective-permute-done.15.got2 = bf16[2,144,256]{2,1,0:T(8,128)(2,1)S(1)} collective-permute-done((bf16[2,144,256]{2,1,0:T(8,128)(2,1)S(1)}, bf16[2,144,256]{2,1,0:T(8,128)(2,1)S(1)}, u32[]{:S(2)}, u32[]{:S(2)}) %collective-permute-start.15) | collective-permute-done | bytes 147488 | tf_op jit(solution)/shard_map/ppermute | solution.py:23
  96.2 4.8 %shard_map.222 = (bf16[4,144,512]{2,1,0:T(8,128)(2,1)S(1)}, f32[4,512,128]{2,1,0:T(8,128)S(1)}, bf16[2,4,112,256]{3,2,1,0:T(8,128)(2,1)S(1)}) custom-call(s32[3]{0:T(128)S(1)} %pad_add_fusion.ids, bf16[2,144,256]{2,1,0:T(8,128)(2,1)S(1)} %get-tuple-element.407.got0, bf16[2,144,256]{2,1,0:T(8,128)(2,1)S(1)} %collective-permute-done.14.got1, ...), custom_call_target="tpu_custom_call" | custom-call | tf_op jit(solution)/shard_map/pallas_call | solution.py:382
  111.2 5.7 %collective-permute-done.20.g1 = bf16[2,112,256]{2,1,0:T(8,128)(2,1)S(1)} collective-permute-done((bf16[2,112,256]{2,1,0:T(8,128)(2,1)S(1)}, bf16[2,112,256]{2,1,0:T(8,128)(2,1)S(1)}, u32[]{:S(2)}, u32[]{:S(2)}) %collective-permute-start.20) | collective-permute-done | bytes 114720 | tf_op jit(solution)/shard_map/ppermute | solution.py:23
  130.3 7.6 %copy.64 = bf16[4,4,2,56,2432]{4,3,2,1,0:T(8,128)(2,1)} copy(bf16[4,4,2,56,2432]{4,3,1,2,0:T(8,128)(2,1)} %bitcast.279) | data formatting | bytes 17432576 | tf_op jit(solution)/shard_map/transpose | solution.py:464
  139.0 11.0 %collective-permute-done.26 = bf16[2,64,1792]{2,1,0:T(8,128)(2,1)} collective-permute-done((bf16[2,64,1792]{2,1,0:T(8,128)(2,1)}, bf16[2,64,1792]{2,1,0:T(8,128)(2,1)}, u32[]{:S(2)}, u32[]{:S(2)}) %collective-permute-start.26) | collective-permute-done | bytes 458784 | tf_op jit(solution)/shard_map/ppermute | solution.py:23
  155.0 5.0 %fusion.70 = f32[128,2432]{1,0:T(8,128)S(1)} fusion(bf16[128,1792]{1,0:T(8,128)(2,1)S(1)} %bitcast.282, bf16[1792,2432]{1,0:T(8,128)(2,1)} %bitcast.262), kind=kOutput, calls=%fused_computation.210 | convolution fusion | flops 1115684864 | bytes 10420224 | tf_op jit(solution)/shard_map/dot_general | solution.py:18
  162.7 10.6 %collective-permute-done.28 = bf16[2,64,1792]{2,1,0:T(8,128)(2,1)S(1)} collective-permute-done((bf16[2,64,1792]{2,1,0:T(8,128)(2,1)S(1)}, bf16[2,64,1792]{2,1,0:T(8,128)(2,1)S(1)}, u32[]{:S(2)}, u32[]{:S(2)}) %collective-permute-start.28) | collective-permute-done | bytes 458784 | tf_op jit(solution)/shard_map/ppermute | solution.py:23
  188.9 8.7 %collective-permute-done.31 = bf16[2,64,1792]{2,1,0:T(8,128)(2,1)S(1)} collective-permute-done((bf16[2,64,1792]{2,1,0:T(8,128)(2,1)S(1)}, bf16[2,64,1792]{2,1,0:T(8,128)(2,1)S(1)}, u32[]{:S(2)}, u32[]{:S(2)}) %collective-permute-start.31) | collective-permute-done | bytes 458784 | tf_op jit(solution)/shard_map/ppermute | solution.py:23
  199.5 6.6 %collective-permute-start.33 = (bf16[2,64,1792]{2,1,0:T(8,128)(2,1)S(1)}, bf16[2,64,1792]{2,1,0:T(8,128)(2,1)S(1)}, u32[]{:S(2)}, u32[]{:S(2)}) collective-permute-start(bf16[2,64,1792]{2,1,0:T(8,128)(2,1)S(1)} %fusion.27), channel_id=1, source_target_pairs={{0,4},{2,6},{4,0},{6,2},{1,5},{3,7},{5,1},{7,3},{8,12},{10,14},{12... | collective-permute-start | bytes 1376264 | tf_op jit(solution)/shard_map/ppermute | solution.py:23
  207.5 8.2 %collective-permute-done.32 = bf16[2,64,1792]{2,1,0:T(8,128)(2,1)S(1)} collective-permute-done((bf16[2,64,1792]{2,1,0:T(8,128)(2,1)S(1)}, bf16[2,64,1792]{2,1,0:T(8,128)(2,1)S(1)}, u32[]{:S(2)}, u32[]{:S(2)}) %collective-permute-start.32) | collective-permute-done | bytes 458784 | tf_op jit(solution)/shard_map/ppermute | solution.py:23
  223.0 3.4 collective-permute-start.35
  227.9 4.0 fusion.73
  232.5 7.2 %fusion.74 = f32[128,1792]{1,0:T(8,128)} fusion(bf16[128,2432]{1,0:T(8,128)(2,1)S(1)} %pad_maximum_fusion.4, bf16[1792,2432]{1,0:T(8,128)(2,1)} %bitcast.263), kind=kOutput, calls=%fused_computation.214 | convolution fusion | flops 1115684864 | bytes 10256384 | tf_op jit(solution)/shard_map/dot_general | solution.py:18
  259.1 5.9 %convolution_convert_fusion = bf16[1216,1792]{1,0:T(8,128)(2,1)} fusion(bf16[512,1216]{1,0:T(8,128)(2,1)S(1)} %copy-done.48, bf16[128,1792]{1,0:T(8,128)(2,1)S(1)} %bitcast.303, bf16[128,1792]{1,0:T(8,128)(2,1)} %bitcast.77, bf16[128,1792]{1,0:T(8,128)(2,1)} %bitcast.76, bf16[128,1792]{1,0:T(8,128)(2,1)} %bitcast.73), kind=kOutput, calls=%fused_computation | convolution fusion | flops 2240888832 | bytes 7438336 | tf_op jit(solution)/shard_map/dot_general | solution.py:18
  271.8 5.8 %shard_map.224 = bf16[4,2,4,56,2432]{4,3,2,1,0:T(8,128)(2,1)S(1)} custom-call(s32[3]{0:T(128)S(1)} %pad_add_fusion.ids, bf16[512,1792]{1,0:T(8,128)(2,1)S(1)} %pad_maximum_fusion.1.x, bf16[512,2432]{1,0:T(8,128)(2,1)S(1)} %copy-done.2), custom_call_target="tpu_custom_call" | custom-call | tf_op jit(solution)/shard_map/pallas_call | solution.py:568
  277.7 3.5 copy-done
  281.1 6.7 %collective-permute-done.38 = bf16[2,64,1792]{2,1,0:T(8,128)(2,1)} collective-permute-done((bf16[2,64,1792]{2,1,0:T(8,128)(2,1)}, bf16[2,64,1792]{2,1,0:T(8,128)(2,1)}, u32[]{:S(2)}, u32[]{:S(2)}) %collective-permute-start.38) | collective-permute-done | bytes 458784 | tf_op jit(solution)/shard_map/ppermute | solution.py:23
  299.5 10.0 %collective-permute-done.40.x1 = bf16[2,64,1792]{2,1,0:T(8,128)(2,1)S(1)} collective-permute-done((bf16[2,64,1792]{2,1,0:T(8,128)(2,1)S(1)}, bf16[2,64,1792]{2,1,0:T(8,128)(2,1)S(1)}, u32[]{:S(2)}, u32[]{:S(2)}) %collective-permute-start.40) | collective-permute-done | bytes 458784 | tf_op jit(solution)/shard_map/ppermute | solution.py:23
  309.5 7.2 %collective-permute-done.41.x2 = bf16[2,64,1792]{2,1,0:T(8,128)(2,1)S(1)} collective-permute-done((bf16[2,64,1792]{2,1,0:T(8,128)(2,1)S(1)}, bf16[2,64,1792]{2,1,0:T(8,128)(2,1)S(1)}, u32[]{:S(2)}, u32[]{:S(2)}) %collective-permute-start.41) | collective-permute-done | bytes 458784 | tf_op jit(solution)/shard_map/ppermute | solution.py:23
  329.4 4.8 %collective-permute-done.45.got2 = bf16[2,112,256]{2,1,0:T(8,128)(2,1)S(1)} collective-permute-done((bf16[2,112,256]{2,1,0:T(8,128)(2,1)S(1)}, bf16[2,112,256]{2,1,0:T(8,128)(2,1)S(1)}, u32[]{:S(2)}, u32[]{:S(2)}) %collective-permute-start.45) | collective-permute-done | bytes 114720 | tf_op jit(solution)/shard_map/ppermute | solution.py:23
  338.4 8.3 %shard_map.226 = bf16[2,4,144,256]{3,2,1,0:T(8,128)(2,1)S(1)} custom-call(s32[3]{0:T(128)S(1)} %pad_add_fusion.ids, bf16[4,144,512]{2,1,0:T(8,128)(2,1)S(1)} %copy-done.22, f32[4,512,128]{2,1,0:T(8,128)S(1)} %copy-done.18, bf16[2,112,256]{2,1,0:T(8,128)(2,1)S(1)} %get-tuple-element.303.got0, bf16[2,112,256]{2,1,0:T(8,128)(2,1)S(1)} %collective-permute-done.44.got1, ...), custom_call_target="tpu_custom_call" | custom-call | tf_op jit(solution)/shard_map/pallas_call | solution.py:382
  356.0 3.6 collective-permute-done.54
  359.6 4.1 collective-permute-done.51.g1
  363.7 6.7 %collective-permute-done.52.g2 = bf16[2,144,256]{2,1,0:T(8,128)(2,1)S(1)} collective-permute-done((bf16[2,144,256]{2,1,0:T(8,128)(2,1)S(1)}, bf16[2,144,256]{2,1,0:T(8,128)(2,1)S(1)}, u32[]{:S(2)}, u32[]{:S(2)}) %collective-permute-start.52) | collective-permute-done | bytes 147488 | tf_op jit(solution)/shard_map/ppermute | solution.py:23
  370.5 5.1 %shard_map.227 = (bf16[2,4,4,56,576]{4,3,2,1,0:T(8,128)(2,1)S(1)}, f32[2,64,1792]{2,1,0:T(8,128)S(1)}, bf16[3,2,64,1792]{3,2,1,0:T(8,128)(2,1)S(1)}) custom-call(s32[3]{0:T(128)S(1)} %pad_add_fusion.ids, bf16[2,144,256]{2,1,0:T(8,128)(2,1)S(1)} %get-tuple-element.401.g0, bf16[2,144,256]{2,1,0:T(8,128)(2,1)S(1)} %collective-permute-done.51.g1, ...), custom_call_target="tpu_custom_call" | custom-call | tf_op jit(solution)/shard_map/pallas_call | solution.py:382
  382.6 3.8 collective-permute-start.57
  388.6 10.5 %collective-permute-done.56 = bf16[4,56,576]{2,1,0:T(8,128)(2,1)} collective-permute-done((bf16[4,56,576]{2,1,0:T(8,128)(2,1)}, bf16[4,56,576]{2,1,0:T(8,128)(2,1)}, u32[]{:S(2)}, u32[]{:S(2)}) %collective-permute-start.56) | collective-permute-done | bytes 258080 | tf_op jit(solution)/shard_map/ppermute | solution.py:23
  406.4 7.4 %collective-permute-done.60 = bf16[4,56,576]{2,1,0:T(8,128)(2,1)S(1)} collective-permute-done((bf16[4,56,576]{2,1,0:T(8,128)(2,1)}, bf16[4,56,576]{2,1,0:T(8,128)(2,1)S(1)}, u32[]{:S(2)}, u32[]{:S(2)}) %collective-permute-start.60) | collective-permute-done | bytes 258080 | tf_op jit(solution)/shard_map/ppermute | solution.py:23
  (372 shorter events, 228.0 us)
Async XLA Ops:
  7.2 85.6 %all-gather.8.cloned.1.call-start = ((), (), s32[]{:S(2)}) async-start(), calls=%async_computation.5 | async-start | bytes 4902912 | tf_op jit(solution)/shard_map/all_gather | solution.py:424
  7.9 122.4 %all-gather.10.cloned.1.call-start = ((), (), s32[]{:S(2)}) async-start(), calls=%async_computation.6 | async-start | bytes 9805824 | tf_op jit(solution)/shard_map/all_gather | solution.py:424
  15.5 15.6 %collective-permute-start.3 = (bf16[56,2432]{1,0:T(8,128)(2,1)S(1)}, bf16[56,2432]{1,0:T(8,128)(2,1)S(1)}, u32[]{:S(2)}, u32[]{:S(2)}) collective-permute-start(bf16[56,2432]{1,0:T(8,128)(2,1)S(1)} %get-tuple-element.191), channel_id=1, source_target_pairs={{0,2},{2,0},{4,6},{6,4},{1,3},{3,1},{5,7},{7,5},{8,10},{10,8},{12,... | collective-permute-start | bytes 817160 | tf_op jit(solution)/shard_map/ppermute | solution.py:23
  18.5 14.8 %collective-permute-start.4 = (bf16[56,2432]{1,0:T(8,128)(2,1)S(1)}, bf16[56,2432]{1,0:T(8,128)(2,1)S(1)}, u32[]{:S(2)}, u32[]{:S(2)}) collective-permute-start(bf16[56,2432]{1,0:T(8,128)(2,1)S(1)} %get-tuple-element.192), channel_id=1, source_target_pairs={{0,4},{2,6},{4,0},{6,2},{1,5},{3,7},{5,1},{7,3},{8,12},{10,14},{12... | collective-permute-start | bytes 817160 | tf_op jit(solution)/shard_map/ppermute | solution.py:23
  33.4 19.8 %collective-permute-start.5 = (bf16[2,64,1792]{2,1,0:T(8,128)(2,1)S(1)}, bf16[2,64,1792]{2,1,0:T(8,128)(2,1)S(1)}, u32[]{:S(2)}, u32[]{:S(2)}) collective-permute-start(bf16[2,64,1792]{2,1,0:T(8,128)(2,1)S(1)} %fusion.12.x0), channel_id=1, source_target_pairs={{0,8},{8,0},{16,24},{24,16},{1,9},{9,1},{17,25},{25,17},{2,10},{10... | collective-permute-start | bytes 1376264 | tf_op jit(solution)/shard_map/ppermute | solution.py:23
  34.9 20.7 %collective-permute-start.6 = (bf16[2,64,1792]{2,1,0:T(8,128)(2,1)S(1)}, bf16[2,64,1792]{2,1,0:T(8,128)(2,1)S(1)}, u32[]{:S(2)}, u32[]{:S(2)}) collective-permute-start(bf16[2,64,1792]{2,1,0:T(8,128)(2,1)S(1)} %fusion.12.x0), channel_id=1, source_target_pairs={{0,16},{8,24},{16,0},{24,8},{1,17},{9,25},{17,1},{25,9},{2,18},{10... | collective-permute-start | bytes 1376264 | tf_op jit(solution)/shard_map/ppermute | solution.py:23
  36.9 13.9 %collective-permute-start.8 = (bf16[4,56,576]{2,1,0:T(8,128)(2,1)S(1)}, bf16[4,56,576]{2,1,0:T(8,128)(2,1)S(1)}, u32[]{:S(2)}, u32[]{:S(2)}) collective-permute-start(bf16[4,56,576]{2,1,0:T(8,128)(2,1)S(1)} %bitcast_dynamic-update-slice_fusion.15), channel_id=1, source_target_pairs={{0,4},{2,6},{4,0},{6,2},{1,5},{3,7},{5,1},{7,3},{8,12},{10,14},{12... | collective-permute-start | bytes 774152 | tf_op jit(solution)/shard_map/ppermute | solution.py:23
  70.7 219.2 %all-gather.6.cloned.1.call-start = ((), (), s32[]{:S(2)}) async-start(), calls=%async_computation.2 | async-start | bytes 1081344 | tf_op jit(solution)/shard_map/all_gather | solution.py:535
  78.8 13.9 %collective-permute-start.15 = (bf16[2,144,256]{2,1,0:T(8,128)(2,1)S(1)}, bf16[2,144,256]{2,1,0:T(8,128)(2,1)S(1)}, u32[]{:S(2)}, u32[]{:S(2)}) collective-permute-start(bf16[2,144,256]{2,1,0:T(8,128)(2,1)S(1)} %get-tuple-element.215), channel_id=1, source_target_pairs={{0,4},{2,6},{4,0},{6,2},{1,5},{3,7},{5,1},{7,3},{8,12},{10,14},{12... | collective-permute-start | bytes 442376 | tf_op jit(solution)/shard_map/ppermute | solution.py:23
  125.4 13.6 %collective-permute-start.25 = (bf16[2,64,1792]{2,1,0:T(8,128)(2,1)}, bf16[2,64,1792]{2,1,0:T(8,128)(2,1)S(1)}, u32[]{:S(2)}, u32[]{:S(2)}) collective-permute-start(bf16[2,64,1792]{2,1,0:T(8,128)(2,1)} %get-tuple-element.237), channel_id=1, source_target_pairs={{0,8},{8,0},{16,24},{24,16},{1,9},{9,1},{17,25},{25,17},{2,10},{10... | collective-permute-start | bytes 1376264 | tf_op jit(solution)/shard_map/ppermute | solution.py:23
  127.5 22.5 %collective-permute-start.26 = (bf16[2,64,1792]{2,1,0:T(8,128)(2,1)}, bf16[2,64,1792]{2,1,0:T(8,128)(2,1)}, u32[]{:S(2)}, u32[]{:S(2)}) collective-permute-start(bf16[2,64,1792]{2,1,0:T(8,128)(2,1)} %get-tuple-element.238), channel_id=1, source_target_pairs={{0,16},{8,24},{16,0},{24,8},{1,17},{9,25},{17,1},{25,9},{2,18},{10... | collective-permute-start | bytes 1376264 | tf_op jit(solution)/shard_map/ppermute | solution.py:23
  127.5 22.5 %collective-permute-start.27 = (bf16[2,64,1792]{2,1,0:T(8,128)(2,1)}, bf16[2,64,1792]{2,1,0:T(8,128)(2,1)}, u32[]{:S(2)}, u32[]{:S(2)}) collective-permute-start(bf16[2,64,1792]{2,1,0:T(8,128)(2,1)} %get-tuple-element.239), channel_id=1, source_target_pairs={{0,24},{8,16},{16,8},{24,0},{1,25},{9,17},{17,9},{25,1},{2,26},{10... | collective-permute-start | bytes 1376264 | tf_op jit(solution)/shard_map/ppermute | solution.py:23
  151.8 21.4 %collective-permute-start.28 = (bf16[2,64,1792]{2,1,0:T(8,128)(2,1)S(1)}, bf16[2,64,1792]{2,1,0:T(8,128)(2,1)S(1)}, u32[]{:S(2)}, u32[]{:S(2)}) collective-permute-start(bf16[2,64,1792]{2,1,0:T(8,128)(2,1)S(1)} %multiply_convert_fusion.3), channel_id=1, source_target_pairs={{0,2},{2,0},{4,6},{6,4},{1,3},{3,1},{5,7},{7,5},{8,10},{10,8},{12,... | collective-permute-start | bytes 1376264 | tf_op jit(solution)/shard_map/ppermute | solution.py:23
  152.7 20.6 %collective-permute-start.29 = (bf16[2,64,1792]{2,1,0:T(8,128)(2,1)S(1)}, bf16[2,64,1792]{2,1,0:T(8,128)(2,1)S(1)}, u32[]{:S(2)}, u32[]{:S(2)}) collective-permute-start(bf16[2,64,1792]{2,1,0:T(8,128)(2,1)S(1)} %multiply_convert_fusion.3), channel_id=1, source_target_pairs={{0,4},{2,6},{4,0},{6,2},{1,5},{3,7},{5,1},{7,3},{8,12},{10,14},{12... | collective-permute-start | bytes 1376264 | tf_op jit(solution)/shard_map/ppermute | solution.py:23
  197.7 17.9 %collective-permute-start.32 = (bf16[2,64,1792]{2,1,0:T(8,128)(2,1)S(1)}, bf16[2,64,1792]{2,1,0:T(8,128)(2,1)S(1)}, u32[]{:S(2)}, u32[]{:S(2)}) collective-permute-start(bf16[2,64,1792]{2,1,0:T(8,128)(2,1)S(1)} %slice_bitcast_fusion.5), channel_id=1, source_target_pairs={{0,2},{2,0},{4,6},{6,4},{1,3},{3,1},{5,7},{7,5},{8,10},{10,8},{12,... | collective-permute-start | bytes 1376264 | tf_op jit(solution)/shard_map/ppermute | solution.py:23
  199.5 18.7 %collective-permute-start.33 = (bf16[2,64,1792]{2,1,0:T(8,128)(2,1)S(1)}, bf16[2,64,1792]{2,1,0:T(8,128)(2,1)S(1)}, u32[]{:S(2)}, u32[]{:S(2)}) collective-permute-start(bf16[2,64,1792]{2,1,0:T(8,128)(2,1)S(1)} %fusion.27), channel_id=1, source_target_pairs={{0,4},{2,6},{4,0},{6,2},{1,5},{3,7},{5,1},{7,3},{8,12},{10,14},{12... | collective-permute-start | bytes 1376264 | tf_op jit(solution)/shard_map/ppermute | solution.py:23
  221.3 18.3 %collective-permute-start.34 = (bf16[2,64,1792]{2,1,0:T(8,128)(2,1)}, bf16[2,64,1792]{2,1,0:T(8,128)(2,1)}, u32[]{:S(2)}, u32[]{:S(2)}) collective-permute-start(bf16[2,64,1792]{2,1,0:T(8,128)(2,1)} %fusion.67), channel_id=1, source_target_pairs={{0,2},{2,0},{4,6},{6,4},{1,3},{3,1},{5,7},{7,5},{8,10},{10,8},{12,... | collective-permute-start | bytes 1376264 | tf_op jit(solution)/shard_map/ppermute | solution.py:23
  223.0 18.3 %collective-permute-start.35 = (bf16[2,64,1792]{2,1,0:T(8,128)(2,1)}, bf16[2,64,1792]{2,1,0:T(8,128)(2,1)}, u32[]{:S(2)}, u32[]{:S(2)}) collective-permute-start(bf16[2,64,1792]{2,1,0:T(8,128)(2,1)} %fusion.67), channel_id=1, source_target_pairs={{0,4},{2,6},{4,0},{6,2},{1,5},{3,7},{5,1},{7,3},{8,12},{10,14},{12... | collective-permute-start | bytes 1376264 | tf_op jit(solution)/shard_map/ppermute | solution.py:23
  227.7 142.8 %reduce-scatter.3.cloned.1.call-start = ((), (), s32[]{:S(2)}) async-start(), calls=%async_computation.3 | async-start | bytes 9805824 | tf_op jit(solution)/shard_map/reduce_scatter | solution.py:427
  267.0 20.9 %collective-permute-start.38 = (bf16[2,64,1792]{2,1,0:T(8,128)(2,1)}, bf16[2,64,1792]{2,1,0:T(8,128)(2,1)}, u32[]{:S(2)}, u32[]{:S(2)}) collective-permute-start(bf16[2,64,1792]{2,1,0:T(8,128)(2,1)} %get-tuple-element.276), channel_id=1, source_target_pairs={{0,2},{2,0},{4,6},{6,4},{1,3},{3,1},{5,7},{7,5},{8,10},{10,8},{12,... | collective-permute-start | bytes 1376264 | tf_op jit(solution)/shard_map/ppermute | solution.py:23
  268.0 21.9 %collective-permute-start.39 = (bf16[2,64,1792]{2,1,0:T(8,128)(2,1)S(1)}, bf16[2,64,1792]{2,1,0:T(8,128)(2,1)}, u32[]{:S(2)}, u32[]{:S(2)}) collective-permute-start(bf16[2,64,1792]{2,1,0:T(8,128)(2,1)S(1)} %add_convert_fusion), channel_id=1, source_target_pairs={{0,4},{2,6},{4,0},{6,2},{1,5},{3,7},{5,1},{7,3},{8,12},{10,14},{12... | collective-permute-start | bytes 1376264 | tf_op jit(solution)/shard_map/ppermute | solution.py:23
  290.0 146.4 %reduce-scatter.5.cloned.1.call-start = ((), (), s32[]{:S(2)}) async-start(), calls=%async_computation.4 | async-start | bytes 4902912 | tf_op jit(solution)/shard_map/reduce_scatter | solution.py:427
  296.0 13.5 %collective-permute-start.40 = (bf16[2,64,1792]{2,1,0:T(8,128)(2,1)S(1)}, bf16[2,64,1792]{2,1,0:T(8,128)(2,1)S(1)}, u32[]{:S(2)}, u32[]{:S(2)}) collective-permute-start(bf16[2,64,1792]{2,1,0:T(8,128)(2,1)S(1)} %get-tuple-element.288.x0), channel_id=1, source_target_pairs={{0,8},{8,0},{16,24},{24,16},{1,9},{9,1},{17,25},{25,17},{2,10},{10... | collective-permute-start | bytes 1376264 | tf_op jit(solution)/shard_map/ppermute | solution.py:23
  297.0 19.7 %collective-permute-start.41 = (bf16[2,64,1792]{2,1,0:T(8,128)(2,1)S(1)}, bf16[2,64,1792]{2,1,0:T(8,128)(2,1)S(1)}, u32[]{:S(2)}, u32[]{:S(2)}) collective-permute-start(bf16[2,64,1792]{2,1,0:T(8,128)(2,1)S(1)} %get-tuple-element.288.x0), channel_id=1, source_target_pairs={{0,16},{8,24},{16,0},{24,8},{1,17},{9,25},{17,1},{25,9},{2,18},{10... | collective-permute-start | bytes 1376264 | tf_op jit(solution)/shard_map/ppermute | solution.py:23
  298.5 19.1 %collective-permute-start.42 = (bf16[2,64,1792]{2,1,0:T(8,128)(2,1)S(1)}, bf16[2,64,1792]{2,1,0:T(8,128)(2,1)S(1)}, u32[]{:S(2)}, u32[]{:S(2)}) collective-permute-start(bf16[2,64,1792]{2,1,0:T(8,128)(2,1)S(1)} %get-tuple-element.288.x0), channel_id=1, source_target_pairs={{0,24},{8,16},{16,8},{24,0},{1,25},{9,17},{17,9},{25,1},{2,26},{10... | collective-permute-start | bytes 1376264 | tf_op jit(solution)/shard_map/ppermute | solution.py:23
  351.6 18.8 %collective-permute-start.52 = (bf16[2,144,256]{2,1,0:T(8,128)(2,1)S(1)}, bf16[2,144,256]{2,1,0:T(8,128)(2,1)S(1)}, u32[]{:S(2)}, u32[]{:S(2)}) collective-permute-start(bf16[2,144,256]{2,1,0:T(8,128)(2,1)S(1)} %get-tuple-element.310), channel_id=1, source_target_pairs={{0,4},{2,6},{4,0},{6,2},{1,5},{3,7},{5,1},{7,3},{8,12},{10,14},{12... | collective-permute-start | bytes 442376 | tf_op jit(solution)/shard_map/ppermute | solution.py:23
  354.5 16.0 %collective-permute-start.53 = (bf16[2,144,256]{2,1,0:T(8,128)(2,1)S(1)}, bf16[2,144,256]{2,1,0:T(8,128)(2,1)S(1)}, u32[]{:S(2)}, u32[]{:S(2)}) collective-permute-start(bf16[2,144,256]{2,1,0:T(8,128)(2,1)S(1)} %get-tuple-element.311), channel_id=1, source_target_pairs={{0,6},{2,4},{4,2},{6,0},{1,7},{3,5},{5,3},{7,1},{8,14},{10,12},{12... | collective-permute-start | bytes 442376 | tf_op jit(solution)/shard_map/ppermute | solution.py:23
  380.1 19.0 %collective-permute-start.58 = (bf16[2,64,1792]{2,1,0:T(8,128)(2,1)}, bf16[2,64,1792]{2,1,0:T(8,128)(2,1)S(1)}, u32[]{:S(2)}, u32[]{:S(2)}) collective-permute-start(bf16[2,64,1792]{2,1,0:T(8,128)(2,1)} %get-tuple-element.324), channel_id=1, source_target_pairs={{0,8},{8,0},{16,24},{24,16},{1,9},{9,1},{17,25},{25,17},{2,10},{10... | collective-permute-start | bytes 1376264 | tf_op jit(solution)/shard_map/ppermute | solution.py:23
  381.5 17.6 %collective-permute-start.59 = (bf16[2,64,1792]{2,1,0:T(8,128)(2,1)}, bf16[2,64,1792]{2,1,0:T(8,128)(2,1)S(1)}, u32[]{:S(2)}, u32[]{:S(2)}) collective-permute-start(bf16[2,64,1792]{2,1,0:T(8,128)(2,1)} %get-tuple-element.325), channel_id=1, source_target_pairs={{0,16},{8,24},{16,0},{24,8},{1,17},{9,25},{17,1},{25,9},{2,18},{10... | collective-permute-start | bytes 1376264 | tf_op jit(solution)/shard_map/ppermute | solution.py:23
  382.6 16.5 %collective-permute-start.57 = (bf16[56,2432]{1,0:T(8,128)(2,1)}, bf16[56,2432]{1,0:T(8,128)(2,1)S(1)}, u32[]{:S(2)}, u32[]{:S(2)}) collective-permute-start(bf16[56,2432]{1,0:T(8,128)(2,1)} %get-tuple-element.323), channel_id=1, source_target_pairs={{0,4},{2,6},{4,0},{6,2},{1,5},{3,7},{5,1},{7,3},{8,12},{10,14},{12... | collective-permute-start | bytes 817160 | tf_op jit(solution)/shard_map/ppermute | solution.py:23
  400.2 16.8 %collective-permute-start.62 = (bf16[2,64,1792]{2,1,0:T(8,128)(2,1)}, bf16[2,64,1792]{2,1,0:T(8,128)(2,1)S(1)}, u32[]{:S(2)}, u32[]{:S(2)}) collective-permute-start(bf16[2,64,1792]{2,1,0:T(8,128)(2,1)} %get-tuple-element.331), channel_id=1, source_target_pairs={{0,24},{8,16},{16,8},{24,0},{1,25},{9,17},{17,9},{25,1},{2,26},{10... | collective-permute-start | bytes 1376264 | tf_op jit(solution)/shard_map/ppermute | solution.py:23
  419.0 13.3 %collective-permute-start.67 = (bf16[56,2432]{1,0:T(8,128)(2,1)S(1)}, bf16[56,2432]{1,0:T(8,128)(2,1)S(1)}, u32[]{:S(2)}, u32[]{:S(2)}) collective-permute-start(bf16[56,2432]{1,0:T(8,128)(2,1)S(1)} %copy-done.50), channel_id=1, source_target_pairs={{0,6},{2,4},{4,2},{6,0},{1,7},{3,5},{5,3},{7,1},{8,14},{10,12},{12... | collective-permute-start | bytes 817160 | tf_op jit(solution)/shard_map/ppermute | solution.py:23
  (110 other events, 1068.2 us)
Sparse Core Ops, SparseCore 0:
  9.9 57.0 all-gather.7
  70.9 56.3 all-gather.9
  227.8 56.1 all-gather.5
  290.1 74.3 reduce-scatter.2
  367.8 66.6 reduce-scatter.4
